TPU v7x, 512 devices: a whole 4x4x16 slice. The times are simulated.
512 devices in a mesh: pair: 32 (over z, x_lo), row: 16 (over y, x_hi, core).
Axes of the slice: x: 4 (x_hi: 2, x_lo: 2; x = x_hi * 2 + x_lo), y: 4, z: 16, core: 2. Of those that a mesh axis runs over, the one named last changes fastest.
Arguments:
- matrix: float32 [65536, 4096], P('row', 'pair'), may hold values from -60 to 60, as said below
- stay_side: int32 [4, 32], P(None, 'pair'), may hold values from 0 to 1
Outputs:
- rotated: float32 [65536, 4096], P('row', 'pair')
Inputs may be any that keep to these rules, and one draw needn't show every extreme that they name: `matrix`: entries are real-valued and of mixed magnitude.
All inputs are finite; a program needn't handle non-finite values.
Results may differ from a plain program's by a relative error of at most 0.0003.
Values sent between devices are 32-bit elements; how exact they have to be, the bound alone decides.
No kernel may reach another device: no remote copies, remote signals or barrier semaphores. Data moves between devices by JAX's collectives and lax.ppermute only.
A program may use at most 64 MiB of HBM per device.

v0:
```python
import jax
import jax.numpy as jnp
from jax import lax
from jax.sharding import PartitionSpec as P

ROUNDS = 4
NS_STEPS = 6


def passed_along(shard, axis, by):
    peers = lax.axis_size(axis)
    return lax.ppermute(shard, axis, [(i, (i + by) % peers) for i in range(peers)])


def newton_schulz(gram):
    order = gram.shape[0]
    scale = jnp.sqrt(jnp.sum(gram * gram) + 1e-06)
    ident = jnp.eye(order, dtype=jnp.float32)
    ymat = gram / scale
    zmat = ident
    for step in range(NS_STEPS):
        stepper = 1.5 * ident - 0.5 * jnp.dot(zmat, ymat, precision=lax.Precision.HIGHEST)
        ymat = jnp.dot(ymat, stepper, precision=lax.Precision.HIGHEST)
        zmat = jnp.dot(stepper, zmat, precision=lax.Precision.HIGHEST)
    return (zmat, scale)


def full_gram(slab):
    local_gram = jnp.dot(slab.T, slab, precision=lax.Precision.HIGHEST)
    return lax.psum(local_gram, "row")


def shift_block(move):
    return passed_along(move, "pair", 1)


def local(matrix, stay_side):
    width = matrix.shape[1] // 2
    total_rows = matrix.shape[0] * lax.axis_size("row")
    current = matrix
    stay = matrix[:, :width]
    arrived = matrix[:, width:]
    for round_index in range(ROUNDS):
        side = stay_side[round_index, 0]
        if round_index == 0:
            gram = full_gram(current)
        else:
            gram = full_gram(current)
        zmat, scale = newton_schulz(gram)
        factor = jnp.sqrt(total_rows / scale)
        newer = jnp.dot(current, zmat, precision=lax.Precision.HIGHEST) * factor
        stay = jnp.where(side == 0, newer[:, :width], newer[:, width:])
        move = jnp.where(side == 0, newer[:, width:], newer[:, :width])
        if round_index + 1 == ROUNDS:
            arrived = shift_block(move)
        else:
            arrived = shift_block(move)
        current = jnp.concatenate([stay, arrived], axis=1)
    return current


def solution(mesh):
    return jax.shard_map(
        local,
        mesh=mesh,
        in_specs=(P("row", "pair"), P(None, "pair")),
        out_specs=P("row", "pair"),
        check_vma=False,
    )
```

profile of v0, /device:TPU:1, one launch (start us, length us, event | category | flops | bytes accessed | tf_op | source)
XLA Modules:
  0.0 752.0 jit_solution(14753400239175456678)
XLA Ops:
  6.5 1.6 copy-done
  8.1 4.1 fusion.43
  13.7 145.2 %all-reduce.5.cloned.1.call-done = f32[128,128]{1,0:T(8,128)} async-done(((f32[128,128]{1,0:T(8,128)}), f32[128,128]{1,0:T(8,128)}) %all-reduce.5.cloned.1.call-update) | async-done | bytes 65552 | tf_op jit(solution)/shard_map/psum | solution.py:30
  158.9 1.5 multiply_reduce_fusion.3
  162.3 1.0 fusion.32
  166.4 2.0 fusion
  168.5 2.2 collective-permute-start
  170.7 23.7 %collective-permute-done = f32[4096,64]{0,1:T(8,128)S(1)} collective-permute-done((f32[4096,64]{0,1:T(8,128)S(1)}, f32[4096,64]{0,1:T(8,128)S(1)}, u32[]{:S(2)}, u32[]{:S(2)}) %collective-permute-start) | collective-permute-done | bytes 1048608 | tf_op jit(solution)/shard_map/ppermute | solution.py:12
  195.4 2.4 fusion.3
  198.7 141.0 %all-reduce.7.cloned.1.call-done = f32[128,128]{1,0:T(8,128)} async-done(((f32[128,128]{1,0:T(8,128)}), f32[128,128]{1,0:T(8,128)}) %all-reduce.7.cloned.1.call-update) | async-done | bytes 65552 | tf_op jit(solution)/shard_map/psum | solution.py:30
  339.8 1.5 multiply_reduce_fusion.2
  343.2 1.0 fusion.33
  347.3 3.2 convolution_multiply_fusion.2
  350.7 2.2 collective-permute-start.1
  352.9 23.7 %collective-permute-done.1 = f32[4096,64]{0,1:T(8,128)S(1)} collective-permute-done((f32[4096,64]{0,1:T(8,128)S(1)}, f32[4096,64]{0,1:T(8,128)S(1)}, u32[]{:S(2)}, u32[]{:S(2)}) %collective-permute-start.1) | collective-permute-done | bytes 1048608 | tf_op jit(solution)/shard_map/ppermute | solution.py:12
  377.6 2.4 fusion.2
  380.7 141.3 %all-reduce.9.cloned.1.call-done = f32[128,128]{1,0:T(8,128)} async-done(((f32[128,128]{1,0:T(8,128)}), f32[128,128]{1,0:T(8,128)}) %all-reduce.9.cloned.1.call-update) | async-done | bytes 65552 | tf_op jit(solution)/shard_map/psum | solution.py:30
  521.9 1.5 multiply_reduce_fusion.1
  525.4 1.0 fusion.34
  529.5 3.2 convolution_multiply_fusion.1
  532.9 2.4 collective-permute-start.2
  535.3 23.5 %collective-permute-done.2 = f32[4096,64]{0,1:T(8,128)S(1)} collective-permute-done((f32[4096,64]{0,1:T(8,128)S(1)}, f32[4096,64]{0,1:T(8,128)S(1)}, u32[]{:S(2)}, u32[]{:S(2)}) %collective-permute-start.2) | collective-permute-done | bytes 1048608 | tf_op jit(solution)/shard_map/ppermute | solution.py:12
  559.8 2.4 fusion.1
  562.8 141.3 %all-reduce.11.cloned.1.call-done = f32[128,128]{1,0:T(8,128)} async-done(((f32[128,128]{1,0:T(8,128)}), f32[128,128]{1,0:T(8,128)}) %all-reduce.11.cloned.1.call-update) | async-done | bytes 65552 | tf_op jit(solution)/shard_map/psum | solution.py:30
  704.1 1.5 multiply_reduce_fusion
  706.4 1.0 fusion.9
  707.7 1.0 fusion.35
  711.7 3.2 convolution_multiply_fusion
  715.2 2.2 collective-permute-start.3
  717.4 23.7 %collective-permute-done.3 = f32[4096,64]{0,1:T(8,128)S(1)} collective-permute-done((f32[4096,64]{0,1:T(8,128)S(1)}, f32[4096,64]{0,1:T(8,128)S(1)}, u32[]{:S(2)}, u32[]{:S(2)}) %collective-permute-start.3) | collective-permute-done | bytes 1048608 | tf_op jit(solution)/shard_map/ppermute | solution.py:12
  741.1 1.5 pad_maximum_fusion.3
  742.6 2.9 copy.3
  (85 shorter events, 19.8 us)
Async XLA Ops:
  6.5 1.6 copy-start
  6.5 5.8 copy-start.4
  6.5 152.4 %all-reduce.5.cloned.1.call-start = ((), (), s32[]{:S(2)}) async-start(), calls=%async_computation | async-start | bytes 131072 | tf_op jit(solution)/shard_map/psum | solution.py:30
  12.2 327.5 %all-reduce.7.cloned.1.call-start = ((), (), s32[]{:S(2)}) async-start(), calls=%async_computation.1 | async-start | bytes 131072 | tf_op jit(solution)/shard_map/psum | solution.py:30
  168.5 25.9 %collective-permute-start = (f32[4096,64]{0,1:T(8,128)S(1)}, f32[4096,64]{0,1:T(8,128)S(1)}, u32[]{:S(2)}, u32[]{:S(2)}) collective-permute-start(f32[4096,64]{0,1:T(8,128)S(1)} %get-tuple-element.12), channel_id=1, source_target_pairs={{0,16},{16,32},{32,48},{48,64},{64,80},{80,96},{96,112},{112,128},... | collective-permute-start | bytes 3145736 | tf_op jit(solution)/shard_map/ppermute | solution.py:12
  194.5 1.0 copy-start.2
  197.9 324.1 %all-reduce.9.cloned.1.call-start = ((), (), s32[]{:S(2)}) async-start(), calls=%async_computation.2 | async-start | bytes 131072 | tf_op jit(solution)/shard_map/psum | solution.py:30
  350.7 25.9 %collective-permute-start.1 = (f32[4096,64]{0,1:T(8,128)S(1)}, f32[4096,64]{0,1:T(8,128)S(1)}, u32[]{:S(2)}, u32[]{:S(2)}) collective-permute-start(f32[4096,64]{0,1:T(8,128)S(1)} %get-tuple-element.10), channel_id=1, source_target_pairs={{0,16},{16,32},{32,48},{48,64},{64,80},{80,96},{96,112},{112,128},... | collective-permute-start | bytes 3145736 | tf_op jit(solution)/shard_map/ppermute | solution.py:12
  376.6 1.0 copy-start.3
  380.0 324.1 %all-reduce.11.cloned.1.call-start = ((), (), s32[]{:S(2)}) async-start(), calls=%async_computation.3 | async-start | bytes 131072 | tf_op jit(solution)/shard_map/psum | solution.py:30
  532.9 25.9 %collective-permute-start.2 = (f32[4096,64]{0,1:T(8,128)S(1)}, f32[4096,64]{0,1:T(8,128)S(1)}, u32[]{:S(2)}, u32[]{:S(2)}) collective-permute-start(f32[4096,64]{0,1:T(8,128)S(1)} %get-tuple-element.8), channel_id=1, source_target_pairs={{0,16},{16,32},{32,48},{48,64},{64,80},{80,96},{96,112},{112,128},... | collective-permute-start | bytes 3145736 | tf_op jit(solution)/shard_map/ppermute | solution.py:12
  558.8 1.0 copy-start.1
  715.2 25.9 %collective-permute-start.3 = (f32[4096,64]{0,1:T(8,128)S(1)}, f32[4096,64]{0,1:T(8,128)S(1)}, u32[]{:S(2)}, u32[]{:S(2)}) collective-permute-start(f32[4096,64]{0,1:T(8,128)S(1)} %get-tuple-element.6), channel_id=1, source_target_pairs={{0,16},{16,32},{32,48},{48,64},{64,80},{80,96},{96,112},{112,128},... | collective-permute-start | bytes 3145736 | tf_op jit(solution)/shard_map/ppermute | solution.py:12
Sparse Core Ops, SparseCore 0:
  12.4 146.5 all-reduce.4
  198.0 141.7 all-reduce.6
  380.1 141.7 all-reduce.8
  562.3 141.7 all-reduce.10
where the time goes:
time: 754 us; the launch traced here: 752 us
  waiting for transfers between devices  664 us (88%)
  matrix products  43.5 us (6%)
  between operations  19.5 us (3%)
  starting transfers between devices  9.31 us (1%)
  other arithmetic  8.12 us (1%)
  local copies, waits for them, and re-layouts  8.04 us (1%)
    psum x4, waiting for transfers between devices, full_gram(): return lax.psum(local_gram, 'row')  569 us
    ppermute x4, waiting for transfers between devices, passed_along(): lax.ppermute(shard, axis, [(i, (i + by) % peers) for i in range(peers)])  94.7 us
  transfers between devices with their start and end apart: 8, of which 8 were waited for; matrix products, arithmetic and copies ran while one was open for 0% of the time, Pallas kernels for 0%

commit v1 on v0

--- a/solution.py
+++ b/solution.py
@@ -25,9 +25,18 @@
     return (zmat, scale)
 
 
+def row_sum(part):
+    peers = lax.axis_size("row")
+    part = part + lax.ppermute(part, "row", [(i, i ^ 1) for i in range(peers)])
+    same_core = [[core + 2 * chip for chip in range(peers // 2)] for core in range(2)]
+    copies = jnp.broadcast_to(part[None], (peers // 2,) + part.shape)
+    gathered = lax.all_to_all(copies, "row", 0, 0, axis_index_groups=same_core)
+    return jnp.sum(gathered, axis=0)
+
+
 def full_gram(slab):
     local_gram = jnp.dot(slab.T, slab, precision=lax.Precision.HIGHEST)
-    return lax.psum(local_gram, "row")
+    return row_sum(local_gram)
 
 
 def shift_block(move):

time: 754 us -> 255 us (0.34)
  waiting for transfers between devices: 664 us -> 148 us
  starting transfers between devices: 9.31 us -> 46.1 us
  between operations: 19.5 us -> 6.35 us
  matrix products: 43.5 us -> 34.2 us
    psum x4 -> x0, waiting for transfers between devices: 569 us -> none  [full_gram(): return lax.psum(local_gram, 'row')]
    all_to_all x0 -> x4, waiting for transfers between devices: none -> 40.5 us  [row_sum(): gathered = lax.all_to_all(copies, 'row', 0, 0, axis_index_groups=same_core)]
    ppermute x0 -> x4, starting transfers between devices: none -> 22.1 us  [row_sum(): part = part + lax.ppermute(part, 'row', [(i, i ^ 1) for i in range(peers)])]
    all_to_all x0 -> x4, starting transfers between devices: none -> 16.1 us  [row_sum(): gathered = lax.all_to_all(copies, 'row', 0, 0, axis_index_groups=same_core)]
    ppermute x4, waiting for transfers between devices: 94.7 us -> 104 us  [passed_along(): lax.ppermute(shard, axis, [(i, (i + by) % peers) for i in range(peers)])]
  transfers between devices with their start and end apart: 8 -> 12, of which waited for: 8 -> 12; matrix products, arithmetic and copies ran while one was open for 0% -> 0% of each run, Pallas kernels for 0% -> 0%
where the time goes in v1:
time: 255 us; the launch traced here: 254 us
  waiting for transfers between devices  148 us (58%)
  starting transfers between devices  46.1 us (18%)
  matrix products  34.2 us (13%)
  local copies, waits for them, and re-layouts  11.4 us (4%)
  other arithmetic  7.98 us (3%)
  between operations  6.35 us (2%)
    ppermute x4, waiting for transfers between devices, passed_along(): lax.ppermute(shard, axis, [(i, (i + by) % peers) for i in range(peers)])  104 us
    all_to_all x4, waiting for transfers between devices, row_sum(): gathered = lax.all_to_all(copies, 'row', 0, 0, axis_index_groups=same_core)  40.5 us
    ppermute x4, starting transfers between devices, row_sum(): part = part + lax.ppermute(part, 'row', [(i, i ^ 1) for i in range(peers)])  22.1 us
    all_to_all x4, starting transfers between devices, row_sum(): gathered = lax.all_to_all(copies, 'row', 0, 0, axis_index_groups=same_core)  16.1 us
    dot_general x4, matrix products, local(): newer = jnp.dot(current, zmat, precision=lax.Precision.HIGHEST) * factor  11.7 us
    dot_general x4, matrix products, full_gram(): local_gram = jnp.dot(slab.T, slab, precision=lax.Precision.HIGHEST)  8.82 us
    ppermute x4, starting transfers between devices, passed_along(): lax.ppermute(shard, axis, [(i, (i + by) % peers) for i in range(peers)])  7.9 us
  transfers between devices with their start and end apart: 12, of which 12 were waited for; matrix products, arithmetic and copies ran while one was open for 0% of the time, Pallas kernels for 0%

profile of v1, /device:TPU:1, one launch (start us, length us, event | category | flops | bytes accessed | tf_op | source)
XLA Modules:
  0.0 253.6 jit_solution(1535599175397544710)
XLA Ops:
  0.0 1.6 copy-done
  1.6 3.5 %fusion.43 = f32[128,128]{1,0:T(8,128)S(1)} fusion(f32[4096,128]{1,0:T(8,128)S(1)} %copy-done), kind=kOutput, calls=%fused_computation.92 | convolution fusion | flops 805306368 | bytes 2162688 | tf_op jit(solution)/shard_map/dot_general | solution.py:38
  5.1 8.8 %collective-permute-start = (f32[128,128]{1,0:T(8,128)S(1)}, f32[128,128]{1,0:T(8,128)S(1)}, u32[]{:S(2)}, u32[]{:S(2)}) collective-permute-start(f32[128,128]{1,0:T(8,128)S(1)} %fusion.43), channel_id=1, source_target_pairs={{0,1},{1,0},{2,3},{3,2},{4,5},{5,4},{6,7},{7,6},{8,9},{9,8},{10,11... | collective-permute-start | bytes 196616 | tf_op jit(solution)/shard_map/ppermute | solution.py:30
  15.6 3.5 %all-to-all-start = ((f32[8,128,128]{2,1,0:T(8,128)}), f32[8,128,128]{2,1,0:T(8,128)S(1)}, u32[]{:S(2)}, u32[]{:S(2)}) async-start(f32[8,128,128]{2,1,0:T(8,128)} %broadcast_in_dim.8), calls=%async_computation | async-start | bytes 1048576 | tf_op jit(solution)/shard_map/all_to_all | solution.py:33
  20.4 9.7 %all-to-all-done = f32[8,128,128]{2,1,0:T(8,128)S(1)} async-done(((f32[8,128,128]{2,1,0:T(8,128)}), f32[8,128,128]{2,1,0:T(8,128)S(1)}, u32[]{:S(2)}, u32[]{:S(2)}) %all-to-all-start) | async-done | bytes 524320 | tf_op jit(solution)/shard_map/all_to_all | solution.py:33
  35.1 2.0 fusion
  37.2 1.9 collective-permute-start.1
  39.1 28.4 %collective-permute-done.1 = f32[4096,64]{0,1:T(8,128)S(1)} collective-permute-done((f32[4096,64]{0,1:T(8,128)S(1)}, f32[4096,64]{0,1:T(8,128)S(1)}, u32[]{:S(2)}, u32[]{:S(2)}) %collective-permute-start.1) | collective-permute-done | bytes 1048608 | tf_op jit(solution)/shard_map/ppermute | solution.py:12
  68.5 1.8 fusion.3
  70.3 4.3 %collective-permute-start.2 = (f32[128,128]{1,0:T(8,128)S(1)}, f32[128,128]{1,0:T(8,128)S(1)}, u32[]{:S(2)}, u32[]{:S(2)}) collective-permute-start(f32[128,128]{1,0:T(8,128)S(1)} %fusion.3), channel_id=1, source_target_pairs={{0,1},{1,0},{2,3},{3,2},{4,5},{5,4},{6,7},{7,6},{8,9},{9,8},{10,11... | collective-permute-start | bytes 196616 | tf_op jit(solution)/shard_map/ppermute | solution.py:30
  76.4 4.3 %all-to-all-start.1 = ((f32[8,128,128]{2,1,0:T(8,128)}), f32[8,128,128]{2,1,0:T(8,128)}, u32[]{:S(2)}, u32[]{:S(2)}) async-start(f32[8,128,128]{2,1,0:T(8,128)} %broadcast_in_dim.9), calls=%async_computation.1 | async-start | bytes 1048576 | tf_op jit(solution)/shard_map/all_to_all | solution.py:33
  81.4 9.9 %all-to-all-done.1 = f32[8,128,128]{2,1,0:T(8,128)} async-done(((f32[8,128,128]{2,1,0:T(8,128)}), f32[8,128,128]{2,1,0:T(8,128)}, u32[]{:S(2)}, u32[]{:S(2)}) %all-to-all-start.1) | async-done | bytes 524320 | tf_op jit(solution)/shard_map/all_to_all | solution.py:33
  91.3 1.1 reduce_sum.74
  97.4 3.2 %convolution_multiply_fusion.2 = f32[4096,128]{0,1:T(8,128)S(1)} fusion(f32[128,128]{1,0:T(8,128)S(1)} %fusion.61, f32[4096,64]{0,1:T(8,128)} %copy-done.2, f32[4096,64]{0,1:T(8,128)S(1)} %get-tuple-element.11, f32[]{:T(128)S(6)} %sqrt.27), kind=kOutput, calls=%fused_computation.2 | convolution fusion | flops 806354944 | bytes 4259844 | tf_op jit(solution)/shard_map/dot_general | solution.py:60
  100.8 1.9 collective-permute-start.3
  102.8 24.9 %collective-permute-done.3 = f32[4096,64]{0,1:T(8,128)S(1)} collective-permute-done((f32[4096,64]{0,1:T(8,128)S(1)}, f32[4096,64]{0,1:T(8,128)S(1)}, u32[]{:S(2)}, u32[]{:S(2)}) %collective-permute-start.3) | collective-permute-done | bytes 1048608 | tf_op jit(solution)/shard_map/ppermute | solution.py:12
  128.7 1.8 fusion.2
  130.5 4.6 %collective-permute-start.4 = (f32[128,128]{1,0:T(8,128)S(1)}, f32[128,128]{1,0:T(8,128)S(1)}, u32[]{:S(2)}, u32[]{:S(2)}) collective-permute-start(f32[128,128]{1,0:T(8,128)S(1)} %fusion.2), channel_id=1, source_target_pairs={{0,1},{1,0},{2,3},{3,2},{4,5},{5,4},{6,7},{7,6},{8,9},{9,8},{10,11... | collective-permute-start | bytes 196616 | tf_op jit(solution)/shard_map/ppermute | solution.py:30
  136.8 4.1 %all-to-all-start.2 = ((f32[8,128,128]{2,1,0:T(8,128)}), f32[8,128,128]{2,1,0:T(8,128)}, u32[]{:S(2)}, u32[]{:S(2)}) async-start(f32[8,128,128]{2,1,0:T(8,128)} %broadcast_in_dim.10), calls=%async_computation.2 | async-start | bytes 1048576 | tf_op jit(solution)/shard_map/all_to_all | solution.py:33
  141.5 10.5 %all-to-all-done.2 = f32[8,128,128]{2,1,0:T(8,128)} async-done(((f32[8,128,128]{2,1,0:T(8,128)}), f32[8,128,128]{2,1,0:T(8,128)}, u32[]{:S(2)}, u32[]{:S(2)}) %all-to-all-start.2) | async-done | bytes 524320 | tf_op jit(solution)/shard_map/all_to_all | solution.py:33
  158.0 3.2 %convolution_multiply_fusion.1 = f32[4096,128]{0,1:T(8,128)S(1)} fusion(f32[128,128]{1,0:T(8,128)S(1)} %fusion.70, f32[4096,64]{0,1:T(8,128)} %copy-done.3, f32[4096,64]{0,1:T(8,128)S(1)} %get-tuple-element.9, f32[]{:T(128)S(6)} %sqrt.29), kind=kOutput, calls=%fused_computation.1 | convolution fusion | flops 806354944 | bytes 4259844 | tf_op jit(solution)/shard_map/dot_general | solution.py:60
  161.4 2.1 collective-permute-start.5
  163.5 25.0 %collective-permute-done.5 = f32[4096,64]{0,1:T(8,128)S(1)} collective-permute-done((f32[4096,64]{0,1:T(8,128)S(1)}, f32[4096,64]{0,1:T(8,128)S(1)}, u32[]{:S(2)}, u32[]{:S(2)}) %collective-permute-start.5) | collective-permute-done | bytes 1048608 | tf_op jit(solution)/shard_map/ppermute | solution.py:12
  189.5 1.8 fusion.1
  191.3 4.3 %collective-permute-start.6 = (f32[128,128]{1,0:T(8,128)S(1)}, f32[128,128]{1,0:T(8,128)S(1)}, u32[]{:S(2)}, u32[]{:S(2)}) collective-permute-start(f32[128,128]{1,0:T(8,128)S(1)} %fusion.1), channel_id=1, source_target_pairs={{0,1},{1,0},{2,3},{3,2},{4,5},{5,4},{6,7},{7,6},{8,9},{9,8},{10,11... | collective-permute-start | bytes 196616 | tf_op jit(solution)/shard_map/ppermute | solution.py:30
  197.3 4.1 %all-to-all-start.3 = ((f32[8,128,128]{2,1,0:T(8,128)}), f32[8,128,128]{2,1,0:T(8,128)}, u32[]{:S(2)}, u32[]{:S(2)}) async-start(f32[8,128,128]{2,1,0:T(8,128)} %broadcast_in_dim.11), calls=%async_computation.3 | async-start | bytes 1048576 | tf_op jit(solution)/shard_map/all_to_all | solution.py:33
  202.1 10.4 %all-to-all-done.3 = f32[8,128,128]{2,1,0:T(8,128)} async-done(((f32[8,128,128]{2,1,0:T(8,128)}), f32[8,128,128]{2,1,0:T(8,128)}, u32[]{:S(2)}, u32[]{:S(2)}) %all-to-all-start.3) | async-done | bytes 524320 | tf_op jit(solution)/shard_map/all_to_all | solution.py:33
  218.6 3.2 %convolution_multiply_fusion = f32[4096,128]{0,1:T(8,128)S(1)} fusion(f32[128,128]{1,0:T(8,128)S(1)} %fusion.79, f32[4096,64]{0,1:T(8,128)} %copy-done.1, f32[4096,64]{0,1:T(8,128)S(1)} %get-tuple-element.7, f32[]{:T(128)S(6)} %sqrt.31), kind=kOutput, calls=%fused_computation | convolution fusion | flops 806354944 | bytes 4259844 | tf_op jit(solution)/shard_map/dot_general | solution.py:60
  222.1 1.9 collective-permute-start.7
  224.0 25.2 %collective-permute-done.7 = f32[4096,64]{0,1:T(8,128)S(1)} collective-permute-done((f32[4096,64]{0,1:T(8,128)S(1)}, f32[4096,64]{0,1:T(8,128)S(1)}, u32[]{:S(2)}, u32[]{:S(2)}) %collective-permute-start.7) | collective-permute-done | bytes 1048608 | tf_op jit(solution)/shard_map/ppermute | solution.py:12
  249.3 1.5 pad_maximum_fusion.3
  250.8 2.9 %copy.4 = f32[4096,128]{1,0:T(8,128)} copy(f32[4096,128]{0,1:T(8,128)} %pad_maximum_fusion.3) | data formatting | bytes 4194304 | tf_op jit(solution)/shard_map/concatenate | solution.py:67
  (101 shorter events, 29.5 us)
Async XLA Ops:
  0.0 1.6 copy-start
  1.6 17.5 %copy-start.4 = (s32[4,1]{0,1:T(1,128)S(1)}, s32[4,1]{0,1:T(1,128)}, u32[]{:S(2)}) copy-start(s32[4,1]{0,1:T(1,128)} %param.3) | copy-start | bytes 52
  5.1 9.7 %collective-permute-start = (f32[128,128]{1,0:T(8,128)S(1)}, f32[128,128]{1,0:T(8,128)S(1)}, u32[]{:S(2)}, u32[]{:S(2)}) collective-permute-start(f32[128,128]{1,0:T(8,128)S(1)} %fusion.43), channel_id=1, source_target_pairs={{0,1},{1,0},{2,3},{3,2},{4,5},{5,4},{6,7},{7,6},{8,9},{9,8},{10,11... | collective-permute-start | bytes 196616 | tf_op jit(solution)/shard_map/ppermute | solution.py:30
  15.6 14.5 %all-to-all-start = ((f32[8,128,128]{2,1,0:T(8,128)}), f32[8,128,128]{2,1,0:T(8,128)S(1)}, u32[]{:S(2)}, u32[]{:S(2)}) async-start(f32[8,128,128]{2,1,0:T(8,128)} %broadcast_in_dim.8), calls=%async_computation | async-start | bytes 1048576 | tf_op jit(solution)/shard_map/all_to_all | solution.py:33
  37.2 30.3 %collective-permute-start.1 = (f32[4096,64]{0,1:T(8,128)S(1)}, f32[4096,64]{0,1:T(8,128)S(1)}, u32[]{:S(2)}, u32[]{:S(2)}) collective-permute-start(f32[4096,64]{0,1:T(8,128)S(1)} %get-tuple-element.12), channel_id=1, source_target_pairs={{0,16},{16,32},{32,48},{48,64},{64,80},{80,96},{96,112},{112,128},... | collective-permute-start | bytes 3145736 | tf_op jit(solution)/shard_map/ppermute | solution.py:12
  67.5 1.0 copy-start.2
  70.3 5.2 %collective-permute-start.2 = (f32[128,128]{1,0:T(8,128)S(1)}, f32[128,128]{1,0:T(8,128)S(1)}, u32[]{:S(2)}, u32[]{:S(2)}) collective-permute-start(f32[128,128]{1,0:T(8,128)S(1)} %fusion.3), channel_id=1, source_target_pairs={{0,1},{1,0},{2,3},{3,2},{4,5},{5,4},{6,7},{7,6},{8,9},{9,8},{10,11... | collective-permute-start | bytes 196616 | tf_op jit(solution)/shard_map/ppermute | solution.py:30
  76.4 14.9 %all-to-all-start.1 = ((f32[8,128,128]{2,1,0:T(8,128)}), f32[8,128,128]{2,1,0:T(8,128)}, u32[]{:S(2)}, u32[]{:S(2)}) async-start(f32[8,128,128]{2,1,0:T(8,128)} %broadcast_in_dim.9), calls=%async_computation.1 | async-start | bytes 1048576 | tf_op jit(solution)/shard_map/all_to_all | solution.py:33
  100.8 26.9 %collective-permute-start.3 = (f32[4096,64]{0,1:T(8,128)S(1)}, f32[4096,64]{0,1:T(8,128)S(1)}, u32[]{:S(2)}, u32[]{:S(2)}) collective-permute-start(f32[4096,64]{0,1:T(8,128)S(1)} %get-tuple-element.10), channel_id=1, source_target_pairs={{0,16},{16,32},{32,48},{48,64},{64,80},{80,96},{96,112},{112,128},... | collective-permute-start | bytes 3145736 | tf_op jit(solution)/shard_map/ppermute | solution.py:12
  127.7 1.0 copy-start.3
  130.5 5.5 %collective-permute-start.4 = (f32[128,128]{1,0:T(8,128)S(1)}, f32[128,128]{1,0:T(8,128)S(1)}, u32[]{:S(2)}, u32[]{:S(2)}) collective-permute-start(f32[128,128]{1,0:T(8,128)S(1)} %fusion.2), channel_id=1, source_target_pairs={{0,1},{1,0},{2,3},{3,2},{4,5},{5,4},{6,7},{7,6},{8,9},{9,8},{10,11... | collective-permute-start | bytes 196616 | tf_op jit(solution)/shard_map/ppermute | solution.py:30
  136.8 15.2 %all-to-all-start.2 = ((f32[8,128,128]{2,1,0:T(8,128)}), f32[8,128,128]{2,1,0:T(8,128)}, u32[]{:S(2)}, u32[]{:S(2)}) async-start(f32[8,128,128]{2,1,0:T(8,128)} %broadcast_in_dim.10), calls=%async_computation.2 | async-start | bytes 1048576 | tf_op jit(solution)/shard_map/all_to_all | solution.py:33
  161.4 27.2 %collective-permute-start.5 = (f32[4096,64]{0,1:T(8,128)S(1)}, f32[4096,64]{0,1:T(8,128)S(1)}, u32[]{:S(2)}, u32[]{:S(2)}) collective-permute-start(f32[4096,64]{0,1:T(8,128)S(1)} %get-tuple-element.8), channel_id=1, source_target_pairs={{0,16},{16,32},{32,48},{48,64},{64,80},{80,96},{96,112},{112,128},... | collective-permute-start | bytes 3145736 | tf_op jit(solution)/shard_map/ppermute | solution.py:12
  188.5 1.0 copy-start.1
  191.3 5.2 %collective-permute-start.6 = (f32[128,128]{1,0:T(8,128)S(1)}, f32[128,128]{1,0:T(8,128)S(1)}, u32[]{:S(2)}, u32[]{:S(2)}) collective-permute-start(f32[128,128]{1,0:T(8,128)S(1)} %fusion.1), channel_id=1, source_target_pairs={{0,1},{1,0},{2,3},{3,2},{4,5},{5,4},{6,7},{7,6},{8,9},{9,8},{10,11... | collective-permute-start | bytes 196616 | tf_op jit(solution)/shard_map/ppermute | solution.py:30
  197.3 15.2 %all-to-all-start.3 = ((f32[8,128,128]{2,1,0:T(8,128)}), f32[8,128,128]{2,1,0:T(8,128)}, u32[]{:S(2)}, u32[]{:S(2)}) async-start(f32[8,128,128]{2,1,0:T(8,128)} %broadcast_in_dim.11), calls=%async_computation.3 | async-start | bytes 1048576 | tf_op jit(solution)/shard_map/all_to_all | solution.py:33
  222.1 27.2 %collective-permute-start.7 = (f32[4096,64]{0,1:T(8,128)S(1)}, f32[4096,64]{0,1:T(8,128)S(1)}, u32[]{:S(2)}, u32[]{:S(2)}) collective-permute-start(f32[4096,64]{0,1:T(8,128)S(1)} %get-tuple-element.6), channel_id=1, source_target_pairs={{0,16},{16,32},{32,48},{48,64},{64,80},{80,96},{96,112},{112,128},... | collective-permute-start | bytes 3145736 | tf_op jit(solution)/shard_map/ppermute | solution.py:12

commit v2 on v1

v2 whole, which is shorter than its diff:
```python
import jax
import jax.numpy as jnp
from jax import lax
from jax.sharding import PartitionSpec as P

ROUNDS = 4
NS_STEPS = 6
HIGHEST = lax.Precision.HIGHEST


def passed_along(shard, axis, by):
    peers = lax.axis_size(axis)
    return lax.ppermute(shard, axis, [(i, (i + by) % peers) for i in range(peers)])


def newton_schulz(gram):
    order = gram.shape[0]
    scale = jnp.sqrt(jnp.sum(gram * gram) + 1e-06)
    ident = jnp.eye(order, dtype=jnp.float32)
    ymat = gram / scale
    zmat = ident
    for step in range(NS_STEPS):
        stepper = 1.5 * ident - 0.5 * jnp.dot(zmat, ymat, precision=HIGHEST)
        if step + 1 < NS_STEPS:
            ymat = jnp.dot(ymat, stepper, precision=HIGHEST)
        zmat = jnp.dot(stepper, zmat, precision=HIGHEST)
    return (zmat, scale)


def row_sum(part):
    peers = lax.axis_size("row")
    part = part + lax.ppermute(part, "row", [(i, i ^ 1) for i in range(peers)])
    same_core = [[core + 2 * chip for chip in range(peers // 2)] for core in range(2)]
    copies = jnp.broadcast_to(part[None], (peers // 2,) + part.shape)
    gathered = lax.all_to_all(copies, "row", 0, 0, axis_index_groups=same_core)
    return jnp.sum(gathered, axis=0)


def local(matrix, stay_side):
    width = matrix.shape[1] // 2
    total_rows = matrix.shape[0] * lax.axis_size("row")
    mine = matrix
    before = passed_along(matrix, "pair", 1)
    for round_index in range(ROUNDS):
        last = round_index + 1 == ROUNDS
        gram = row_sum(jnp.dot(mine.T, mine, precision=HIGHEST))
        zmat, scale = newton_schulz(gram)
        turn = zmat * jnp.sqrt(total_rows / scale)
        side = stay_side[round_index, 0]
        turn = jnp.where(side == 0, turn, jnp.concatenate([turn[:, width:], turn[:, :width]], axis=1))
        if last:
            turn_before = passed_along(turn[:, width:], "pair", 1)
        else:
            turn_before = passed_along(turn, "pair", 1)
        stay = jnp.dot(mine, turn[:, :width], precision=HIGHEST)
        moved = jnp.dot(before, turn_before, precision=HIGHEST)
        if last:
            return jnp.concatenate([stay, moved], axis=1)
        arrived = moved[:, width:]
        mine = jnp.concatenate([stay, arrived], axis=1)
        before = jnp.concatenate([moved[:, :width], passed_along(arrived, "pair", 1)], axis=1)


def solution(mesh):
    return jax.shard_map(
        local,
        mesh=mesh,
        in_specs=(P("row", "pair"), P(None, "pair")),
        out_specs=P("row", "pair"),
        check_vma=False,
    )
```

time: 255 us -> 277 us (1.086)
  waiting for transfers between devices: 148 us -> 161 us
  matrix products: 34.2 us -> 44.6 us
  starting transfers between devices: 46.1 us -> 52.4 us
  other arithmetic: 7.98 us -> 3.9 us
  local copies, waits for them, and re-layouts: 11.4 us -> 8.32 us
    ppermute x4 -> x8, waiting for transfers between devices: 104 us -> 124 us  [passed_along(): lax.ppermute(shard, axis, [(i, (i + by) % peers) for i in range(peers)])]
    dot_general x76 -> x80, matrix products: 34.2 us -> 44.6 us  [the longest x4 13 us: local(): moved = jnp.dot(before, turn_before, precision=HIGHEST)]
    ppermute x4 -> x8, starting transfers between devices: 7.9 us -> 15.6 us  [passed_along(): lax.ppermute(shard, axis, [(i, (i + by) % peers) for i in range(peers)])]
    all_to_all x4, waiting for transfers between devices: 40.5 us -> 33 us  [row_sum(): gathered = lax.all_to_all(copies, 'row', 0, 0, axis_index_groups=same_core)]
    unnamed x10 -> x4, local copies, waits for them, and re-layouts: 4.5 us -> 0.01 us
  transfers between devices with their start and end apart: 12 -> 16, of which waited for: 12 -> 12; matrix products, arithmetic and copies ran while one was open for 0% -> 9% of each run, Pallas kernels for 0% -> 0%
where the time goes in v2:
time: 277 us; the launch traced here: 276 us
  waiting for transfers between devices  161 us (58%)
  starting transfers between devices  52.4 us (19%)
  matrix products  44.6 us (16%)
  local copies, waits for them, and re-layouts  8.32 us (3%)
  between operations  6.61 us (2%)
  other arithmetic  3.9 us (1%)
    ppermute x8, waiting for transfers between devices, passed_along(): lax.ppermute(shard, axis, [(i, (i + by) % peers) for i in range(peers)])  124 us
    all_to_all x4, waiting for transfers between devices, row_sum(): gathered = lax.all_to_all(copies, 'row', 0, 0, axis_index_groups=same_core)  33 us
    ppermute x4, starting transfers between devices, row_sum(): part = part + lax.ppermute(part, 'row', [(i, i ^ 1) for i in range(peers)])  22.2 us
    ppermute x8, starting transfers between devices, passed_along(): lax.ppermute(shard, axis, [(i, (i + by) % peers) for i in range(peers)])  15.6 us
    all_to_all x4, starting transfers between devices, row_sum(): gathered = lax.all_to_all(copies, 'row', 0, 0, axis_index_groups=same_core)  14.6 us
    dot_general x4, matrix products, local(): moved = jnp.dot(before, turn_before, precision=HIGHEST)  13 us
    dot_general x4, matrix products, local(): gram = row_sum(jnp.dot(mine.T, mine, precision=HIGHEST))  11.2 us
    dot_general x4, matrix products, local(): stay = jnp.dot(mine, turn[:, :width], precision=HIGHEST)  6.31 us
  transfers between devices with their start and end apart: 16, of which 12 were waited for; matrix products, arithmetic and copies ran while one was open for 9% of the time, Pallas kernels for 0%

profile of v2, /device:TPU:1, one launch (start us, length us, event | category | flops | bytes accessed | tf_op | source)
XLA Modules:
  0.0 276.3 jit_solution(13759522181382476783)
XLA Ops:
  0.0 5.8 %fusion.71 = f32[128,128]{1,0:T(8,128)S(1)} fusion(f32[4096,128]{1,0:T(8,128)} %param.2), kind=kOutput, calls=%fused_computation.118 | convolution fusion | flops 805306368 | bytes 2162688 | tf_op jit(solution)/shard_map/dot_general | solution.py:46
  5.8 8.8 %collective-permute-start = (f32[128,128]{1,0:T(8,128)S(1)}, f32[128,128]{1,0:T(8,128)S(1)}, u32[]{:S(2)}, u32[]{:S(2)}) collective-permute-start(f32[128,128]{1,0:T(8,128)S(1)} %fusion.71), channel_id=1, source_target_pairs={{0,1},{1,0},{2,3},{3,2},{4,5},{5,4},{6,7},{7,6},{8,9},{9,8},{10,11... | collective-permute-start | bytes 196616 | tf_op jit(solution)/shard_map/ppermute | solution.py:32
  16.3 3.5 %all-to-all-start = ((f32[8,128,128]{2,1,0:T(8,128)}), f32[8,128,128]{2,1,0:T(8,128)S(1)}, u32[]{:S(2)}, u32[]{:S(2)}) async-start(f32[8,128,128]{2,1,0:T(8,128)} %broadcast_in_dim.8), calls=%async_computation | async-start | bytes 1048576 | tf_op jit(solution)/shard_map/all_to_all | solution.py:35
  19.9 1.9 collective-permute-start.2
  23.1 7.7 %all-to-all-done = f32[8,128,128]{2,1,0:T(8,128)S(1)} async-done(((f32[8,128,128]{2,1,0:T(8,128)}), f32[8,128,128]{2,1,0:T(8,128)S(1)}, u32[]{:S(2)}, u32[]{:S(2)}) %all-to-all-start) | async-done | bytes 524320 | tf_op jit(solution)/shard_map/all_to_all | solution.py:35
  35.9 1.9 collective-permute-start.1
  37.9 2.4 convolution_bitcast_fusion.1
  40.2 51.0 %collective-permute-done.1 = f32[128,128]{0,1:T(8,128)S(1)} collective-permute-done((f32[128,128]{0,1:T(8,128)S(1)}, f32[128,128]{0,1:T(8,128)S(1)}, u32[]{:S(2)}, u32[]{:S(2)}) %collective-permute-start.1) | collective-permute-done | bytes 65568 | tf_op jit(solution)/shard_map/ppermute | solution.py:13
  91.2 3.5 %convolution_bitcast_fusion = f32[4096,128]{0,1:T(8,128)S(1)} fusion(f32[128,128]{0,1:T(8,128)S(1)} %collective-permute-done.1, f32[4096,128]{1,0:T(8,128)} %collective-permute-done.2), kind=kOutput, calls=%fused_computation | convolution fusion | flops 805306368 | bytes 4259840 | tf_op jit(solution)/shard_map/dot_general | solution.py:56
  97.6 4.9 %collective-permute-start.3 = (f32[128,128]{1,0:T(8,128)S(1)}, f32[128,128]{1,0:T(8,128)S(1)}, u32[]{:S(2)}, u32[]{:S(2)}) collective-permute-start(f32[128,128]{1,0:T(8,128)S(1)} %fusion.17), channel_id=1, source_target_pairs={{0,1},{1,0},{2,3},{3,2},{4,5},{5,4},{6,7},{7,6},{8,9},{9,8},{10,11... | collective-permute-start | bytes 196616 | tf_op jit(solution)/shard_map/ppermute | solution.py:32
  104.1 3.5 %all-to-all-start.1 = ((f32[8,128,128]{2,1,0:T(8,128)}), f32[8,128,128]{2,1,0:T(8,128)S(1)}, u32[]{:S(2)}, u32[]{:S(2)}) async-start(f32[8,128,128]{2,1,0:T(8,128)} %broadcast_in_dim.9), calls=%async_computation.1 | async-start | bytes 1048576 | tf_op jit(solution)/shard_map/all_to_all | solution.py:35
  108.2 1.9 collective-permute-start.4
  110.1 8.4 %all-to-all-done.1 = f32[8,128,128]{2,1,0:T(8,128)S(1)} async-done(((f32[8,128,128]{2,1,0:T(8,128)}), f32[8,128,128]{2,1,0:T(8,128)S(1)}, u32[]{:S(2)}, u32[]{:S(2)}) %all-to-all-start.1) | async-done | bytes 524320 | tf_op jit(solution)/shard_map/all_to_all | solution.py:35
  123.7 1.9 collective-permute-start.5
  126.9 24.4 %collective-permute-done.5 = f32[128,128]{0,1:T(8,128)S(1)} collective-permute-done((f32[128,128]{0,1:T(8,128)S(1)}, f32[128,128]{0,1:T(8,128)S(1)}, u32[]{:S(2)}, u32[]{:S(2)}) %collective-permute-start.5) | collective-permute-done | bytes 65568 | tf_op jit(solution)/shard_map/ppermute | solution.py:13
  151.3 3.5 %fusion = f32[4096,128]{0,1:T(8,128)S(1)} fusion(f32[128,128]{0,1:T(8,128)S(1)} %collective-permute-done.5, f32[4096,64]{0,1:T(8,128)} %collective-permute-done.4, f32[4096,64]{0,1:T(8,128)} %get-tuple-element.9), kind=kOutput, calls=%fused_computation.3 | convolution fusion | flops 805830656 | bytes 4259840 | tf_op jit(solution)/shard_map/dot_general | solution.py:56
  157.8 4.3 %collective-permute-start.6 = (f32[128,128]{1,0:T(8,128)S(1)}, f32[128,128]{1,0:T(8,128)S(1)}, u32[]{:S(2)}, u32[]{:S(2)}) collective-permute-start(f32[128,128]{1,0:T(8,128)S(1)} %fusion.15), channel_id=1, source_target_pairs={{0,1},{1,0},{2,3},{3,2},{4,5},{5,4},{6,7},{7,6},{8,9},{9,8},{10,11... | collective-permute-start | bytes 196616 | tf_op jit(solution)/shard_map/ppermute | solution.py:32
  163.8 3.5 %all-to-all-start.2 = ((f32[8,128,128]{2,1,0:T(8,128)}), f32[8,128,128]{2,1,0:T(8,128)S(1)}, u32[]{:S(2)}, u32[]{:S(2)}) async-start(f32[8,128,128]{2,1,0:T(8,128)} %broadcast_in_dim.10), calls=%async_computation.2 | async-start | bytes 1048576 | tf_op jit(solution)/shard_map/all_to_all | solution.py:35
  168.0 1.9 collective-permute-start.7
  169.9 8.4 %all-to-all-done.2 = f32[8,128,128]{2,1,0:T(8,128)S(1)} async-done(((f32[8,128,128]{2,1,0:T(8,128)}), f32[8,128,128]{2,1,0:T(8,128)S(1)}, u32[]{:S(2)}, u32[]{:S(2)}) %all-to-all-start.2) | async-done | bytes 524320 | tf_op jit(solution)/shard_map/all_to_all | solution.py:35
  183.4 2.1 collective-permute-start.8
  186.9 24.3 %collective-permute-done.8 = f32[128,128]{0,1:T(8,128)S(1)} collective-permute-done((f32[128,128]{0,1:T(8,128)S(1)}, f32[128,128]{0,1:T(8,128)S(1)}, u32[]{:S(2)}, u32[]{:S(2)}) %collective-permute-start.8) | collective-permute-done | bytes 65568 | tf_op jit(solution)/shard_map/ppermute | solution.py:13
  211.2 3.5 %fusion.4 = f32[4096,128]{0,1:T(8,128)S(1)} fusion(f32[128,128]{0,1:T(8,128)S(1)} %collective-permute-done.8, f32[4096,64]{0,1:T(8,128)} %collective-permute-done.7, f32[4096,64]{0,1:T(8,128)} %get-tuple-element.7), kind=kOutput, calls=%fused_computation.8 | convolution fusion | flops 805830656 | bytes 4259840 | tf_op jit(solution)/shard_map/dot_general | solution.py:56
  214.9 1.8 fusion.13
  216.7 4.3 %collective-permute-start.9 = (f32[128,128]{1,0:T(8,128)S(1)}, f32[128,128]{1,0:T(8,128)S(1)}, u32[]{:S(2)}, u32[]{:S(2)}) collective-permute-start(f32[128,128]{1,0:T(8,128)S(1)} %fusion.13), channel_id=1, source_target_pairs={{0,1},{1,0},{2,3},{3,2},{4,5},{5,4},{6,7},{7,6},{8,9},{9,8},{10,11... | collective-permute-start | bytes 196616 | tf_op jit(solution)/shard_map/ppermute | solution.py:32
  222.7 4.1 %all-to-all-start.3 = ((f32[8,128,128]{2,1,0:T(8,128)}), f32[8,128,128]{2,1,0:T(8,128)}, u32[]{:S(2)}, u32[]{:S(2)}) async-start(f32[8,128,128]{2,1,0:T(8,128)} %broadcast_in_dim.11), calls=%async_computation.3 | async-start | bytes 1048576 | tf_op jit(solution)/shard_map/all_to_all | solution.py:35
  227.5 1.9 collective-permute-start.10
  229.4 8.5 %all-to-all-done.3 = f32[8,128,128]{2,1,0:T(8,128)} async-done(((f32[8,128,128]{2,1,0:T(8,128)}), f32[8,128,128]{2,1,0:T(8,128)}, u32[]{:S(2)}, u32[]{:S(2)}) %all-to-all-start.3) | async-done | bytes 524320 | tf_op jit(solution)/shard_map/all_to_all | solution.py:35
  244.1 1.9 collective-permute-start.11
  247.3 24.5 %collective-permute-done.11 = f32[128,64]{0,1:T(8,128)S(1)} collective-permute-done((f32[128,64]{0,1:T(8,128)S(1)}, f32[128,64]{0,1:T(8,128)S(1)}, u32[]{:S(2)}, u32[]{:S(2)}) %collective-permute-start.11) | collective-permute-done | bytes 32800 | tf_op jit(solution)/shard_map/ppermute | solution.py:13
  271.8 2.5 fusion.8
  274.5 1.8 copy.4
  (115 shorter events, 35.3 us)
Async XLA Ops:
  0.0 19.8 %copy-start = (f32[4096,128]{1,0:T(8,128)S(1)}, f32[4096,128]{1,0:T(8,128)}, u32[]{:S(2)}) copy-start(f32[4096,128]{1,0:T(8,128)} %param.2) | copy-start | bytes 6291460
  0.0 21.8 %copy-start.1 = (s32[4,1]{0,1:T(1,128)S(1)}, s32[4,1]{0,1:T(1,128)}, u32[]{:S(2)}) copy-start(s32[4,1]{0,1:T(1,128)} %param.3) | copy-start | bytes 52
  5.8 9.7 %collective-permute-start = (f32[128,128]{1,0:T(8,128)S(1)}, f32[128,128]{1,0:T(8,128)S(1)}, u32[]{:S(2)}, u32[]{:S(2)}) collective-permute-start(f32[128,128]{1,0:T(8,128)S(1)} %fusion.71), channel_id=1, source_target_pairs={{0,1},{1,0},{2,3},{3,2},{4,5},{5,4},{6,7},{7,6},{8,9},{9,8},{10,11... | collective-permute-start | bytes 196616 | tf_op jit(solution)/shard_map/ppermute | solution.py:32
  16.3 14.5 %all-to-all-start = ((f32[8,128,128]{2,1,0:T(8,128)}), f32[8,128,128]{2,1,0:T(8,128)S(1)}, u32[]{:S(2)}, u32[]{:S(2)}) async-start(f32[8,128,128]{2,1,0:T(8,128)} %broadcast_in_dim.8), calls=%async_computation | async-start | bytes 1048576 | tf_op jit(solution)/shard_map/all_to_all | solution.py:35
  19.9 71.4 %collective-permute-start.2 = (f32[4096,128]{1,0:T(8,128)S(1)}, f32[4096,128]{1,0:T(8,128)}, u32[]{:S(2)}, u32[]{:S(2)}) collective-permute-start(f32[4096,128]{1,0:T(8,128)S(1)} %copy-done), channel_id=1, source_target_pairs={{0,16},{16,32},{32,48},{48,64},{64,80},{80,96},{96,112},{112,128},... | collective-permute-start | bytes 6291464 | tf_op jit(solution)/shard_map/ppermute | solution.py:13
  35.9 55.3 %collective-permute-start.1 = (f32[128,128]{0,1:T(8,128)S(1)}, f32[128,128]{0,1:T(8,128)S(1)}, u32[]{:S(2)}, u32[]{:S(2)}) collective-permute-start(f32[128,128]{0,1:T(8,128)S(1)} %maximum_select_fusion), channel_id=1, source_target_pairs={{0,16},{16,32},{32,48},{48,64},{64,80},{80,96},{96,112},{112,128},... | collective-permute-start | bytes 196616 | tf_op jit(solution)/shard_map/ppermute | solution.py:13
  97.6 5.6 %collective-permute-start.3 = (f32[128,128]{1,0:T(8,128)S(1)}, f32[128,128]{1,0:T(8,128)S(1)}, u32[]{:S(2)}, u32[]{:S(2)}) collective-permute-start(f32[128,128]{1,0:T(8,128)S(1)} %fusion.17), channel_id=1, source_target_pairs={{0,1},{1,0},{2,3},{3,2},{4,5},{5,4},{6,7},{7,6},{8,9},{9,8},{10,11... | collective-permute-start | bytes 196616 | tf_op jit(solution)/shard_map/ppermute | solution.py:32
  104.1 14.5 %all-to-all-start.1 = ((f32[8,128,128]{2,1,0:T(8,128)}), f32[8,128,128]{2,1,0:T(8,128)S(1)}, u32[]{:S(2)}, u32[]{:S(2)}) async-start(f32[8,128,128]{2,1,0:T(8,128)} %broadcast_in_dim.9), calls=%async_computation.1 | async-start | bytes 1048576 | tf_op jit(solution)/shard_map/all_to_all | solution.py:35
  108.2 43.1 %collective-permute-start.4 = (f32[4096,64]{0,1:T(8,128)S(1)}, f32[4096,64]{0,1:T(8,128)}, u32[]{:S(2)}, u32[]{:S(2)}) collective-permute-start(f32[4096,64]{0,1:T(8,128)S(1)} %get-tuple-element.10), channel_id=1, source_target_pairs={{0,16},{16,32},{32,48},{48,64},{64,80},{80,96},{96,112},{112,128},... | collective-permute-start | bytes 3145736 | tf_op jit(solution)/shard_map/ppermute | solution.py:13
  123.7 27.7 %collective-permute-start.5 = (f32[128,128]{0,1:T(8,128)S(1)}, f32[128,128]{0,1:T(8,128)S(1)}, u32[]{:S(2)}, u32[]{:S(2)}) collective-permute-start(f32[128,128]{0,1:T(8,128)S(1)} %maximum_select_fusion.1), channel_id=1, source_target_pairs={{0,16},{16,32},{32,48},{48,64},{64,80},{80,96},{96,112},{112,128},... | collective-permute-start | bytes 196616 | tf_op jit(solution)/shard_map/ppermute | solution.py:13
  157.8 5.1 %collective-permute-start.6 = (f32[128,128]{1,0:T(8,128)S(1)}, f32[128,128]{1,0:T(8,128)S(1)}, u32[]{:S(2)}, u32[]{:S(2)}) collective-permute-start(f32[128,128]{1,0:T(8,128)S(1)} %fusion.15), channel_id=1, source_target_pairs={{0,1},{1,0},{2,3},{3,2},{4,5},{5,4},{6,7},{7,6},{8,9},{9,8},{10,11... | collective-permute-start | bytes 196616 | tf_op jit(solution)/shard_map/ppermute | solution.py:32
  163.8 14.5 %all-to-all-start.2 = ((f32[8,128,128]{2,1,0:T(8,128)}), f32[8,128,128]{2,1,0:T(8,128)S(1)}, u32[]{:S(2)}, u32[]{:S(2)}) async-start(f32[8,128,128]{2,1,0:T(8,128)} %broadcast_in_dim.10), calls=%async_computation.2 | async-start | bytes 1048576 | tf_op jit(solution)/shard_map/all_to_all | solution.py:35
  168.0 43.2 %collective-permute-start.7 = (f32[4096,64]{0,1:T(8,128)S(1)}, f32[4096,64]{0,1:T(8,128)}, u32[]{:S(2)}, u32[]{:S(2)}) collective-permute-start(f32[4096,64]{0,1:T(8,128)S(1)} %get-tuple-element.8), channel_id=1, source_target_pairs={{0,16},{16,32},{32,48},{48,64},{64,80},{80,96},{96,112},{112,128},... | collective-permute-start | bytes 3145736 | tf_op jit(solution)/shard_map/ppermute | solution.py:13
  183.4 27.8 %collective-permute-start.8 = (f32[128,128]{0,1:T(8,128)S(1)}, f32[128,128]{0,1:T(8,128)S(1)}, u32[]{:S(2)}, u32[]{:S(2)}) collective-permute-start(f32[128,128]{0,1:T(8,128)S(1)} %maximum_select_fusion.2), channel_id=1, source_target_pairs={{0,16},{16,32},{32,48},{48,64},{64,80},{80,96},{96,112},{112,128},... | collective-permute-start | bytes 196616 | tf_op jit(solution)/shard_map/ppermute | solution.py:13
  216.7 5.1 %collective-permute-start.9 = (f32[128,128]{1,0:T(8,128)S(1)}, f32[128,128]{1,0:T(8,128)S(1)}, u32[]{:S(2)}, u32[]{:S(2)}) collective-permute-start(f32[128,128]{1,0:T(8,128)S(1)} %fusion.13), channel_id=1, source_target_pairs={{0,1},{1,0},{2,3},{3,2},{4,5},{5,4},{6,7},{7,6},{8,9},{9,8},{10,11... | collective-permute-start | bytes 196616 | tf_op jit(solution)/shard_map/ppermute | solution.py:32
  222.7 15.2 %all-to-all-start.3 = ((f32[8,128,128]{2,1,0:T(8,128)}), f32[8,128,128]{2,1,0:T(8,128)}, u32[]{:S(2)}, u32[]{:S(2)}) async-start(f32[8,128,128]{2,1,0:T(8,128)} %broadcast_in_dim.11), calls=%async_computation.3 | async-start | bytes 1048576 | tf_op jit(solution)/shard_map/all_to_all | solution.py:35
  227.5 44.3 %collective-permute-start.10 = (f32[4096,64]{0,1:T(8,128)S(1)}, f32[4096,64]{0,1:T(8,128)}, u32[]{:S(2)}, u32[]{:S(2)}) collective-permute-start(f32[4096,64]{0,1:T(8,128)S(1)} %get-tuple-element.6), channel_id=1, source_target_pairs={{0,16},{16,32},{32,48},{48,64},{64,80},{80,96},{96,112},{112,128},... | collective-permute-start | bytes 3145736 | tf_op jit(solution)/shard_map/ppermute | solution.py:13
  244.1 27.8 %collective-permute-start.11 = (f32[128,64]{0,1:T(8,128)S(1)}, f32[128,64]{0,1:T(8,128)S(1)}, u32[]{:S(2)}, u32[]{:S(2)}) collective-permute-start(f32[128,64]{0,1:T(8,128)S(1)} %slice.110), channel_id=1, source_target_pairs={{0,16},{16,32},{32,48},{48,64},{64,80},{80,96},{96,112},{112,128},... | collective-permute-start | bytes 98312 | tf_op jit(solution)/shard_map/ppermute | solution.py:13

commit v3 on v2

v3 whole, which is shorter than its diff:
```python
import functools

import jax
import jax.numpy as jnp
from jax import lax
from jax.experimental import pallas as pl
from jax.experimental.pallas import tpu as pltpu
from jax.sharding import PartitionSpec as P

ROUNDS = 4
NS_STEPS = 6
HIGHEST = lax.Precision.HIGHEST


def mul(a, b):
    return jnp.dot(a, b, precision=HIGHEST)


def passed_along(shard, axis, by):
    peers = lax.axis_size(axis)
    return lax.ppermute(shard, axis, [(i, (i + by) % peers) for i in range(peers)])


def turn_kernel(total_rows, cross, side_ref, sums_ref, *refs):
    if cross:
        gram_stay_ref, gram_arrived_ref, gram_ref, turn_ref = refs
    else:
        gram_ref, turn_ref = refs
    order = gram_ref.shape[0]
    width = order // 2
    total = sums_ref[0]
    for device in range(1, sums_ref.shape[0]):
        total = total + sums_ref[device]
    if cross:
        block = jnp.concatenate([total[:, :width], total[:, width:]], axis=0)
        gram_ref[:width, :width] = gram_stay_ref[...]
        gram_ref[:width, width:] = block
        gram_ref[width:, :width] = block.T
        gram_ref[width:, width:] = gram_arrived_ref[...]
    else:
        gram_ref[:width, :] = total[:width]
        gram_ref[width:, :width] = total[:width, width:].T
        gram_ref[width:, width:] = jnp.concatenate([total[width:, :width], total[width:, width:]], axis=0)
    gram = gram_ref[...]
    scale = jnp.sqrt(jnp.sum(gram * gram) + 1e-06)
    down = lax.broadcasted_iota(jnp.int32, (order, order), 0)
    along = lax.broadcasted_iota(jnp.int32, (order, order), 1)
    half_more = jnp.where(down == along, 1.5, 0.0).astype(jnp.float32)
    ymat = gram / scale
    stepper = half_more - 0.5 * ymat
    both = jnp.concatenate([mul(stepper, ymat), stepper], axis=1)
    for step in range(1, NS_STEPS):
        ymat, zmat = both[:, :order], both[:, order:]
        stepper = half_more - 0.5 * mul(zmat, ymat)
        if step + 1 < NS_STEPS:
            both = mul(stepper, both)
        else:
            zmat = mul(stepper, zmat)
    zmat = zmat * jnp.sqrt(total_rows / scale)
    swapped = pltpu.roll(zmat, width, 1)
    turn_ref[...] = jnp.where(side_ref[0] == 0, zmat, swapped)


def turned(sums, side, total_rows, blocks=()):
    order = sums.shape[-1]
    square = jax.ShapeDtypeStruct((order, order), jnp.float32)
    in_vmem = pl.BlockSpec(memory_space=pltpu.VMEM)
    return pl.pallas_call(
        functools.partial(turn_kernel, total_rows, bool(blocks)),
        out_shape=(square, square),
        in_specs=[pl.BlockSpec(memory_space=pltpu.SMEM)] + [in_vmem] * (1 + len(blocks)),
        out_specs=(in_vmem, in_vmem),
        compiler_params=pltpu.CompilerParams(vmem_limit_bytes=3 << 20),
        cost_estimate=pl.CostEstimate(flops=200_000_000, bytes_accessed=500_000, transcendentals=0),
    )(side, sums, *blocks)


def shares(part, over_cores):
    peers = lax.axis_size("row")
    groups = None
    if over_cores:
        part = part + lax.ppermute(part, "row", [(i, i ^ 1) for i in range(peers)])
        groups = [[core + 2 * chip for chip in range(peers // 2)] for core in range(2)]
        peers = peers // 2
    copies = jnp.broadcast_to(part[None], (peers,) + part.shape)
    return lax.all_to_all(copies, "row", 0, 0, axis_index_groups=groups)


def folded(block):
    half = block.shape[0] // 2
    return jnp.concatenate([block[:half], block[half:]], axis=1)


def gram_shares(stay, arrived):
    slab = jnp.concatenate([stay, arrived], axis=1)
    width = stay.shape[1]
    part = mul(slab.T, slab)
    return shares(jnp.concatenate([part[:width], folded(part[width:, width:])], axis=0), True)


def local(matrix, stay_side):
    rows, width = matrix.shape[0], matrix.shape[1] // 2
    total_rows = float(rows * lax.axis_size("row"))
    stay, arrived = matrix[:, :width], matrix[:, width:]
    gram, turn = turned(gram_shares(stay, arrived), stay_side[0], total_rows)
    for round_index in range(ROUNDS):
        following = round_index + 1
        current = jnp.concatenate([stay, arrived], axis=1)
        to_stay, to_move = turn[:, :width], turn[:, width:]
        arrived = passed_along(mul(current, to_move), "pair", 1)
        stay = mul(current, to_stay)
        if following == ROUNDS:
            return jnp.concatenate([stay, arrived], axis=1)
        if following % 2 == 0:
            gram, turn = turned(gram_shares(stay, arrived), stay_side[following], total_rows)
        else:
            gram_stay = mul(to_stay.T, mul(gram, to_stay))
            gram_arrived = passed_along(mul(to_move.T, mul(gram, to_move)), "pair", 1)
            cross = shares(folded(mul(stay.T, arrived)), False)
            gram, turn = turned(cross, stay_side[following], total_rows, (gram_stay, gram_arrived))


def solution(mesh):
    return jax.shard_map(
        local,
        mesh=mesh,
        in_specs=(P("row", "pair"), P(None, "pair")),
        out_specs=P("row", "pair"),
        check_vma=False,
    )
```

time: 277 us -> 227 us (0.82)
  waiting for transfers between devices: 161 us -> 117 us
  matrix products: 44.6 us -> 27.5 us
  Pallas kernels: 0 us -> 15.4 us
  blocking collectives: 0 us -> 14.2 us
  starting transfers between devices: 52.4 us -> 40.1 us
  between operations: 6.61 us -> 0.3 us
    all_to_all x4 -> x3, waiting for transfers between devices: 33 us -> 11.5 us  [shares(): return lax.all_to_all(copies, 'row', 0, 0, axis_index_groups=groups)]
    ppermute x8 -> x6, waiting for transfers between devices: 124 us -> 104 us  [passed_along(): lax.ppermute(shard, axis, [(i, (i + by) % peers) for i in range(peers)])]
    dot_general x80 -> x20, matrix products: 44.6 us -> 27.5 us  [mul(): return jnp.dot(a, b, precision=HIGHEST)]
    pallas_call x0 -> x4, Pallas kernels: none -> 15.4 us  [turned(): pl.pallas_call(functools.partial(turn_kernel, total_rows, bool(blocks)),...]
    all_to_all x0 -> x1, blocking collectives: none -> 14.2 us  [shares(): return lax.all_to_all(copies, 'row', 0, 0, axis_index_groups=groups)]
    ppermute x4 -> x2, starting transfers between devices: 22.2 us -> 13 us  [shares(): part = part + lax.ppermute(part, 'row', [(i, i ^ 1) for i in range(peers)])]
    ppermute x8 -> x6, starting transfers between devices: 15.6 us -> 11.7 us  [passed_along(): lax.ppermute(shard, axis, [(i, (i + by) % peers) for i in range(peers)])]
    reduce_sum x8 -> x0, other arithmetic: 3.68 us -> none  [the longest x4 2.51 us: newton_schulz(): scale = jnp.sqrt(jnp.sum(gram * gram) + 1e-06)]
  transfers between devices with their start and end apart: 16 -> 11, of which waited for: 12 -> 11; matrix products, arithmetic and copies ran while one was open for 9% -> 5% of each run, Pallas kernels for 0% -> 0%
where the time goes in v3:
time: 227 us; the launch traced here: 226 us
  waiting for transfers between devices  117 us (52%)
  starting transfers between devices  40.1 us (18%)
  matrix products  27.5 us (12%)
  Pallas kernels  15.4 us (7%)
  blocking collectives  14.2 us (6%)
  local copies, waits for them, and re-layouts  9.54 us (4%)
    ppermute x6, waiting for transfers between devices, passed_along(): lax.ppermute(shard, axis, [(i, (i + by) % peers) for i in range(peers)])  104 us
    dot_general x20, matrix products, mul(): return jnp.dot(a, b, precision=HIGHEST)  27.5 us
    all_to_all x3, starting transfers between devices, shares(): return lax.all_to_all(copies, 'row', 0, 0, axis_index_groups=groups)  15.4 us
    pallas_call x4, Pallas kernels, turned(): pl.pallas_call(functools.partial(turn_kernel, total_rows, bool(blocks)),...  15.4 us
    all_to_all x1, blocking collectives, shares(): return lax.all_to_all(copies, 'row', 0, 0, axis_index_groups=groups)  14.2 us
    ppermute x2, starting transfers between devices, shares(): part = part + lax.ppermute(part, 'row', [(i, i ^ 1) for i in range(peers)])  13 us
    ppermute x6, starting transfers between devices, passed_along(): lax.ppermute(shard, axis, [(i, (i + by) % peers) for i in range(peers)])  11.7 us
    all_to_all x3, waiting for transfers between devices, shares(): return lax.all_to_all(copies, 'row', 0, 0, axis_index_groups=groups)  11.5 us
  transfers between devices with their start and end apart: 11, of which 11 were waited for; matrix products, arithmetic and copies ran while one was open for 5% of the time, Pallas kernels for 0%

profile of v3, /device:TPU:1, one launch (start us, length us, event | category | flops | bytes accessed | tf_op | source)
XLA Modules:
  0.0 226.0 jit_solution(13118995456576392947)
XLA Ops:
  0.0 1.6 copy-done
  1.6 3.5 %fusion.44 = f32[128,128]{1,0:T(8,128)S(1)} fusion(f32[4096,128]{1,0:T(8,128)S(1)} %copy-done), kind=kOutput, calls=%fused_computation.53 | convolution fusion | flops 805306368 | bytes 2162688 | tf_op jit(solution)/shard_map/dot_general | solution.py:16
  5.2 8.8 %collective-permute-start = (f32[96,128]{1,0:T(8,128)S(1)}, f32[96,128]{1,0:T(8,128)S(1)}, u32[]{:S(2)}, u32[]{:S(2)}) collective-permute-start(f32[96,128]{1,0:T(8,128)S(1)} %maximum_maximum_fusion), channel_id=1, source_target_pairs={{0,1},{1,0},{2,3},{3,2},{4,5},{5,4},{6,7},{7,6},{8,9},{9,8},{10,11... | collective-permute-start | bytes 147464 | tf_op jit(solution)/shard_map/ppermute | solution.py:82
  15.7 3.5 %all-to-all-start = ((f32[8,96,128]{2,1,0:T(8,128)}), f32[8,96,128]{2,1,0:T(8,128)S(1)}, u32[]{:S(2)}, u32[]{:S(2)}) async-start(f32[8,96,128]{2,1,0:T(8,128)} %broadcast_in_dim.8), calls=%async_computation | async-start | bytes 786432 | tf_op jit(solution)/shard_map/all_to_all | solution.py:86
  19.9 9.0 %all-to-all-done.sums_ref = f32[8,96,128]{2,1,0:T(8,128)S(1)} async-done(((f32[8,96,128]{2,1,0:T(8,128)}), f32[8,96,128]{2,1,0:T(8,128)S(1)}, u32[]{:S(2)}, u32[]{:S(2)}) %all-to-all-start) | async-done | bytes 393248 | tf_op jit(solution)/shard_map/all_to_all | solution.py:86
  28.8 3.9 %shard_map.28 = (f32[128,128]{1,0:T(8,128)S(1)}, f32[128,128]{1,0:T(8,128)S(1)}) custom-call(s32[1]{0:T(128)} %bitcast.side_ref, f32[8,96,128]{2,1,0:T(8,128)S(1)} %all-to-all-done.sums_ref), custom_call_target="tpu_custom_call" | custom-call | flops 200000000 | bytes 500000 | tf_op jit(solution)/shard_map/pallas_call | solution.py:68
  32.7 2.4 %convolution_bitcast_fusion = f32[4096,64]{0,1:T(8,128)S(1)} fusion(f32[4096,128]{1,0:T(8,128)S(1)} %copy-done, f32[128,128]{1,0:T(8,128)S(1)} %get-tuple-element.11), kind=kOutput, calls=%fused_computation | convolution fusion | flops 402653184 | bytes 3211264 | tf_op jit(solution)/shard_map/dot_general | solution.py:16
  35.1 1.9 collective-permute-start.1
  38.1 2.3 %fusion.30 = f32[64,4096]{1,0:T(8,128)S(1)} fusion(f32[4096,128]{1,0:T(8,128)S(1)} %copy-done, f32[128,128]{1,0:T(8,128)S(1)} %get-tuple-element.11), kind=kOutput, calls=%fused_computation.35 | convolution fusion | flops 402653184 | bytes 3211264 | tf_op jit(solution)/shard_map/dot_general | solution.py:16
  40.4 25.6 %collective-permute-done.1 = f32[4096,64]{0,1:T(8,128)S(1)} collective-permute-done((f32[4096,64]{0,1:T(8,128)S(1)}, f32[4096,64]{0,1:T(8,128)S(1)}, u32[]{:S(2)}, u32[]{:S(2)}) %collective-permute-start.1) | collective-permute-done | bytes 1048608 | tf_op jit(solution)/shard_map/ppermute | solution.py:21
  68.8 5.5 %all-to-all-start.1 = ((f32[16,32,128]{2,1,0:T(8,128)}), f32[16,32,128]{2,1,0:T(8,128)S(1)}, u32[]{:S(2)}, u32[]{:S(2)}) async-start(f32[16,32,128]{2,1,0:T(8,128)} %broadcast_in_dim.9), calls=%async_computation.1 | async-start | bytes 524288 | tf_op jit(solution)/shard_map/all_to_all | solution.py:86
  74.6 2.1 collective-permute-start.2
  77.9 3.8 %collective-permute-done.2.refs_1_ = f32[64,64]{1,0:T(8,128)S(1)} collective-permute-done((f32[64,64]{1,0:T(8,128)S(1)}, f32[64,64]{1,0:T(8,128)S(1)}, u32[]{:S(2)}, u32[]{:S(2)}) %collective-permute-start.2) | collective-permute-done | bytes 16416 | tf_op jit(solution)/shard_map/ppermute | solution.py:21
  83.0 3.9 %shard_map.29 = (f32[128,128]{1,0:T(8,128)}, f32[128,128]{1,0:T(8,128)S(1)}) custom-call(s32[1]{0:T(128)} %bitcast.3.side_ref, f32[16,32,128]{2,1,0:T(8,128)S(1)} %all-to-all-done.1.sums_ref, f32[64,64]{1,0:T(8,128)S(1)} %fusion.26.refs_0_, f32[64,64]{1,0:T(8,128)S(1)} %collective-permute-done.2.refs_1_), custom_call_target="tpu_custom_call" | custom-call | flops 200000000 | bytes 500000 | tf_op jit(solution)/shard_map/pallas_call | solution.py:68
  86.9 2.6 %fusion.2 = f32[4096,64]{0,1:T(8,128)S(1)} fusion(f32[4096,64]{0,1:T(8,128)} %copy-done.3, f32[4096,64]{0,1:T(8,128)S(1)} %bitcast.23, f32[128,128]{1,0:T(8,128)S(1)} %get-tuple-element.13), kind=kOutput, calls=%fused_computation.7 | convolution fusion | flops 403177472 | bytes 3211264 | tf_op jit(solution)/shard_map/dot_general | solution.py:16
  89.5 1.9 collective-permute-start.3
  92.7 24.0 %collective-permute-done.3 = f32[4096,64]{0,1:T(8,128)S(1)} collective-permute-done((f32[4096,64]{0,1:T(8,128)S(1)}, f32[4096,64]{0,1:T(8,128)S(1)}, u32[]{:S(2)}, u32[]{:S(2)}) %collective-permute-start.3) | collective-permute-done | bytes 1048608 | tf_op jit(solution)/shard_map/ppermute | solution.py:21
  116.8 1.8 fusion.6
  118.7 4.2 %collective-permute-start.4 = (f32[96,128]{1,0:T(8,128)S(1)}, f32[96,128]{1,0:T(8,128)S(1)}, u32[]{:S(2)}, u32[]{:S(2)}) collective-permute-start(f32[96,128]{1,0:T(8,128)S(1)} %maximum_maximum_fusion.1), channel_id=1, source_target_pairs={{0,1},{1,0},{2,3},{3,2},{4,5},{5,4},{6,7},{7,6},{8,9},{9,8},{10,11... | collective-permute-start | bytes 147464 | tf_op jit(solution)/shard_map/ppermute | solution.py:82
  123.9 14.2 %all_to_all.20.sums_ref = f32[8,96,128]{2,1,0:T(8,128)S(1)} all-to-all(f32[8,96,128]{2,1,0:T(8,128)S(1)} %broadcast_in_dim.10), channel_id=1, replica_groups={{0,2,4,6,8,10,12,14},{1,3,5,7,9,11,13,15},{16,18,20,22,24,26,28,30},{17..., dimensions={0} | all-to-all | bytes 786432 | tf_op jit(solution)/shard_map/all_to_all | solution.py:86
  138.0 3.8 %shard_map.30 = (f32[128,128]{1,0:T(8,128)S(1)}, f32[128,128]{1,0:T(8,128)S(1)}) custom-call(s32[1]{0:T(128)} %bitcast.4.side_ref, f32[8,96,128]{2,1,0:T(8,128)S(1)} %all_to_all.20.sums_ref), custom_call_target="tpu_custom_call" | custom-call | flops 200000000 | bytes 500000 | tf_op jit(solution)/shard_map/pallas_call | solution.py:68
  143.2 1.9 collective-permute-start.5
  147.6 22.4 %collective-permute-done.5 = f32[4096,64]{0,1:T(8,128)S(1)} collective-permute-done((f32[4096,64]{0,1:T(8,128)S(1)}, f32[4096,64]{0,1:T(8,128)S(1)}, u32[]{:S(2)}, u32[]{:S(2)}) %collective-permute-start.5) | collective-permute-done | bytes 1048608 | tf_op jit(solution)/shard_map/ppermute | solution.py:21
  172.8 6.4 %all-to-all-start.3 = ((f32[16,32,128]{2,1,0:T(8,128)}), f32[16,32,128]{2,1,0:T(8,128)S(1)}, u32[]{:S(2)}, u32[]{:S(2)}) async-start(f32[16,32,128]{2,1,0:T(8,128)} %broadcast_in_dim.11), calls=%async_computation.3 | async-start | bytes 524288 | tf_op jit(solution)/shard_map/all_to_all | solution.py:86
  179.6 1.9 collective-permute-start.6
  182.6 4.0 %collective-permute-done.6.refs_1_ = f32[64,64]{1,0:T(8,128)S(1)} collective-permute-done((f32[64,64]{1,0:T(8,128)S(1)}, f32[64,64]{1,0:T(8,128)S(1)}, u32[]{:S(2)}, u32[]{:S(2)}) %collective-permute-start.6) | collective-permute-done | bytes 16416 | tf_op jit(solution)/shard_map/ppermute | solution.py:21
  187.9 3.8 %shard_map.31 = (f32[128,128]{1,0:T(8,128)}, f32[128,128]{1,0:T(8,128)S(1)}) custom-call(s32[1]{0:T(128)} %bitcast.5.side_ref, f32[16,32,128]{2,1,0:T(8,128)S(1)} %all-to-all-done.3.sums_ref, f32[64,64]{1,0:T(8,128)S(1)} %fusion.16.refs_0_, f32[64,64]{1,0:T(8,128)S(1)} %collective-permute-done.6.refs_1_), custom_call_target="tpu_custom_call" | custom-call | flops 200000000 | bytes 500000 | tf_op jit(solution)/shard_map/pallas_call | solution.py:68
  191.7 2.6 %fusion = f32[4096,64]{0,1:T(8,128)S(1)} fusion(f32[4096,64]{0,1:T(8,128)} %copy-done.1, f32[4096,64]{0,1:T(8,128)S(1)} %fusion.5, f32[128,128]{1,0:T(8,128)S(1)} %get-tuple-element.16), kind=kOutput, calls=%fused_computation.5 | convolution fusion | flops 403177472 | bytes 3211264 | tf_op jit(solution)/shard_map/dot_general | solution.py:16
  194.3 1.9 collective-permute-start.7
  197.6 24.0 %collective-permute-done.7 = f32[4096,64]{0,1:T(8,128)S(1)} collective-permute-done((f32[4096,64]{0,1:T(8,128)S(1)}, f32[4096,64]{0,1:T(8,128)S(1)}, u32[]{:S(2)}, u32[]{:S(2)}) %collective-permute-start.7) | collective-permute-done | bytes 1048608 | tf_op jit(solution)/shard_map/ppermute | solution.py:21
  221.6 1.5 pad_maximum_fusion.3
  223.1 2.9 %copy.3 = f32[4096,128]{1,0:T(8,128)} copy(f32[4096,128]{0,1:T(8,128)} %pad_maximum_fusion.3) | data formatting | bytes 4194304 | tf_op jit(solution)/shard_map/concatenate | solution.py:113
  (46 shorter events, 22.2 us)
Async XLA Ops:
  0.0 1.6 copy-start
  1.6 17.6 %copy-start.5 = (s32[4,1]{0,1:T(1,128)S(1)}, s32[4,1]{0,1:T(1,128)}, u32[]{:S(2)}) copy-start(s32[4,1]{0,1:T(1,128)} %param.3) | copy-start | bytes 52
  5.2 9.6 %collective-permute-start = (f32[96,128]{1,0:T(8,128)S(1)}, f32[96,128]{1,0:T(8,128)S(1)}, u32[]{:S(2)}, u32[]{:S(2)}) collective-permute-start(f32[96,128]{1,0:T(8,128)S(1)} %maximum_maximum_fusion), channel_id=1, source_target_pairs={{0,1},{1,0},{2,3},{3,2},{4,5},{5,4},{6,7},{7,6},{8,9},{9,8},{10,11... | collective-permute-start | bytes 147464 | tf_op jit(solution)/shard_map/ppermute | solution.py:82
  15.7 13.1 %all-to-all-start = ((f32[8,96,128]{2,1,0:T(8,128)}), f32[8,96,128]{2,1,0:T(8,128)S(1)}, u32[]{:S(2)}, u32[]{:S(2)}) async-start(f32[8,96,128]{2,1,0:T(8,128)} %broadcast_in_dim.8), calls=%async_computation | async-start | bytes 786432 | tf_op jit(solution)/shard_map/all_to_all | solution.py:86
  35.1 30.9 %collective-permute-start.1 = (f32[4096,64]{0,1:T(8,128)S(1)}, f32[4096,64]{0,1:T(8,128)S(1)}, u32[]{:S(2)}, u32[]{:S(2)}) collective-permute-start(f32[4096,64]{0,1:T(8,128)S(1)} %convolution_bitcast_fusion), channel_id=1, source_target_pairs={{0,16},{16,32},{32,48},{48,64},{64,80},{80,96},{96,112},{112,128},... | collective-permute-start | bytes 3145736 | tf_op jit(solution)/shard_map/ppermute | solution.py:21
  66.0 1.0 copy-start.3
  68.8 14.2 %all-to-all-start.1 = ((f32[16,32,128]{2,1,0:T(8,128)}), f32[16,32,128]{2,1,0:T(8,128)S(1)}, u32[]{:S(2)}, u32[]{:S(2)}) async-start(f32[16,32,128]{2,1,0:T(8,128)} %broadcast_in_dim.9), calls=%async_computation.1 | async-start | bytes 524288 | tf_op jit(solution)/shard_map/all_to_all | solution.py:86
  74.6 7.1 %collective-permute-start.2 = (f32[64,64]{1,0:T(8,128)S(1)}, f32[64,64]{1,0:T(8,128)S(1)}, u32[]{:S(2)}, u32[]{:S(2)}) collective-permute-start(f32[64,64]{1,0:T(8,128)S(1)} %fusion.21), channel_id=1, source_target_pairs={{0,16},{16,32},{32,48},{48,64},{64,80},{80,96},{96,112},{112,128},... | collective-permute-start | bytes 49160 | tf_op jit(solution)/shard_map/ppermute | solution.py:21
  83.0 8.4 %copy-start.4 = (f32[4096,64]{0,1:T(8,128)S(1)}, f32[4096,64]{0,1:T(8,128)}, u32[]{:S(2)}) copy-start(f32[4096,64]{0,1:T(8,128)} %copy-done.3) | copy-start | bytes 3145732
  89.5 27.3 %collective-permute-start.3 = (f32[4096,64]{0,1:T(8,128)S(1)}, f32[4096,64]{0,1:T(8,128)S(1)}, u32[]{:S(2)}, u32[]{:S(2)}) collective-permute-start(f32[4096,64]{0,1:T(8,128)S(1)} %fusion.2), channel_id=1, source_target_pairs={{0,16},{16,32},{32,48},{48,64},{64,80},{80,96},{96,112},{112,128},... | collective-permute-start | bytes 3145736 | tf_op jit(solution)/shard_map/ppermute | solution.py:21
  118.7 5.0 %collective-permute-start.4 = (f32[96,128]{1,0:T(8,128)S(1)}, f32[96,128]{1,0:T(8,128)S(1)}, u32[]{:S(2)}, u32[]{:S(2)}) collective-permute-start(f32[96,128]{1,0:T(8,128)S(1)} %maximum_maximum_fusion.1), channel_id=1, source_target_pairs={{0,1},{1,0},{2,3},{3,2},{4,5},{5,4},{6,7},{7,6},{8,9},{9,8},{10,11... | collective-permute-start | bytes 147464 | tf_op jit(solution)/shard_map/ppermute | solution.py:82
  143.2 26.8 %collective-permute-start.5 = (f32[4096,64]{0,1:T(8,128)S(1)}, f32[4096,64]{0,1:T(8,128)S(1)}, u32[]{:S(2)}, u32[]{:S(2)}) collective-permute-start(f32[4096,64]{0,1:T(8,128)S(1)} %fusion.4), channel_id=1, source_target_pairs={{0,16},{16,32},{32,48},{48,64},{64,80},{80,96},{96,112},{112,128},... | collective-permute-start | bytes 3145736 | tf_op jit(solution)/shard_map/ppermute | solution.py:21
  170.0 1.0 copy-start.1
  172.8 15.1 %all-to-all-start.3 = ((f32[16,32,128]{2,1,0:T(8,128)}), f32[16,32,128]{2,1,0:T(8,128)S(1)}, u32[]{:S(2)}, u32[]{:S(2)}) async-start(f32[16,32,128]{2,1,0:T(8,128)} %broadcast_in_dim.11), calls=%async_computation.3 | async-start | bytes 524288 | tf_op jit(solution)/shard_map/all_to_all | solution.py:86
  179.6 7.1 %collective-permute-start.6 = (f32[64,64]{1,0:T(8,128)S(1)}, f32[64,64]{1,0:T(8,128)S(1)}, u32[]{:S(2)}, u32[]{:S(2)}) collective-permute-start(f32[64,64]{1,0:T(8,128)S(1)} %fusion.11), channel_id=1, source_target_pairs={{0,16},{16,32},{32,48},{48,64},{64,80},{80,96},{96,112},{112,128},... | collective-permute-start | bytes 49160 | tf_op jit(solution)/shard_map/ppermute | solution.py:21
  187.9 8.4 %copy-start.2 = (f32[4096,64]{0,1:T(8,128)S(1)}, f32[4096,64]{0,1:T(8,128)}, u32[]{:S(2)}) copy-start(f32[4096,64]{0,1:T(8,128)} %copy-done.1) | copy-start | bytes 3145732
  194.3 27.3 %collective-permute-start.7 = (f32[4096,64]{0,1:T(8,128)S(1)}, f32[4096,64]{0,1:T(8,128)S(1)}, u32[]{:S(2)}, u32[]{:S(2)}) collective-permute-start(f32[4096,64]{0,1:T(8,128)S(1)} %fusion), channel_id=1, source_target_pairs={{0,16},{16,32},{32,48},{48,64},{64,80},{80,96},{96,112},{112,128},... | collective-permute-start | bytes 3145736 | tf_op jit(solution)/shard_map/ppermute | solution.py:21

commit v4 on v3

v4 whole, which is shorter than its diff:
```python
import functools

import jax
import jax.numpy as jnp
from jax import lax
from jax.experimental import pallas as pl
from jax.experimental.pallas import tpu as pltpu
from jax.sharding import PartitionSpec as P

ROUNDS = 4
NS_STEPS = 6
HIGHEST = lax.Precision.HIGHEST
IN_VMEM = pl.BlockSpec(memory_space=pltpu.VMEM)


def mul(a, b):
    return jnp.dot(a, b, precision=HIGHEST)


def terms(x):
    first = x.astype(jnp.bfloat16)
    rest = x - first.astype(jnp.float32)
    second = rest.astype(jnp.bfloat16)
    third = (rest - second.astype(jnp.float32)).astype(jnp.bfloat16)
    return first, second, third


def mul_terms(a, b):
    left = jnp.concatenate([a[0], a[0], a[0], a[1], a[1], a[2]], axis=1)
    right = jnp.concatenate([b[0], b[1], b[2], b[0], b[1], b[0]], axis=0)
    return jnp.dot(left, right, preferred_element_type=jnp.float32)


def added_up(products, height, width):
    block = lambda i, j: products[i * height : (i + 1) * height, j * width : (j + 1) * width]
    small = (block(2, 2) + (block(1, 2) + block(2, 1))) + (block(0, 2) + block(2, 0) + block(1, 1))
    return small + (block(0, 1) + block(1, 0)) + block(0, 0)


def passed_along(shard, axis, by):
    peers = lax.axis_size(axis)
    return lax.ppermute(shard, axis, [(i, (i + by) % peers) for i in range(peers)])


def turn_kernel(total_rows, cross, side_ref, sums_ref, *refs):
    if cross:
        gram_stay_ref, gram_arrived_ref, gram_ref, turn_ref = refs
    else:
        gram_ref, turn_ref = refs
    order = gram_ref.shape[0]
    width = order // 2
    total = sums_ref[0]
    for device in range(1, sums_ref.shape[0]):
        total = total + sums_ref[device]
    if cross:
        block = jnp.concatenate([total[:, :width], total[:, width:]], axis=0)
        gram_ref[:width, :width] = gram_stay_ref[...]
        gram_ref[:width, width:] = block
        gram_ref[width:, :width] = block.T
        gram_ref[width:, width:] = gram_arrived_ref[...]
    else:
        gram_ref[:width, :] = total[:width]
        gram_ref[width:, :width] = total[:width, width:].T
        gram_ref[width:, width:] = jnp.concatenate([total[width:, :width], total[width:, width:]], axis=0)
    gram = gram_ref[...]
    scale = jnp.sqrt(jnp.sum(gram * gram) + 1e-06)
    down = lax.broadcasted_iota(jnp.int32, (order, order), 0)
    along = lax.broadcasted_iota(jnp.int32, (order, order), 1)
    half_more = jnp.where(down == along, 1.5, 0.0).astype(jnp.float32)
    ymat = gram / scale
    stepper = half_more - 0.5 * ymat
    beside = lambda y, z: [jnp.concatenate(pair, axis=1) for pair in zip(y, z)]
    z_terms = terms(stepper)
    y_terms = terms(mul_terms(z_terms, terms(ymat)))
    for step in range(1, NS_STEPS):
        stepper = half_more - 0.5 * mul_terms(z_terms, y_terms)
        if step + 1 < NS_STEPS:
            both = mul_terms(terms(stepper), beside(y_terms, z_terms))
            y_terms, z_terms = terms(both[:, :order]), terms(both[:, order:])
        else:
            zmat = mul_terms(terms(stepper), z_terms)
    zmat = zmat * jnp.sqrt(total_rows / scale)
    swapped = pltpu.roll(zmat, width, 0)
    turn_ref[...] = jnp.where(side_ref[0] == 0, zmat, swapped)


def turned(sums, side, total_rows, blocks=()):
    order = sums.shape[-1]
    square = jax.ShapeDtypeStruct((order, order), jnp.float32)
    return pl.pallas_call(
        functools.partial(turn_kernel, total_rows, bool(blocks)),
        out_shape=(square, square),
        in_specs=[pl.BlockSpec(memory_space=pltpu.SMEM)] + [IN_VMEM] * (1 + len(blocks)),
        out_specs=(IN_VMEM, IN_VMEM),
        compiler_params=pltpu.CompilerParams(vmem_limit_bytes=4 << 20),
        cost_estimate=pl.CostEstimate(flops=200_000_000, bytes_accessed=500_000, transcendentals=0),
    )(side, sums, *blocks)


def shares(copies):
    return lax.all_to_all(copies, "row", 0, 0)


def shares_of_chips(part):
    peers = lax.axis_size("row")
    part = part + lax.ppermute(part, "row", [(i, i ^ 1) for i in range(peers)])
    groups = [[core + 2 * chip for chip in range(peers // 2)] for core in range(2)]
    copies = jnp.broadcast_to(part[None], (peers // 2,) + part.shape)
    return lax.all_to_all(copies, "row", 0, 0, axis_index_groups=groups)


def folded(block):
    half = block.shape[0] // 2
    return jnp.concatenate([block[:half], block[half:]], axis=1)


def packed_gram(gram):
    width = gram.shape[0] // 2
    return jnp.concatenate([gram[:width], folded(gram[width:, width:])], axis=0)


def mul_nt(a, b):
    return lax.dot_general(a, b, (((1,), (1,)), ((), ())), precision=HIGHEST, preferred_element_type=jnp.float32)


def entry_kernel(x_ref, xt_ref, part_ref):
    pieces = 8
    height = x_ref.shape[0] // pieces
    gram = None
    for piece in range(pieces):
        slab = x_ref[piece * height : (piece + 1) * height, :]
        turned_over = slab.T
        xt_ref[:, piece * height : (piece + 1) * height] = turned_over
        product = jnp.dot(
            jnp.concatenate(terms(turned_over), axis=0),
            jnp.concatenate(terms(slab), axis=1),
            preferred_element_type=jnp.float32,
        )
        gram = product if gram is None else gram + product
    part_ref[...] = packed_gram(added_up(gram, gram.shape[0] // 3, gram.shape[1] // 3))


def entry(matrix):
    rows, order = matrix.shape
    return pl.pallas_call(
        entry_kernel,
        out_shape=(
            jax.ShapeDtypeStruct((order, rows), jnp.float32),
            jax.ShapeDtypeStruct((3 * order // 4, order), jnp.float32),
        ),
        in_specs=[IN_VMEM],
        out_specs=(IN_VMEM, IN_VMEM),
        compiler_params=pltpu.CompilerParams(vmem_limit_bytes=10 << 20),
        cost_estimate=pl.CostEstimate(flops=800_000_000, bytes_accessed=4_000_000, transcendentals=0),
    )(matrix)


def gram_kernel(stay_ref, arrived_ref, part_ref):
    rows = stay_ref.shape[1]
    whole = len(part_ref.shape) == 2
    pieces = 4
    length = rows // pieces
    gram = None
    for piece in range(pieces):
        where = slice(piece * length, (piece + 1) * length)
        left, right = stay_ref[:, where], arrived_ref[:, where]
        if whole:
            left = right = jnp.concatenate([left, right], axis=0)
        left = jnp.concatenate(terms(left), axis=0)
        right = left if whole else jnp.concatenate(terms(right), axis=0)
        product = lax.dot_general(left, right, (((1,), (1,)), ((), ())), preferred_element_type=jnp.float32)
        gram = product if gram is None else gram + product
    gram = added_up(gram, gram.shape[0] // 3, gram.shape[1] // 3)
    if whole:
        part_ref[...] = packed_gram(gram)
    else:
        packed = folded(gram)
        for device in range(part_ref.shape[0]):
            part_ref[device] = packed


def gram_part(stay, arrived, copies=None):
    width = stay.shape[0]
    shape = (3 * width // 2, 2 * width) if copies is None else (copies, width // 2, 2 * width)
    return pl.pallas_call(
        gram_kernel,
        out_shape=jax.ShapeDtypeStruct(shape, jnp.float32),
        in_specs=[IN_VMEM, IN_VMEM],
        out_specs=IN_VMEM,
        compiler_params=pltpu.CompilerParams(vmem_limit_bytes=8 << 20),
        cost_estimate=pl.CostEstimate(flops=400_000_000, bytes_accessed=3_000_000, transcendentals=0),
    )(stay, arrived)


def exit_kernel(stay_ref, arrived_ref, out_ref, held_ref, sems):
    pieces = sems.shape[0]
    height = out_ref.shape[0] // pieces
    copies = []
    for piece in range(pieces):
        where = slice(piece * height, (piece + 1) * height)
        held_ref[where, :] = jnp.concatenate([stay_ref[:, where], arrived_ref[:, where]], axis=0).T
        rows = pl.ds(piece * height, height)
        copy = pltpu.make_async_copy(held_ref.at[rows], out_ref.at[rows], sems.at[piece])
        copy.start()
        copies.append(copy)
    for copy in copies:
        copy.wait()


def assembled(stay, arrived):
    width, rows = stay.shape
    pieces = 8
    return pl.pallas_call(
        exit_kernel,
        out_shape=jax.ShapeDtypeStruct((rows, 2 * width), jnp.float32),
        in_specs=[IN_VMEM, IN_VMEM],
        out_specs=pl.BlockSpec(memory_space=pltpu.HBM),
        scratch_shapes=[pltpu.VMEM((rows, 2 * width), jnp.float32), pltpu.SemaphoreType.DMA((pieces,))],
        compiler_params=pltpu.CompilerParams(vmem_limit_bytes=8 << 20),
        cost_estimate=pl.CostEstimate(flops=0, bytes_accessed=4_000_000, transcendentals=0),
    )(stay, arrived)


def local(matrix, stay_side):
    rows, width = matrix.shape[0], matrix.shape[1] // 2
    total_rows = float(rows * lax.axis_size("row"))
    peers = lax.axis_size("row")
    current, part = entry(matrix)
    gram, turn = turned(shares_of_chips(part), stay_side[0], total_rows)
    for round_index in range(ROUNDS):
        following = round_index + 1
        to_stay, to_move = turn[:width], turn[width:]
        arrived = passed_along(mul(to_move, current), "pair", 1)
        stay = mul(to_stay, current)
        if following == ROUNDS:
            return assembled(stay, arrived)
        current = jnp.concatenate([stay, arrived], axis=0)
        if following % 2 == 0:
            gram, turn = turned(shares_of_chips(gram_part(stay, arrived)), stay_side[following], total_rows)
        else:
            gram_stay = mul_nt(mul(to_stay, gram), to_stay)
            gram_arrived = passed_along(mul_nt(mul(to_move, gram), to_move), "pair", 1)
            arrived, gram_arrived = lax.optimization_barrier((arrived, gram_arrived))
            current = jnp.concatenate([stay, arrived], axis=0)
            copies = gram_part(stay, arrived, peers)
            gram, turn = turned(shares(copies), stay_side[following], total_rows, (gram_stay, gram_arrived))


def solution(mesh):
    return jax.shard_map(
        local,
        mesh=mesh,
        in_specs=(P("row", "pair"), P(None, "pair")),
        out_specs=P("row", "pair"),
        check_vma=False,
    )
```

time: 227 us -> 212 us (0.934)
  matrix products: 27.5 us -> 12.8 us
  local copies, waits for them, and re-layouts: 9.54 us -> 3.05 us
  Pallas kernels: 15.4 us -> 21 us
  waiting for transfers between devices: 117 us -> 122 us
  blocking collectives: 14.2 us -> 11.9 us
    dot_general x20 -> x12, matrix products: 27.5 us -> 12 us  [mul(): return jnp.dot(a, b, precision=HIGHEST)]
    all_to_all x3, waiting for transfers between devices: 11.5 us -> 25.6 us  [the longest x2 16.6 us: shares(): return lax.all_to_all(copies, 'row', 0, 0)]
    ppermute x6, waiting for transfers between devices: 104 us -> 94.8 us  [passed_along(): lax.ppermute(shard, axis, [(i, (i + by) % peers) for i in range(peers)])]
    pallas_call x0 -> x5, Pallas kernels: none -> 8.35 us  [the longest x3 4.93 us: gram_part(): pl.pallas_call(gram_kernel, out_shape=jax.ShapeDtypeStruct(shape, jnp.flo...]
    concatenate x1 -> x0, local copies, waits for them, and re-layouts: 2.88 us -> none  [local(): return jnp.concatenate([stay, arrived], axis=1)]
    pallas_call x4, Pallas kernels: 15.4 us -> 12.7 us  [turned(): pl.pallas_call(functools.partial(turn_kernel, total_rows, bool(blocks)),...]
  transfers between devices with their start and end apart: 11 -> 11, of which waited for: 11 -> 9; matrix products, arithmetic and copies ran while one was open for 5% -> 4% of each run, Pallas kernels for 0% -> 0%
where the time goes in v4:
time: 212 us; the launch traced here: 211 us
  waiting for transfers between devices  122 us (58%)
  starting transfers between devices  40.1 us (19%)
  Pallas kernels  21 us (10%)
  matrix products  12.8 us (6%)
  blocking collectives  11.9 us (6%)
  local copies, waits for them, and re-layouts  3.05 us (1%)
    ppermute x6, waiting for transfers between devices, passed_along(): lax.ppermute(shard, axis, [(i, (i + by) % peers) for i in range(peers)])  94.8 us
    all_to_all x2, waiting for transfers between devices, shares(): return lax.all_to_all(copies, 'row', 0, 0)  16.6 us
    pallas_call x4, Pallas kernels, turned(): pl.pallas_call(functools.partial(turn_kernel, total_rows, bool(blocks)),...  12.7 us
    ppermute x2, starting transfers between devices, shares_of_chips(): part = part + lax.ppermute(part, 'row', [(i, i ^ 1) for i in range(peers)])  12.6 us
    ppermute x6, starting transfers between devices, passed_along(): lax.ppermute(shard, axis, [(i, (i + by) % peers) for i in range(peers)])  12.3 us
    dot_general x12, matrix products, mul(): return jnp.dot(a, b, precision=HIGHEST)  12 us
    all_to_all x1, blocking collectives, shares_of_chips(): return lax.all_to_all(copies, 'row', 0, 0, axis_index_groups=groups)  11.9 us
    all_to_all x2, starting transfers between devices, shares(): return lax.all_to_all(copies, 'row', 0, 0)  11.8 us
  transfers between devices with their start and end apart: 11, of which 9 were waited for; matrix products, arithmetic and copies ran while one was open for 4% of the time, Pallas kernels for 0%

profile of v4, /device:TPU:1, one launch (start us, length us, event | category | flops | bytes accessed | tf_op | source)
XLA Modules:
  0.0 211.5 jit_solution(13490649094586495932)
XLA Ops:
  0.0 1.6 copy-done.1
  1.6 1.9 shard_map.28
  3.5 8.8 %collective-permute-start = (f32[96,128]{1,0:T(8,128)S(1)}, f32[96,128]{1,0:T(8,128)S(1)}, u32[]{:S(2)}, u32[]{:S(2)}) collective-permute-start(f32[96,128]{1,0:T(8,128)S(1)} %get-tuple-element.17), channel_id=1, source_target_pairs={{0,1},{1,0},{2,3},{3,2},{4,5},{5,4},{6,7},{7,6},{8,9},{9,8},{10,11... | collective-permute-start | bytes 147464 | tf_op jit(solution)/shard_map/ppermute | solution.py:106
  14.0 3.5 %all-to-all-start = ((f32[8,96,128]{2,1,0:T(8,128)}), f32[8,96,128]{2,1,0:T(8,128)S(1)}, u32[]{:S(2)}, u32[]{:S(2)}) async-start(f32[8,96,128]{2,1,0:T(8,128)} %broadcast_in_dim.4), calls=%async_computation | async-start | bytes 786432 | tf_op jit(solution)/shard_map/all_to_all | solution.py:109
  18.1 9.0 %all-to-all-done.sums_ref = f32[8,96,128]{2,1,0:T(8,128)S(1)} async-done(((f32[8,96,128]{2,1,0:T(8,128)}), f32[8,96,128]{2,1,0:T(8,128)S(1)}, u32[]{:S(2)}, u32[]{:S(2)}) %all-to-all-start) | async-done | bytes 393248 | tf_op jit(solution)/shard_map/all_to_all | solution.py:109
  27.0 3.1 %shard_map.29 = (f32[128,128]{1,0:T(8,128)S(1)}, f32[128,128]{1,0:T(8,128)S(1)}) custom-call(s32[1]{0:T(128)} %bitcast.3.side_ref, f32[8,96,128]{2,1,0:T(8,128)S(1)} %all-to-all-done.sums_ref), custom_call_target="tpu_custom_call" | custom-call | flops 200000000 | bytes 500000 | tf_op jit(solution)/shard_map/pallas_call | solution.py:90
  31.4 1.9 collective-permute-start.1
  33.7 2.5 %collective-permute-start.2 = (f32[64,64]{1,0:T(8,128)S(1)}, f32[64,64]{1,0:T(8,128)S(1)}, u32[]{:S(2)}, u32[]{:S(2)}) collective-permute-start(f32[64,64]{1,0:T(8,128)S(1)} %fusion.20), channel_id=1, source_target_pairs={{0,16},{16,32},{32,48},{48,64},{64,80},{80,96},{96,112},{112,128},... | collective-permute-start | bytes 49160 | tf_op jit(solution)/shard_map/ppermute | solution.py:42
  36.3 2.8 %fusion.30.stay_ref = f32[64,4096]{1,0:T(8,128)S(1)} fusion(f32[128,4096]{1,0:T(8,128)} %copy-done, f32[128,128]{1,0:T(8,128)S(1)} %get-tuple-element.18), kind=kOutput, calls=%fused_computation.33 | convolution fusion | flops 402653184 | bytes 3178496 | tf_op jit(solution)/shard_map/dot_general | solution.py:17
  39.1 24.0 %collective-permute-done.2.refs_1_ = f32[64,64]{1,0:T(8,128)S(1)} collective-permute-done((f32[64,64]{1,0:T(8,128)S(1)}, f32[64,64]{1,0:T(8,128)S(1)}, u32[]{:S(2)}, u32[]{:S(2)}) %collective-permute-start.2) | collective-permute-done | bytes 16416 | tf_op jit(solution)/shard_map/ppermute | solution.py:42
  63.0 1.5 shard_map.30
  64.6 5.5 %all-to-all-start.1 = ((f32[16,32,128]{2,1,0:T(8,128)}), f32[16,32,128]{2,1,0:T(8,128)S(1)}, u32[]{:S(2)}, u32[]{:S(2)}) async-start(f32[16,32,128]{2,1,0:T(8,128)} %shard_map.30), calls=%async_computation.1 | async-start | bytes 524288 | tf_op jit(solution)/shard_map/all_to_all | solution.py:101
  70.5 8.3 %all-to-all-done.1.sums_ref = f32[16,32,128]{2,1,0:T(8,128)S(1)} async-done(((f32[16,32,128]{2,1,0:T(8,128)}), f32[16,32,128]{2,1,0:T(8,128)S(1)}, u32[]{:S(2)}, u32[]{:S(2)}) %all-to-all-start.1) | async-done | bytes 262176 | tf_op jit(solution)/shard_map/all_to_all | solution.py:101
  78.8 3.2 %shard_map.31 = (f32[128,128]{1,0:T(8,128)}, f32[128,128]{1,0:T(8,128)S(1)}) custom-call(s32[1]{0:T(128)} %bitcast.2.side_ref, f32[16,32,128]{2,1,0:T(8,128)S(1)} %all-to-all-done.1.sums_ref, f32[64,64]{1,0:T(8,128)S(1)} %fusion.26.refs_0_, f32[64,64]{1,0:T(8,128)S(1)} %collective-permute-done.2.refs_1_), custom_call_target="tpu_custom_call" | custom-call | flops 200000000 | bytes 500000 | tf_op jit(solution)/shard_map/pallas_call | solution.py:90
  83.2 2.1 collective-permute-start.3
  85.3 1.2 fusion.5.stay_ref
  86.6 24.3 %collective-permute-done.3.arrived_ref = f32[64,4096]{1,0:T(8,128)S(1)} collective-permute-done((f32[64,4096]{1,0:T(8,128)S(1)}, f32[64,4096]{1,0:T(8,128)S(1)}, u32[]{:S(2)}, u32[]{:S(2)}) %collective-permute-start.3) | collective-permute-done | bytes 1048608 | tf_op jit(solution)/shard_map/ppermute | solution.py:42
  110.9 1.9 shard_map.32
  112.8 3.8 %collective-permute-start.4 = (f32[96,128]{1,0:T(8,128)S(1)}, f32[96,128]{1,0:T(8,128)S(1)}, u32[]{:S(2)}, u32[]{:S(2)}) collective-permute-start(f32[96,128]{1,0:T(8,128)S(1)} %shard_map.32), channel_id=1, source_target_pairs={{0,1},{1,0},{2,3},{3,2},{4,5},{5,4},{6,7},{7,6},{8,9},{9,8},{10,11... | collective-permute-start | bytes 147464 | tf_op jit(solution)/shard_map/ppermute | solution.py:106
  117.5 11.9 %all_to_all.20.sums_ref = f32[8,96,128]{2,1,0:T(8,128)S(1)} all-to-all(f32[8,96,128]{2,1,0:T(8,128)S(1)} %broadcast_in_dim.5), channel_id=1, replica_groups={{0,2,4,6,8,10,12,14},{1,3,5,7,9,11,13,15},{16,18,20,22,24,26,28,30},{17..., dimensions={0} | all-to-all | bytes 786432 | tf_op jit(solution)/shard_map/all_to_all | solution.py:109
  129.4 3.2 %shard_map.33 = (f32[128,128]{1,0:T(8,128)S(1)}, f32[128,128]{1,0:T(8,128)S(1)}) custom-call(s32[1]{0:T(128)} %bitcast.1.side_ref, f32[8,96,128]{2,1,0:T(8,128)S(1)} %all_to_all.20.sums_ref), custom_call_target="tpu_custom_call" | custom-call | flops 200000000 | bytes 500000 | tf_op jit(solution)/shard_map/pallas_call | solution.py:90
  132.6 1.2 fusion.2
  133.9 1.9 collective-permute-start.5
  136.2 1.9 collective-permute-start.6
  139.3 22.0 %collective-permute-done.6.refs_1_ = f32[64,64]{1,0:T(8,128)S(1)} collective-permute-done((f32[64,64]{1,0:T(8,128)S(1)}, f32[64,64]{1,0:T(8,128)S(1)}, u32[]{:S(2)}, u32[]{:S(2)}) %collective-permute-start.6) | collective-permute-done | bytes 16416 | tf_op jit(solution)/shard_map/ppermute | solution.py:42
  161.3 1.5 shard_map.34
  162.8 6.2 %all-to-all-start.3 = ((f32[16,32,128]{2,1,0:T(8,128)}), f32[16,32,128]{2,1,0:T(8,128)S(1)}, u32[]{:S(2)}, u32[]{:S(2)}) async-start(f32[16,32,128]{2,1,0:T(8,128)} %shard_map.34), calls=%async_computation.3 | async-start | bytes 524288 | tf_op jit(solution)/shard_map/all_to_all | solution.py:101
  169.4 8.3 %all-to-all-done.3.sums_ref = f32[16,32,128]{2,1,0:T(8,128)S(1)} async-done(((f32[16,32,128]{2,1,0:T(8,128)}), f32[16,32,128]{2,1,0:T(8,128)S(1)}, u32[]{:S(2)}, u32[]{:S(2)}) %all-to-all-start.3) | async-done | bytes 262176 | tf_op jit(solution)/shard_map/all_to_all | solution.py:101
  177.7 3.1 %shard_map.35 = (f32[128,128]{1,0:T(8,128)}, f32[128,128]{1,0:T(8,128)S(1)}) custom-call(s32[1]{0:T(128)} %bitcast.side_ref, f32[16,32,128]{2,1,0:T(8,128)S(1)} %all-to-all-done.3.sums_ref, f32[64,64]{1,0:T(8,128)S(1)} %fusion.15.refs_0_, f32[64,64]{1,0:T(8,128)S(1)} %collective-permute-done.6.refs_1_), custom_call_target="tpu_custom_call" | custom-call | flops 200000000 | bytes 500000 | tf_op jit(solution)/shard_map/pallas_call | solution.py:90
  182.1 1.9 collective-permute-start.7
  185.3 24.5 %collective-permute-done.7.arrived_ref = f32[64,4096]{1,0:T(8,128)S(1)} collective-permute-done((f32[64,4096]{1,0:T(8,128)S(1)}, f32[64,4096]{1,0:T(8,128)S(1)}, u32[]{:S(2)}, u32[]{:S(2)}) %collective-permute-start.7) | collective-permute-done | bytes 1048608 | tf_op jit(solution)/shard_map/ppermute | solution.py:42
  209.8 1.5 shard_map.36
  (27 shorter events, 10.7 us)
Async XLA Ops:
  0.0 1.6 copy-start.1
  1.6 15.8 %copy-start.2 = (s32[4,1]{0,1:T(1,128)S(1)}, s32[4,1]{0,1:T(1,128)}, u32[]{:S(2)}) copy-start(s32[4,1]{0,1:T(1,128)} %param.3) | copy-start | bytes 52
  3.5 26.7 %copy-start = (f32[128,4096]{1,0:T(8,128)}, f32[128,4096]{1,0:T(8,128)S(1)}, u32[]{:S(2)}) copy-start(f32[128,4096]{1,0:T(8,128)S(1)} %get-tuple-element.19) | copy-start | bytes 6291460
  3.5 9.7 %collective-permute-start = (f32[96,128]{1,0:T(8,128)S(1)}, f32[96,128]{1,0:T(8,128)S(1)}, u32[]{:S(2)}, u32[]{:S(2)}) collective-permute-start(f32[96,128]{1,0:T(8,128)S(1)} %get-tuple-element.17), channel_id=1, source_target_pairs={{0,1},{1,0},{2,3},{3,2},{4,5},{5,4},{6,7},{7,6},{8,9},{9,8},{10,11... | collective-permute-start | bytes 147464 | tf_op jit(solution)/shard_map/ppermute | solution.py:106
  14.0 13.1 %all-to-all-start = ((f32[8,96,128]{2,1,0:T(8,128)}), f32[8,96,128]{2,1,0:T(8,128)S(1)}, u32[]{:S(2)}, u32[]{:S(2)}) async-start(f32[8,96,128]{2,1,0:T(8,128)} %broadcast_in_dim.4), calls=%async_computation | async-start | bytes 786432 | tf_op jit(solution)/shard_map/all_to_all | solution.py:109
  31.4 31.6 %collective-permute-start.1 = (f32[64,4096]{1,0:T(8,128)S(1)}, f32[64,4096]{1,0:T(8,128)S(1)}, u32[]{:S(2)}, u32[]{:S(2)}) collective-permute-start(f32[64,4096]{1,0:T(8,128)S(1)} %fusion.24), channel_id=1, source_target_pairs={{0,16},{16,32},{32,48},{48,64},{64,80},{80,96},{96,112},{112,128},... | collective-permute-start | bytes 3145736 | tf_op jit(solution)/shard_map/ppermute | solution.py:42
  33.7 29.3 %collective-permute-start.2 = (f32[64,64]{1,0:T(8,128)S(1)}, f32[64,64]{1,0:T(8,128)S(1)}, u32[]{:S(2)}, u32[]{:S(2)}) collective-permute-start(f32[64,64]{1,0:T(8,128)S(1)} %fusion.20), channel_id=1, source_target_pairs={{0,16},{16,32},{32,48},{48,64},{64,80},{80,96},{96,112},{112,128},... | collective-permute-start | bytes 49160 | tf_op jit(solution)/shard_map/ppermute | solution.py:42
  64.6 14.2 %all-to-all-start.1 = ((f32[16,32,128]{2,1,0:T(8,128)}), f32[16,32,128]{2,1,0:T(8,128)S(1)}, u32[]{:S(2)}, u32[]{:S(2)}) async-start(f32[16,32,128]{2,1,0:T(8,128)} %shard_map.30), calls=%async_computation.1 | async-start | bytes 524288 | tf_op jit(solution)/shard_map/all_to_all | solution.py:101
  83.2 27.6 %collective-permute-start.3 = (f32[64,4096]{1,0:T(8,128)S(1)}, f32[64,4096]{1,0:T(8,128)S(1)}, u32[]{:S(2)}, u32[]{:S(2)}) collective-permute-start(f32[64,4096]{1,0:T(8,128)S(1)} %fusion.4), channel_id=1, source_target_pairs={{0,16},{16,32},{32,48},{48,64},{64,80},{80,96},{96,112},{112,128},... | collective-permute-start | bytes 3145736 | tf_op jit(solution)/shard_map/ppermute | solution.py:42
  112.8 4.7 %collective-permute-start.4 = (f32[96,128]{1,0:T(8,128)S(1)}, f32[96,128]{1,0:T(8,128)S(1)}, u32[]{:S(2)}, u32[]{:S(2)}) collective-permute-start(f32[96,128]{1,0:T(8,128)S(1)} %shard_map.32), channel_id=1, source_target_pairs={{0,1},{1,0},{2,3},{3,2},{4,5},{5,4},{6,7},{7,6},{8,9},{9,8},{10,11... | collective-permute-start | bytes 147464 | tf_op jit(solution)/shard_map/ppermute | solution.py:106
  133.9 27.4 %collective-permute-start.5 = (f32[64,4096]{1,0:T(8,128)S(1)}, f32[64,4096]{1,0:T(8,128)S(1)}, u32[]{:S(2)}, u32[]{:S(2)}) collective-permute-start(f32[64,4096]{1,0:T(8,128)S(1)} %fusion.2), channel_id=1, source_target_pairs={{0,16},{16,32},{32,48},{48,64},{64,80},{80,96},{96,112},{112,128},... | collective-permute-start | bytes 3145736 | tf_op jit(solution)/shard_map/ppermute | solution.py:42
  136.2 25.1 %collective-permute-start.6 = (f32[64,64]{1,0:T(8,128)S(1)}, f32[64,64]{1,0:T(8,128)S(1)}, u32[]{:S(2)}, u32[]{:S(2)}) collective-permute-start(f32[64,64]{1,0:T(8,128)S(1)} %fusion.10), channel_id=1, source_target_pairs={{0,16},{16,32},{32,48},{48,64},{64,80},{80,96},{96,112},{112,128},... | collective-permute-start | bytes 49160 | tf_op jit(solution)/shard_map/ppermute | solution.py:42
  162.8 14.9 %all-to-all-start.3 = ((f32[16,32,128]{2,1,0:T(8,128)}), f32[16,32,128]{2,1,0:T(8,128)S(1)}, u32[]{:S(2)}, u32[]{:S(2)}) async-start(f32[16,32,128]{2,1,0:T(8,128)} %shard_map.34), calls=%async_computation.3 | async-start | bytes 524288 | tf_op jit(solution)/shard_map/all_to_all | solution.py:101
  182.1 27.7 %collective-permute-start.7 = (f32[64,4096]{1,0:T(8,128)S(1)}, f32[64,4096]{1,0:T(8,128)S(1)}, u32[]{:S(2)}, u32[]{:S(2)}) collective-permute-start(f32[64,4096]{1,0:T(8,128)S(1)} %fusion), channel_id=1, source_target_pairs={{0,16},{16,32},{32,48},{48,64},{64,80},{80,96},{96,112},{112,128},... | collective-permute-start | bytes 3145736 | tf_op jit(solution)/shard_map/ppermute | solution.py:42

commit v5 on v4

--- a/solution.py
+++ b/solution.py
@@ -9,6 +9,7 @@
 
 ROUNDS = 4
 NS_STEPS = 6
+GROUPS = 2
 HIGHEST = lax.Precision.HIGHEST
 IN_VMEM = pl.BlockSpec(memory_space=pltpu.VMEM)
 
@@ -123,14 +124,17 @@
     return lax.dot_general(a, b, (((1,), (1,)), ((), ())), precision=HIGHEST, preferred_element_type=jnp.float32)
 
 
-def entry_kernel(x_ref, xt_ref, part_ref):
+def entry_kernel(x_ref, *refs):
+    part_ref, xt_refs = refs[-1], refs[:-1]
     pieces = 8
     height = x_ref.shape[0] // pieces
+    each = pieces // len(xt_refs)
     gram = None
     for piece in range(pieces):
         slab = x_ref[piece * height : (piece + 1) * height, :]
         turned_over = slab.T
-        xt_ref[:, piece * height : (piece + 1) * height] = turned_over
+        start = piece % each * height
+        xt_refs[piece // each][:, start : start + height] = turned_over
         product = jnp.dot(
             jnp.concatenate(terms(turned_over), axis=0),
             jnp.concatenate(terms(slab), axis=1),
@@ -144,23 +148,20 @@
     rows, order = matrix.shape
     return pl.pallas_call(
         entry_kernel,
-        out_shape=(
-            jax.ShapeDtypeStruct((order, rows), jnp.float32),
-            jax.ShapeDtypeStruct((3 * order // 4, order), jnp.float32),
-        ),
+        out_shape=[jax.ShapeDtypeStruct((order, rows // GROUPS), jnp.float32)] * GROUPS
+        + [jax.ShapeDtypeStruct((3 * order // 4, order), jnp.float32)],
         in_specs=[IN_VMEM],
-        out_specs=(IN_VMEM, IN_VMEM),
+        out_specs=[IN_VMEM] * (GROUPS + 1),
         compiler_params=pltpu.CompilerParams(vmem_limit_bytes=10 << 20),
         cost_estimate=pl.CostEstimate(flops=800_000_000, bytes_accessed=4_000_000, transcendentals=0),
     )(matrix)
 
 
-def gram_kernel(stay_ref, arrived_ref, part_ref):
+def products(stay_ref, arrived_ref, whole):
     rows = stay_ref.shape[1]
-    whole = len(part_ref.shape) == 2
-    pieces = 4
+    pieces = 2
     length = rows // pieces
-    gram = None
+    total = None
     for piece in range(pieces):
         where = slice(piece * length, (piece + 1) * length)
         left, right = stay_ref[:, where], arrived_ref[:, where]
@@ -169,81 +170,107 @@
         left = jnp.concatenate(terms(left), axis=0)
         right = left if whole else jnp.concatenate(terms(right), axis=0)
         product = lax.dot_general(left, right, (((1,), (1,)), ((), ())), preferred_element_type=jnp.float32)
-        gram = product if gram is None else gram + product
-    gram = added_up(gram, gram.shape[0] // 3, gram.shape[1] // 3)
+        total = product if total is None else total + product
+    total = added_up(total, total.shape[0] // 3, total.shape[1] // 3)
+    return packed_gram(total) if whole else folded(total)
+
+
+def first_gram_kernel(whole, stay_ref, arrived_ref, part_ref):
+    part_ref[...] = products(stay_ref, arrived_ref, whole)
+
+
+def last_gram_kernel(whole, before_ref, stay_ref, arrived_ref, part_ref):
+    part = before_ref[...] + products(stay_ref, arrived_ref, whole)
     if whole:
-        part_ref[...] = packed_gram(gram)
+        part_ref[...] = part
     else:
-        packed = folded(gram)
         for device in range(part_ref.shape[0]):
-            part_ref[device] = packed
-
-
-def gram_part(stay, arrived, copies=None):
-    width = stay.shape[0]
-    shape = (3 * width // 2, 2 * width) if copies is None else (copies, width // 2, 2 * width)
-    return pl.pallas_call(
-        gram_kernel,
-        out_shape=jax.ShapeDtypeStruct(shape, jnp.float32),
-        in_specs=[IN_VMEM, IN_VMEM],
+            part_ref[device] = part
+
+
+def gram_part(stays, arriveds, copies=None, beside=None):
+    width = stays[0].shape[0]
+    whole = copies is None
+    part = jax.ShapeDtypeStruct((3 * width // 2 if whole else width // 2, 2 * width), jnp.float32)
+    result = part if whole else jax.ShapeDtypeStruct((copies,) + part.shape, jnp.float32)
+    options = dict(
         out_specs=IN_VMEM,
         compiler_params=pltpu.CompilerParams(vmem_limit_bytes=8 << 20),
         cost_estimate=pl.CostEstimate(flops=400_000_000, bytes_accessed=3_000_000, transcendentals=0),
-    )(stay, arrived)
-
-
-def exit_kernel(stay_ref, arrived_ref, out_ref, held_ref, sems):
+    )
+    first = pl.pallas_call(
+        functools.partial(first_gram_kernel, whole), out_shape=part, in_specs=[IN_VMEM] * 2, **options
+    )(stays[0], arriveds[0])
+    if beside is not None:
+        first, beside = lax.optimization_barrier((first, beside))
+    result = pl.pallas_call(
+        functools.partial(last_gram_kernel, whole), out_shape=result, in_specs=[IN_VMEM] * 3, **options
+    )(first, stays[1], arriveds[1])
+    return result, beside
+
+
+def exit_kernel(group, *refs):
+    stay_ref, arrived_ref, out_ref, held_ref, sems = refs[-5:]
     pieces = sems.shape[0]
-    height = out_ref.shape[0] // pieces
+    height = held_ref.shape[0] // pieces
     copies = []
     for piece in range(pieces):
         where = slice(piece * height, (piece + 1) * height)
         held_ref[where, :] = jnp.concatenate([stay_ref[:, where], arrived_ref[:, where]], axis=0).T
-        rows = pl.ds(piece * height, height)
-        copy = pltpu.make_async_copy(held_ref.at[rows], out_ref.at[rows], sems.at[piece])
+        copy = pltpu.make_async_copy(
+            held_ref.at[pl.ds(piece * height, height)],
+            out_ref.at[pl.ds(group * pieces * height + piece * height, height)],
+            sems.at[piece],
+        )
         copy.start()
         copies.append(copy)
     for copy in copies:
         copy.wait()
 
 
-def assembled(stay, arrived):
-    width, rows = stay.shape
-    pieces = 8
-    return pl.pallas_call(
-        exit_kernel,
-        out_shape=jax.ShapeDtypeStruct((rows, 2 * width), jnp.float32),
-        in_specs=[IN_VMEM, IN_VMEM],
-        out_specs=pl.BlockSpec(memory_space=pltpu.HBM),
-        scratch_shapes=[pltpu.VMEM((rows, 2 * width), jnp.float32), pltpu.SemaphoreType.DMA((pieces,))],
-        compiler_params=pltpu.CompilerParams(vmem_limit_bytes=8 << 20),
-        cost_estimate=pl.CostEstimate(flops=0, bytes_accessed=4_000_000, transcendentals=0),
-    )(stay, arrived)
+def assembled(stays, arriveds):
+    width, rows = stays[0].shape
+    pieces = 4
+    whole = ()
+    for group in range(GROUPS):
+        whole = (
+            pl.pallas_call(
+                functools.partial(exit_kernel, group),
+                out_shape=jax.ShapeDtypeStruct((rows * GROUPS, 2 * width), jnp.float32),
+                in_specs=[pl.BlockSpec(memory_space=pltpu.HBM)] * len(whole) + [IN_VMEM, IN_VMEM],
+                out_specs=pl.BlockSpec(memory_space=pltpu.HBM),
+                scratch_shapes=[pltpu.VMEM((rows, 2 * width), jnp.float32), pltpu.SemaphoreType.DMA((pieces,))],
+                input_output_aliases={0: 0} if whole else {},
+                compiler_params=pltpu.CompilerParams(vmem_limit_bytes=8 << 20),
+                cost_estimate=pl.CostEstimate(flops=0, bytes_accessed=2_000_000, transcendentals=0),
+            )(*whole, stays[group], arriveds[group]),
+        )
+    return whole[0]
 
 
 def local(matrix, stay_side):
     rows, width = matrix.shape[0], matrix.shape[1] // 2
     total_rows = float(rows * lax.axis_size("row"))
     peers = lax.axis_size("row")
-    current, part = entry(matrix)
+    *currents, part = entry(matrix)
     gram, turn = turned(shares_of_chips(part), stay_side[0], total_rows)
     for round_index in range(ROUNDS):
         following = round_index + 1
         to_stay, to_move = turn[:width], turn[width:]
-        arrived = passed_along(mul(to_move, current), "pair", 1)
-        stay = mul(to_stay, current)
+        arriveds = [passed_along(mul(to_move, current), "pair", 1) for current in currents]
+        stays = [mul(to_stay, current) for current in currents]
         if following == ROUNDS:
-            return assembled(stay, arrived)
-        current = jnp.concatenate([stay, arrived], axis=0)
+            return assembled(stays, arriveds)
         if following % 2 == 0:
-            gram, turn = turned(shares_of_chips(gram_part(stay, arrived)), stay_side[following], total_rows)
+            part, _ = gram_part(stays, arriveds)
+            gram, turn = turned(shares_of_chips(part), stay_side[following], total_rows)
         else:
             gram_stay = mul_nt(mul(to_stay, gram), to_stay)
-            gram_arrived = passed_along(mul_nt(mul(to_move, gram), to_move), "pair", 1)
-            arrived, gram_arrived = lax.optimization_barrier((arrived, gram_arrived))
-            current = jnp.concatenate([stay, arrived], axis=0)
-            copies = gram_part(stay, arrived, peers)
+            gram_move = mul_nt(mul(to_move, gram), to_move)
+            copies, gram_move = gram_part(stays, arriveds, peers, gram_move)
+            gram_arrived = passed_along(gram_move, "pair", 1)
             gram, turn = turned(shares(copies), stay_side[following], total_rows, (gram_stay, gram_arrived))
+        currents = [jnp.concatenate(pair, axis=0) for pair in zip(stays, arriveds)]
 
 
 def solution(mesh):

time: 212 us -> 211 us (level)
  waiting for transfers between devices: 122 us -> 109 us
  starting transfers between devices: 40.1 us -> 48.2 us
    all_to_all x2, waiting for transfers between devices: 16.6 us -> 2.86 us  [shares(): return lax.all_to_all(copies, 'row', 0, 0)]
    ppermute x6 -> x10, starting transfers between devices: 12.3 us -> 20 us  [passed_along(): lax.ppermute(shard, axis, [(i, (i + by) % peers) for i in range(peers)])]
    pallas_call x5 -> x9, Pallas kernels: 8.35 us -> 10.1 us  [the longest x3 3.69 us: gram_part(): pl.pallas_call(functools.partial(last_gram_kernel, whole), out_shape=resu...]
    dot_general x12 -> x20, matrix products: 12 us -> 11.7 us  [mul(): return jnp.dot(a, b, precision=HIGHEST)]
    ppermute x6 -> x10, waiting for transfers between devices: 94.8 us -> 95.1 us  [passed_along(): lax.ppermute(shard, axis, [(i, (i + by) % peers) for i in range(peers)])]
  transfers between devices with their start and end apart: 11 -> 15, of which waited for: 9 -> 15; matrix products, arithmetic and copies ran while one was open for 4% -> 4% of each run, Pallas kernels for 0% -> 2%
where the time goes in v5:
time: 211 us; the launch traced here: 210 us
  waiting for transfers between devices  109 us (52%)
  starting transfers between devices  48.2 us (23%)
  Pallas kernels  23 us (11%)
  blocking collectives  14 us (7%)
  matrix products  12.4 us (6%)
  local copies, waits for them, and re-layouts  3.07 us (1%)
    ppermute x10, waiting for transfers between devices, passed_along(): lax.ppermute(shard, axis, [(i, (i + by) % peers) for i in range(peers)])  95.1 us
    ppermute x10, starting transfers between devices, passed_along(): lax.ppermute(shard, axis, [(i, (i + by) % peers) for i in range(peers)])  20 us
    all_to_all x1, blocking collectives, shares_of_chips(): return lax.all_to_all(copies, 'row', 0, 0, axis_index_groups=groups)  14 us
    ppermute x2, starting transfers between devices, shares_of_chips(): part = part + lax.ppermute(part, 'row', [(i, i ^ 1) for i in range(peers)])  13 us
    pallas_call x4, Pallas kernels, turned(): pl.pallas_call(functools.partial(turn_kernel, total_rows, bool(blocks)),...  13 us
    all_to_all x2, starting transfers between devices, shares(): return lax.all_to_all(copies, 'row', 0, 0)  11.7 us
    dot_general x20, matrix products, mul(): return jnp.dot(a, b, precision=HIGHEST)  11.7 us
    all_to_all x1, waiting for transfers between devices, shares_of_chips(): return lax.all_to_all(copies, 'row', 0, 0, axis_index_groups=groups)  8.94 us
  transfers between devices with their start and end apart: 15, of which 15 were waited for; matrix products, arithmetic and copies ran while one was open for 4% of the time, Pallas kernels for 2%

profile of v5, /device:TPU:1, one launch (start us, length us, event | category | flops | bytes accessed | tf_op | source)
XLA Modules:
  0.0 209.8 jit_solution(17564338810434711023)
XLA Ops:
  1.6 1.9 shard_map.28
  3.5 8.8 %collective-permute-start = (f32[96,128]{1,0:T(8,128)S(1)}, f32[96,128]{1,0:T(8,128)S(1)}, u32[]{:S(2)}, u32[]{:S(2)}) collective-permute-start(f32[96,128]{1,0:T(8,128)S(1)} %get-tuple-element.18), channel_id=1, source_target_pairs={{0,1},{1,0},{2,3},{3,2},{4,5},{5,4},{6,7},{7,6},{8,9},{9,8},{10,11... | collective-permute-start | bytes 147464 | tf_op jit(solution)/shard_map/ppermute | solution.py:107
  13.9 3.5 %all-to-all-start = ((f32[8,96,128]{2,1,0:T(8,128)}), f32[8,96,128]{2,1,0:T(8,128)S(1)}, u32[]{:S(2)}, u32[]{:S(2)}) async-start(f32[8,96,128]{2,1,0:T(8,128)} %broadcast_in_dim.4), calls=%async_computation | async-start | bytes 786432 | tf_op jit(solution)/shard_map/all_to_all | solution.py:110
  18.1 8.9 %all-to-all-done.sums_ref = f32[8,96,128]{2,1,0:T(8,128)S(1)} async-done(((f32[8,96,128]{2,1,0:T(8,128)}), f32[8,96,128]{2,1,0:T(8,128)S(1)}, u32[]{:S(2)}, u32[]{:S(2)}) %all-to-all-start) | async-done | bytes 393248 | tf_op jit(solution)/shard_map/all_to_all | solution.py:110
  27.0 3.2 %shard_map.29 = (f32[128,128]{1,0:T(8,128)S(1)}, f32[128,128]{1,0:T(8,128)S(1)}) custom-call(s32[1]{0:T(128)} %bitcast.3.side_ref, f32[8,96,128]{2,1,0:T(8,128)S(1)} %all-to-all-done.sums_ref), custom_call_target="tpu_custom_call" | custom-call | flops 200000000 | bytes 500000 | tf_op jit(solution)/shard_map/pallas_call | solution.py:91
  32.4 1.9 collective-permute-start.1
  34.5 2.5 %collective-permute-start.2 = (f32[64,2048]{1,0:T(8,128)S(1)}, f32[64,2048]{1,0:T(8,128)S(1)}, u32[]{:S(2)}, u32[]{:S(2)}) collective-permute-start(f32[64,2048]{1,0:T(8,128)S(1)} %fusion.32), channel_id=1, source_target_pairs={{0,16},{16,32},{32,48},{48,64},{64,80},{80,96},{96,112},{112,128},... | collective-permute-start | bytes 1572872 | tf_op jit(solution)/shard_map/ppermute | solution.py:43
  37.9 14.1 %collective-permute-done.1.arrived_ref = f32[64,2048]{1,0:T(8,128)S(1)} collective-permute-done((f32[64,2048]{1,0:T(8,128)S(1)}, f32[64,2048]{1,0:T(8,128)S(1)}, u32[]{:S(2)}, u32[]{:S(2)}) %collective-permute-start.1) | collective-permute-done | bytes 524320 | tf_op jit(solution)/shard_map/ppermute | solution.py:43
  52.6 10.7 %collective-permute-done.2.arrived_ref = f32[64,2048]{1,0:T(8,128)S(1)} collective-permute-done((f32[64,2048]{1,0:T(8,128)S(1)}, f32[64,2048]{1,0:T(8,128)S(1)}, u32[]{:S(2)}, u32[]{:S(2)}) %collective-permute-start.2) | collective-permute-done | bytes 524320 | tf_op jit(solution)/shard_map/ppermute | solution.py:43
  64.6 5.5 %all-to-all-start.1 = ((f32[16,32,128]{2,1,0:T(8,128)}), f32[16,32,128]{2,1,0:T(8,128)S(1)}, u32[]{:S(2)}, u32[]{:S(2)}) async-start(f32[16,32,128]{2,1,0:T(8,128)} %shard_map.31), calls=%async_computation.1 | async-start | bytes 524288 | tf_op jit(solution)/shard_map/all_to_all | solution.py:102
  70.3 1.9 collective-permute-start.3
  72.4 4.9 %collective-permute-done.3.refs_1_ = f32[64,64]{1,0:T(8,128)S(1)} collective-permute-done((f32[64,64]{1,0:T(8,128)S(1)}, f32[64,64]{1,0:T(8,128)S(1)}, u32[]{:S(2)}, u32[]{:S(2)}) %collective-permute-start.3) | collective-permute-done | bytes 16416 | tf_op jit(solution)/shard_map/ppermute | solution.py:43
  78.8 3.3 %shard_map.32 = (f32[128,128]{1,0:T(8,128)}, f32[128,128]{1,0:T(8,128)S(1)}) custom-call(s32[1]{0:T(128)} %bitcast.2.side_ref, f32[16,32,128]{2,1,0:T(8,128)S(1)} %all-to-all-done.1.sums_ref, f32[64,64]{1,0:T(8,128)S(1)} %fusion.40.refs_0_, f32[64,64]{1,0:T(8,128)S(1)} %collective-permute-done.3.refs_1_), custom_call_target="tpu_custom_call" | custom-call | flops 200000000 | bytes 500000 | tf_op jit(solution)/shard_map/pallas_call | solution.py:91
  82.8 1.9 collective-permute-start.4
  85.4 2.1 %collective-permute-start.5 = (f32[64,2048]{1,0:T(8,128)S(1)}, f32[64,2048]{1,0:T(8,128)S(1)}, u32[]{:S(2)}, u32[]{:S(2)}) collective-permute-start(f32[64,2048]{1,0:T(8,128)S(1)} %fusion.8), channel_id=1, source_target_pairs={{0,16},{16,32},{32,48},{48,64},{64,80},{80,96},{96,112},{112,128},... | collective-permute-start | bytes 1572872 | tf_op jit(solution)/shard_map/ppermute | solution.py:43
  88.9 10.0 %collective-permute-done.4.arrived_ref = f32[64,2048]{1,0:T(8,128)S(1)} collective-permute-done((f32[64,2048]{1,0:T(8,128)S(1)}, f32[64,2048]{1,0:T(8,128)S(1)}, u32[]{:S(2)}, u32[]{:S(2)}) %collective-permute-start.4) | collective-permute-done | bytes 524320 | tf_op jit(solution)/shard_map/ppermute | solution.py:43
  99.9 10.2 %collective-permute-done.5.arrived_ref = f32[64,2048]{1,0:T(8,128)S(1)} collective-permute-done((f32[64,2048]{1,0:T(8,128)S(1)}, f32[64,2048]{1,0:T(8,128)S(1)}, u32[]{:S(2)}, u32[]{:S(2)}) %collective-permute-start.5) | collective-permute-done | bytes 524320 | tf_op jit(solution)/shard_map/ppermute | solution.py:43
  111.2 4.2 %collective-permute-start.6 = (f32[96,128]{1,0:T(8,128)S(1)}, f32[96,128]{1,0:T(8,128)S(1)}, u32[]{:S(2)}, u32[]{:S(2)}) collective-permute-start(f32[96,128]{1,0:T(8,128)S(1)} %shard_map.34), channel_id=1, source_target_pairs={{0,1},{1,0},{2,3},{3,2},{4,5},{5,4},{6,7},{7,6},{8,9},{9,8},{10,11... | collective-permute-start | bytes 147464 | tf_op jit(solution)/shard_map/ppermute | solution.py:107
  116.2 14.0 %all_to_all.20.sums_ref = f32[8,96,128]{2,1,0:T(8,128)S(1)} all-to-all(f32[8,96,128]{2,1,0:T(8,128)S(1)} %broadcast_in_dim.5), channel_id=1, replica_groups={{0,2,4,6,8,10,12,14},{1,3,5,7,9,11,13,15},{16,18,20,22,24,26,28,30},{17..., dimensions={0} | all-to-all | bytes 786432 | tf_op jit(solution)/shard_map/all_to_all | solution.py:110
  130.3 3.1 %shard_map.35 = (f32[128,128]{1,0:T(8,128)S(1)}, f32[128,128]{1,0:T(8,128)S(1)}) custom-call(s32[1]{0:T(128)} %bitcast.1.side_ref, f32[8,96,128]{2,1,0:T(8,128)S(1)} %all_to_all.20.sums_ref), custom_call_target="tpu_custom_call" | custom-call | flops 200000000 | bytes 500000 | tf_op jit(solution)/shard_map/pallas_call | solution.py:91
  134.3 1.9 collective-permute-start.7
  136.9 1.9 collective-permute-start.8
  140.4 9.4 %collective-permute-done.7.arrived_ref = f32[64,2048]{1,0:T(8,128)S(1)} collective-permute-done((f32[64,2048]{1,0:T(8,128)S(1)}, f32[64,2048]{1,0:T(8,128)S(1)}, u32[]{:S(2)}, u32[]{:S(2)}) %collective-permute-start.7) | collective-permute-done | bytes 524320 | tf_op jit(solution)/shard_map/ppermute | solution.py:43
  150.4 10.7 %collective-permute-done.8.arrived_ref = f32[64,2048]{1,0:T(8,128)S(1)} collective-permute-done((f32[64,2048]{1,0:T(8,128)S(1)}, f32[64,2048]{1,0:T(8,128)S(1)}, u32[]{:S(2)}, u32[]{:S(2)}) %collective-permute-start.8) | collective-permute-done | bytes 524320 | tf_op jit(solution)/shard_map/ppermute | solution.py:43
  162.3 6.2 %all-to-all-start.3 = ((f32[16,32,128]{2,1,0:T(8,128)}), f32[16,32,128]{2,1,0:T(8,128)S(1)}, u32[]{:S(2)}, u32[]{:S(2)}) async-start(f32[16,32,128]{2,1,0:T(8,128)} %shard_map.37), calls=%async_computation.3 | async-start | bytes 524288 | tf_op jit(solution)/shard_map/all_to_all | solution.py:102
  168.8 1.9 collective-permute-start.9
  170.9 4.9 %collective-permute-done.9.refs_1_ = f32[64,64]{1,0:T(8,128)S(1)} collective-permute-done((f32[64,64]{1,0:T(8,128)S(1)}, f32[64,64]{1,0:T(8,128)S(1)}, u32[]{:S(2)}, u32[]{:S(2)}) %collective-permute-start.9) | collective-permute-done | bytes 16416 | tf_op jit(solution)/shard_map/ppermute | solution.py:43
  177.2 3.3 %shard_map.38 = (f32[128,128]{1,0:T(8,128)}, f32[128,128]{1,0:T(8,128)S(1)}) custom-call(s32[1]{0:T(128)} %bitcast.side_ref, f32[16,32,128]{2,1,0:T(8,128)S(1)} %all-to-all-done.3.sums_ref, f32[64,64]{1,0:T(8,128)S(1)} %fusion.26.refs_0_, f32[64,64]{1,0:T(8,128)S(1)} %collective-permute-done.9.refs_1_), custom_call_target="tpu_custom_call" | custom-call | flops 200000000 | bytes 500000 | tf_op jit(solution)/shard_map/pallas_call | solution.py:91
  181.2 1.9 collective-permute-start.10
  183.8 1.9 collective-permute-start.11
  187.2 10.1 %collective-permute-done.10.refs_1_ = f32[64,2048]{1,0:T(8,128)S(1)} collective-permute-done((f32[64,2048]{1,0:T(8,128)S(1)}, f32[64,2048]{1,0:T(8,128)S(1)}, u32[]{:S(2)}, u32[]{:S(2)}) %collective-permute-start.10) | collective-permute-done | bytes 524320 | tf_op jit(solution)/shard_map/ppermute | solution.py:43
  198.4 10.1 %collective-permute-done.11.refs_2_ = f32[64,2048]{1,0:T(8,128)S(1)} collective-permute-done((f32[64,2048]{1,0:T(8,128)S(1)}, f32[64,2048]{1,0:T(8,128)S(1)}, u32[]{:S(2)}, u32[]{:S(2)}) %collective-permute-start.11) | collective-permute-done | bytes 524320 | tf_op jit(solution)/shard_map/ppermute | solution.py:43
  (45 shorter events, 28.2 us)
Async XLA Ops:
  0.0 1.6 copy-start
  1.6 15.8 %copy-start.1 = (s32[4,1]{0,1:T(1,128)S(1)}, s32[4,1]{0,1:T(1,128)}, u32[]{:S(2)}) copy-start(s32[4,1]{0,1:T(1,128)} %param.3) | copy-start | bytes 52
  3.5 9.7 %collective-permute-start = (f32[96,128]{1,0:T(8,128)S(1)}, f32[96,128]{1,0:T(8,128)S(1)}, u32[]{:S(2)}, u32[]{:S(2)}) collective-permute-start(f32[96,128]{1,0:T(8,128)S(1)} %get-tuple-element.18), channel_id=1, source_target_pairs={{0,1},{1,0},{2,3},{3,2},{4,5},{5,4},{6,7},{7,6},{8,9},{9,8},{10,11... | collective-permute-start | bytes 147464 | tf_op jit(solution)/shard_map/ppermute | solution.py:107
  13.9 13.1 %all-to-all-start = ((f32[8,96,128]{2,1,0:T(8,128)}), f32[8,96,128]{2,1,0:T(8,128)S(1)}, u32[]{:S(2)}, u32[]{:S(2)}) async-start(f32[8,96,128]{2,1,0:T(8,128)} %broadcast_in_dim.4), calls=%async_computation | async-start | bytes 786432 | tf_op jit(solution)/shard_map/all_to_all | solution.py:110
  32.4 19.7 %collective-permute-start.1 = (f32[64,2048]{1,0:T(8,128)S(1)}, f32[64,2048]{1,0:T(8,128)S(1)}, u32[]{:S(2)}, u32[]{:S(2)}) collective-permute-start(f32[64,2048]{1,0:T(8,128)S(1)} %fusion.38), channel_id=1, source_target_pairs={{0,16},{16,32},{32,48},{48,64},{64,80},{80,96},{96,112},{112,128},... | collective-permute-start | bytes 1572872 | tf_op jit(solution)/shard_map/ppermute | solution.py:43
  34.5 28.8 %collective-permute-start.2 = (f32[64,2048]{1,0:T(8,128)S(1)}, f32[64,2048]{1,0:T(8,128)S(1)}, u32[]{:S(2)}, u32[]{:S(2)}) collective-permute-start(f32[64,2048]{1,0:T(8,128)S(1)} %fusion.32), channel_id=1, source_target_pairs={{0,16},{16,32},{32,48},{48,64},{64,80},{80,96},{96,112},{112,128},... | collective-permute-start | bytes 1572872 | tf_op jit(solution)/shard_map/ppermute | solution.py:43
  64.6 14.2 %all-to-all-start.1 = ((f32[16,32,128]{2,1,0:T(8,128)}), f32[16,32,128]{2,1,0:T(8,128)S(1)}, u32[]{:S(2)}, u32[]{:S(2)}) async-start(f32[16,32,128]{2,1,0:T(8,128)} %shard_map.31), calls=%async_computation.1 | async-start | bytes 524288 | tf_op jit(solution)/shard_map/all_to_all | solution.py:102
  70.3 7.1 %collective-permute-start.3 = (f32[64,64]{1,0:T(8,128)S(1)}, f32[64,64]{1,0:T(8,128)S(1)}, u32[]{:S(2)}, u32[]{:S(2)}) collective-permute-start(f32[64,64]{1,0:T(8,128)S(1)} %fusion.34), channel_id=1, source_target_pairs={{0,16},{16,32},{32,48},{48,64},{64,80},{80,96},{96,112},{112,128},... | collective-permute-start | bytes 49160 | tf_op jit(solution)/shard_map/ppermute | solution.py:43
  82.8 16.1 %collective-permute-start.4 = (f32[64,2048]{1,0:T(8,128)S(1)}, f32[64,2048]{1,0:T(8,128)S(1)}, u32[]{:S(2)}, u32[]{:S(2)}) collective-permute-start(f32[64,2048]{1,0:T(8,128)S(1)} %fusion.10), channel_id=1, source_target_pairs={{0,16},{16,32},{32,48},{48,64},{64,80},{80,96},{96,112},{112,128},... | collective-permute-start | bytes 1572872 | tf_op jit(solution)/shard_map/ppermute | solution.py:43
  85.4 24.7 %collective-permute-start.5 = (f32[64,2048]{1,0:T(8,128)S(1)}, f32[64,2048]{1,0:T(8,128)S(1)}, u32[]{:S(2)}, u32[]{:S(2)}) collective-permute-start(f32[64,2048]{1,0:T(8,128)S(1)} %fusion.8), channel_id=1, source_target_pairs={{0,16},{16,32},{32,48},{48,64},{64,80},{80,96},{96,112},{112,128},... | collective-permute-start | bytes 1572872 | tf_op jit(solution)/shard_map/ppermute | solution.py:43
  111.2 5.0 %collective-permute-start.6 = (f32[96,128]{1,0:T(8,128)S(1)}, f32[96,128]{1,0:T(8,128)S(1)}, u32[]{:S(2)}, u32[]{:S(2)}) collective-permute-start(f32[96,128]{1,0:T(8,128)S(1)} %shard_map.34), channel_id=1, source_target_pairs={{0,1},{1,0},{2,3},{3,2},{4,5},{5,4},{6,7},{7,6},{8,9},{9,8},{10,11... | collective-permute-start | bytes 147464 | tf_op jit(solution)/shard_map/ppermute | solution.py:107
  134.3 15.5 %collective-permute-start.7 = (f32[64,2048]{1,0:T(8,128)S(1)}, f32[64,2048]{1,0:T(8,128)S(1)}, u32[]{:S(2)}, u32[]{:S(2)}) collective-permute-start(f32[64,2048]{1,0:T(8,128)S(1)} %fusion.6), channel_id=1, source_target_pairs={{0,16},{16,32},{32,48},{48,64},{64,80},{80,96},{96,112},{112,128},... | collective-permute-start | bytes 1572872 | tf_op jit(solution)/shard_map/ppermute | solution.py:43
  136.9 24.1 %collective-permute-start.8 = (f32[64,2048]{1,0:T(8,128)S(1)}, f32[64,2048]{1,0:T(8,128)S(1)}, u32[]{:S(2)}, u32[]{:S(2)}) collective-permute-start(f32[64,2048]{1,0:T(8,128)S(1)} %fusion.4), channel_id=1, source_target_pairs={{0,16},{16,32},{32,48},{48,64},{64,80},{80,96},{96,112},{112,128},... | collective-permute-start | bytes 1572872 | tf_op jit(solution)/shard_map/ppermute | solution.py:43
  162.3 14.9 %all-to-all-start.3 = ((f32[16,32,128]{2,1,0:T(8,128)}), f32[16,32,128]{2,1,0:T(8,128)S(1)}, u32[]{:S(2)}, u32[]{:S(2)}) async-start(f32[16,32,128]{2,1,0:T(8,128)} %shard_map.37), calls=%async_computation.3 | async-start | bytes 524288 | tf_op jit(solution)/shard_map/all_to_all | solution.py:102
  168.8 7.1 %collective-permute-start.9 = (f32[64,64]{1,0:T(8,128)S(1)}, f32[64,64]{1,0:T(8,128)S(1)}, u32[]{:S(2)}, u32[]{:S(2)}) collective-permute-start(f32[64,64]{1,0:T(8,128)S(1)} %fusion.21), channel_id=1, source_target_pairs={{0,16},{16,32},{32,48},{48,64},{64,80},{80,96},{96,112},{112,128},... | collective-permute-start | bytes 49160 | tf_op jit(solution)/shard_map/ppermute | solution.py:43
  181.2 16.1 %collective-permute-start.10 = (f32[64,2048]{1,0:T(8,128)S(1)}, f32[64,2048]{1,0:T(8,128)S(1)}, u32[]{:S(2)}, u32[]{:S(2)}) collective-permute-start(f32[64,2048]{1,0:T(8,128)S(1)} %fusion.2), channel_id=1, source_target_pairs={{0,16},{16,32},{32,48},{48,64},{64,80},{80,96},{96,112},{112,128},... | collective-permute-start | bytes 1572872 | tf_op jit(solution)/shard_map/ppermute | solution.py:43
  183.8 24.7 %collective-permute-start.11 = (f32[64,2048]{1,0:T(8,128)S(1)}, f32[64,2048]{1,0:T(8,128)S(1)}, u32[]{:S(2)}, u32[]{:S(2)}) collective-permute-start(f32[64,2048]{1,0:T(8,128)S(1)} %fusion), channel_id=1, source_target_pairs={{0,16},{16,32},{32,48},{48,64},{64,80},{80,96},{96,112},{112,128},... | collective-permute-start | bytes 1572872 | tf_op jit(solution)/shard_map/ppermute | solution.py:43

commit v6 on v5

--- a/solution.py
+++ b/solution.py
@@ -128,13 +128,15 @@
     part_ref, xt_refs = refs[-1], refs[:-1]
     pieces = 8
     height = x_ref.shape[0] // pieces
-    each = pieces // len(xt_refs)
+    each = pieces // GROUPS
+    width = x_ref.shape[1] // 2
     gram = None
     for piece in range(pieces):
         slab = x_ref[piece * height : (piece + 1) * height, :]
         turned_over = slab.T
         start = piece % each * height
-        xt_refs[piece // each][:, start : start + height] = turned_over
+        xt_refs[piece // each][:, start : start + height] = turned_over[:width]
+        xt_refs[GROUPS + piece // each][:, start : start + height] = turned_over[width:]
         product = jnp.dot(
             jnp.concatenate(terms(turned_over), axis=0),
             jnp.concatenate(terms(slab), axis=1),
@@ -148,10 +150,10 @@
     rows, order = matrix.shape
     return pl.pallas_call(
         entry_kernel,
-        out_shape=[jax.ShapeDtypeStruct((order, rows // GROUPS), jnp.float32)] * GROUPS
+        out_shape=[jax.ShapeDtypeStruct((order // 2, rows // GROUPS), jnp.float32)] * (2 * GROUPS)
         + [jax.ShapeDtypeStruct((3 * order // 4, order), jnp.float32)],
         in_specs=[IN_VMEM],
-        out_specs=[IN_VMEM] * (GROUPS + 1),
+        out_specs=[IN_VMEM] * (2 * GROUPS + 1),
         compiler_params=pltpu.CompilerParams(vmem_limit_bytes=10 << 20),
         cost_estimate=pl.CostEstimate(flops=800_000_000, bytes_accessed=4_000_000, transcendentals=0),
     )(matrix)
@@ -252,7 +254,8 @@
     rows, width = matrix.shape[0], matrix.shape[1] // 2
     total_rows = float(rows * lax.axis_size("row"))
     peers = lax.axis_size("row")
-    *currents, part = entry(matrix)
+    *blocks, part = entry(matrix)
+    currents = [jnp.concatenate(pair, axis=0) for pair in zip(blocks[:GROUPS], blocks[GROUPS:])]
     gram, turn = turned(shares_of_chips(part), stay_side[0], total_rows)
     for round_index in range(ROUNDS):
         following = round_index + 1

time: 211 us -> 210 us (level)
  transfers between devices with their start and end apart: 15 -> 15, of which waited for: 15 -> 15; matrix products, arithmetic and copies ran while one was open for 4% -> 5% of each run, Pallas kernels for 2% -> 2%
where the time goes in v6:
time: 210 us; the launch traced here: 209 us
  waiting for transfers between devices  107 us (51%)
  starting transfers between devices  48.1 us (23%)
  Pallas kernels  22.9 us (11%)
  blocking collectives  14 us (7%)
  matrix products  13 us (6%)
  local copies, waits for them, and re-layouts  3.22 us (2%)
    ppermute x10, waiting for transfers between devices, passed_along(): lax.ppermute(shard, axis, [(i, (i + by) % peers) for i in range(peers)])  93.8 us
    ppermute x10, starting transfers between devices, passed_along(): lax.ppermute(shard, axis, [(i, (i + by) % peers) for i in range(peers)])  20 us
    all_to_all x1, blocking collectives, shares_of_chips(): return lax.all_to_all(copies, 'row', 0, 0, axis_index_groups=groups)  14 us
    ppermute x2, starting transfers between devices, shares_of_chips(): part = part + lax.ppermute(part, 'row', [(i, i ^ 1) for i in range(peers)])  13 us
    pallas_call x4, Pallas kernels, turned(): pl.pallas_call(functools.partial(turn_kernel, total_rows, bool(blocks)),...  12.8 us
    all_to_all x2, starting transfers between devices, shares(): return lax.all_to_all(copies, 'row', 0, 0)  11.7 us
    dot_general x20, matrix products, mul(): return jnp.dot(a, b, precision=HIGHEST)  11.7 us
    all_to_all x1, waiting for transfers between devices, shares_of_chips(): return lax.all_to_all(copies, 'row', 0, 0, axis_index_groups=groups)  8.9 us
  transfers between devices with their start and end apart: 15, of which 15 were waited for; matrix products, arithmetic and copies ran while one was open for 5% of the time, Pallas kernels for 2%

profile of v6, /device:TPU:1, one launch (start us, length us, event | category | flops | bytes accessed | tf_op | source)
XLA Modules:
  0.0 209.0 jit_solution(1436947649624181423)
XLA Ops:
  1.6 1.9 shard_map.28
  3.5 8.8 %collective-permute-start = (f32[96,128]{1,0:T(8,128)S(1)}, f32[96,128]{1,0:T(8,128)S(1)}, u32[]{:S(2)}, u32[]{:S(2)}) collective-permute-start(f32[96,128]{1,0:T(8,128)S(1)} %get-tuple-element.20), channel_id=1, source_target_pairs={{0,1},{1,0},{2,3},{3,2},{4,5},{5,4},{6,7},{7,6},{8,9},{9,8},{10,11... | collective-permute-start | bytes 147464 | tf_op jit(solution)/shard_map/ppermute | solution.py:107
  13.9 3.5 %all-to-all-start = ((f32[8,96,128]{2,1,0:T(8,128)}), f32[8,96,128]{2,1,0:T(8,128)S(1)}, u32[]{:S(2)}, u32[]{:S(2)}) async-start(f32[8,96,128]{2,1,0:T(8,128)} %broadcast_in_dim.4), calls=%async_computation | async-start | bytes 786432 | tf_op jit(solution)/shard_map/all_to_all | solution.py:110
  18.1 8.9 %all-to-all-done.sums_ref = f32[8,96,128]{2,1,0:T(8,128)S(1)} async-done(((f32[8,96,128]{2,1,0:T(8,128)}), f32[8,96,128]{2,1,0:T(8,128)S(1)}, u32[]{:S(2)}, u32[]{:S(2)}) %all-to-all-start) | async-done | bytes 393248 | tf_op jit(solution)/shard_map/all_to_all | solution.py:110
  27.0 3.1 %shard_map.29 = (f32[128,128]{1,0:T(8,128)S(1)}, f32[128,128]{1,0:T(8,128)S(1)}) custom-call(s32[1]{0:T(128)} %bitcast.3.side_ref, f32[8,96,128]{2,1,0:T(8,128)S(1)} %all-to-all-done.sums_ref), custom_call_target="tpu_custom_call" | custom-call | flops 200000000 | bytes 500000 | tf_op jit(solution)/shard_map/pallas_call | solution.py:91
  31.6 1.9 collective-permute-start.1
  34.4 2.5 %collective-permute-start.2 = (f32[64,2048]{1,0:T(8,128)S(1)}, f32[64,2048]{1,0:T(8,128)S(1)}, u32[]{:S(2)}, u32[]{:S(2)}) collective-permute-start(f32[64,2048]{1,0:T(8,128)S(1)} %fusion.32), channel_id=1, source_target_pairs={{0,16},{16,32},{32,48},{48,64},{64,80},{80,96},{96,112},{112,128},... | collective-permute-start | bytes 1572872 | tf_op jit(solution)/shard_map/ppermute | solution.py:43
  38.4 12.9 %collective-permute-done.1.arrived_ref = f32[64,2048]{1,0:T(8,128)S(1)} collective-permute-done((f32[64,2048]{1,0:T(8,128)S(1)}, f32[64,2048]{1,0:T(8,128)S(1)}, u32[]{:S(2)}, u32[]{:S(2)}) %collective-permute-start.1) | collective-permute-done | bytes 524320 | tf_op jit(solution)/shard_map/ppermute | solution.py:43
  51.9 10.7 %collective-permute-done.2.arrived_ref = f32[64,2048]{1,0:T(8,128)S(1)} collective-permute-done((f32[64,2048]{1,0:T(8,128)S(1)}, f32[64,2048]{1,0:T(8,128)S(1)}, u32[]{:S(2)}, u32[]{:S(2)}) %collective-permute-start.2) | collective-permute-done | bytes 524320 | tf_op jit(solution)/shard_map/ppermute | solution.py:43
  63.8 5.5 %all-to-all-start.1 = ((f32[16,32,128]{2,1,0:T(8,128)}), f32[16,32,128]{2,1,0:T(8,128)S(1)}, u32[]{:S(2)}, u32[]{:S(2)}) async-start(f32[16,32,128]{2,1,0:T(8,128)} %shard_map.31), calls=%async_computation.1 | async-start | bytes 524288 | tf_op jit(solution)/shard_map/all_to_all | solution.py:102
  69.5 1.9 collective-permute-start.3
  71.6 4.9 %collective-permute-done.3.refs_1_ = f32[64,64]{1,0:T(8,128)S(1)} collective-permute-done((f32[64,64]{1,0:T(8,128)S(1)}, f32[64,64]{1,0:T(8,128)S(1)}, u32[]{:S(2)}, u32[]{:S(2)}) %collective-permute-start.3) | collective-permute-done | bytes 16416 | tf_op jit(solution)/shard_map/ppermute | solution.py:43
  78.0 3.2 %shard_map.32 = (f32[128,128]{1,0:T(8,128)}, f32[128,128]{1,0:T(8,128)S(1)}) custom-call(s32[1]{0:T(128)} %bitcast.2.side_ref, f32[16,32,128]{2,1,0:T(8,128)S(1)} %all-to-all-done.1.sums_ref, f32[64,64]{1,0:T(8,128)S(1)} %fusion.40.refs_0_, f32[64,64]{1,0:T(8,128)S(1)} %collective-permute-done.3.refs_1_), custom_call_target="tpu_custom_call" | custom-call | flops 200000000 | bytes 500000 | tf_op jit(solution)/shard_map/pallas_call | solution.py:91
  81.9 1.9 collective-permute-start.4
  84.5 2.1 %collective-permute-start.5 = (f32[64,2048]{1,0:T(8,128)S(1)}, f32[64,2048]{1,0:T(8,128)S(1)}, u32[]{:S(2)}, u32[]{:S(2)}) collective-permute-start(f32[64,2048]{1,0:T(8,128)S(1)} %fusion.8), channel_id=1, source_target_pairs={{0,16},{16,32},{32,48},{48,64},{64,80},{80,96},{96,112},{112,128},... | collective-permute-start | bytes 1572872 | tf_op jit(solution)/shard_map/ppermute | solution.py:43
  88.0 10.0 %collective-permute-done.4.arrived_ref = f32[64,2048]{1,0:T(8,128)S(1)} collective-permute-done((f32[64,2048]{1,0:T(8,128)S(1)}, f32[64,2048]{1,0:T(8,128)S(1)}, u32[]{:S(2)}, u32[]{:S(2)}) %collective-permute-start.4) | collective-permute-done | bytes 524320 | tf_op jit(solution)/shard_map/ppermute | solution.py:43
  99.1 10.2 %collective-permute-done.5.arrived_ref = f32[64,2048]{1,0:T(8,128)S(1)} collective-permute-done((f32[64,2048]{1,0:T(8,128)S(1)}, f32[64,2048]{1,0:T(8,128)S(1)}, u32[]{:S(2)}, u32[]{:S(2)}) %collective-permute-start.5) | collective-permute-done | bytes 524320 | tf_op jit(solution)/shard_map/ppermute | solution.py:43
  110.3 4.2 %collective-permute-start.6 = (f32[96,128]{1,0:T(8,128)S(1)}, f32[96,128]{1,0:T(8,128)S(1)}, u32[]{:S(2)}, u32[]{:S(2)}) collective-permute-start(f32[96,128]{1,0:T(8,128)S(1)} %shard_map.34), channel_id=1, source_target_pairs={{0,1},{1,0},{2,3},{3,2},{4,5},{5,4},{6,7},{7,6},{8,9},{9,8},{10,11... | collective-permute-start | bytes 147464 | tf_op jit(solution)/shard_map/ppermute | solution.py:107
  115.4 14.0 %all_to_all.20.sums_ref = f32[8,96,128]{2,1,0:T(8,128)S(1)} all-to-all(f32[8,96,128]{2,1,0:T(8,128)S(1)} %broadcast_in_dim.5), channel_id=1, replica_groups={{0,2,4,6,8,10,12,14},{1,3,5,7,9,11,13,15},{16,18,20,22,24,26,28,30},{17..., dimensions={0} | all-to-all | bytes 786432 | tf_op jit(solution)/shard_map/all_to_all | solution.py:110
  129.4 3.2 %shard_map.35 = (f32[128,128]{1,0:T(8,128)S(1)}, f32[128,128]{1,0:T(8,128)S(1)}) custom-call(s32[1]{0:T(128)} %bitcast.1.side_ref, f32[8,96,128]{2,1,0:T(8,128)S(1)} %all_to_all.20.sums_ref), custom_call_target="tpu_custom_call" | custom-call | flops 200000000 | bytes 500000 | tf_op jit(solution)/shard_map/pallas_call | solution.py:91
  133.5 1.9 collective-permute-start.7
  136.1 1.9 collective-permute-start.8
  139.6 9.4 %collective-permute-done.7.arrived_ref = f32[64,2048]{1,0:T(8,128)S(1)} collective-permute-done((f32[64,2048]{1,0:T(8,128)S(1)}, f32[64,2048]{1,0:T(8,128)S(1)}, u32[]{:S(2)}, u32[]{:S(2)}) %collective-permute-start.7) | collective-permute-done | bytes 524320 | tf_op jit(solution)/shard_map/ppermute | solution.py:43
  149.6 10.6 %collective-permute-done.8.arrived_ref = f32[64,2048]{1,0:T(8,128)S(1)} collective-permute-done((f32[64,2048]{1,0:T(8,128)S(1)}, f32[64,2048]{1,0:T(8,128)S(1)}, u32[]{:S(2)}, u32[]{:S(2)}) %collective-permute-start.8) | collective-permute-done | bytes 524320 | tf_op jit(solution)/shard_map/ppermute | solution.py:43
  161.5 6.2 %all-to-all-start.3 = ((f32[16,32,128]{2,1,0:T(8,128)}), f32[16,32,128]{2,1,0:T(8,128)S(1)}, u32[]{:S(2)}, u32[]{:S(2)}) async-start(f32[16,32,128]{2,1,0:T(8,128)} %shard_map.37), calls=%async_computation.3 | async-start | bytes 524288 | tf_op jit(solution)/shard_map/all_to_all | solution.py:102
  168.0 1.9 collective-permute-start.9
  170.1 4.9 %collective-permute-done.9.refs_1_ = f32[64,64]{1,0:T(8,128)S(1)} collective-permute-done((f32[64,64]{1,0:T(8,128)S(1)}, f32[64,64]{1,0:T(8,128)S(1)}, u32[]{:S(2)}, u32[]{:S(2)}) %collective-permute-start.9) | collective-permute-done | bytes 16416 | tf_op jit(solution)/shard_map/ppermute | solution.py:43
  176.4 3.3 %shard_map.38 = (f32[128,128]{1,0:T(8,128)}, f32[128,128]{1,0:T(8,128)S(1)}) custom-call(s32[1]{0:T(128)} %bitcast.side_ref, f32[16,32,128]{2,1,0:T(8,128)S(1)} %all-to-all-done.3.sums_ref, f32[64,64]{1,0:T(8,128)S(1)} %fusion.26.refs_0_, f32[64,64]{1,0:T(8,128)S(1)} %collective-permute-done.9.refs_1_), custom_call_target="tpu_custom_call" | custom-call | flops 200000000 | bytes 500000 | tf_op jit(solution)/shard_map/pallas_call | solution.py:91
  180.4 1.9 collective-permute-start.10
  183.0 1.9 collective-permute-start.11
  186.4 10.1 %collective-permute-done.10.refs_1_ = f32[64,2048]{1,0:T(8,128)S(1)} collective-permute-done((f32[64,2048]{1,0:T(8,128)S(1)}, f32[64,2048]{1,0:T(8,128)S(1)}, u32[]{:S(2)}, u32[]{:S(2)}) %collective-permute-start.10) | collective-permute-done | bytes 524320 | tf_op jit(solution)/shard_map/ppermute | solution.py:43
  197.6 10.1 %collective-permute-done.11.refs_2_ = f32[64,2048]{1,0:T(8,128)S(1)} collective-permute-done((f32[64,2048]{1,0:T(8,128)S(1)}, f32[64,2048]{1,0:T(8,128)S(1)}, u32[]{:S(2)}, u32[]{:S(2)}) %collective-permute-start.11) | collective-permute-done | bytes 524320 | tf_op jit(solution)/shard_map/ppermute | solution.py:43
  (51 shorter events, 28.8 us)
Async XLA Ops:
  0.0 1.6 copy-start
  3.5 9.6 %collective-permute-start = (f32[96,128]{1,0:T(8,128)S(1)}, f32[96,128]{1,0:T(8,128)S(1)}, u32[]{:S(2)}, u32[]{:S(2)}) collective-permute-start(f32[96,128]{1,0:T(8,128)S(1)} %get-tuple-element.20), channel_id=1, source_target_pairs={{0,1},{1,0},{2,3},{3,2},{4,5},{5,4},{6,7},{7,6},{8,9},{9,8},{10,11... | collective-permute-start | bytes 147464 | tf_op jit(solution)/shard_map/ppermute | solution.py:107
  12.3 5.1 %copy-start.2 = (s32[4,1]{0,1:T(1,128)S(1)}, s32[4,1]{0,1:T(1,128)}, u32[]{:S(2)}) copy-start(s32[4,1]{0,1:T(1,128)} %param.3) | copy-start | bytes 52
  13.9 13.1 %all-to-all-start = ((f32[8,96,128]{2,1,0:T(8,128)}), f32[8,96,128]{2,1,0:T(8,128)S(1)}, u32[]{:S(2)}, u32[]{:S(2)}) async-start(f32[8,96,128]{2,1,0:T(8,128)} %broadcast_in_dim.4), calls=%async_computation | async-start | bytes 786432 | tf_op jit(solution)/shard_map/all_to_all | solution.py:110
  31.6 19.7 %collective-permute-start.1 = (f32[64,2048]{1,0:T(8,128)S(1)}, f32[64,2048]{1,0:T(8,128)S(1)}, u32[]{:S(2)}, u32[]{:S(2)}) collective-permute-start(f32[64,2048]{1,0:T(8,128)S(1)} %fusion.38), channel_id=1, source_target_pairs={{0,16},{16,32},{32,48},{48,64},{64,80},{80,96},{96,112},{112,128},... | collective-permute-start | bytes 1572872 | tf_op jit(solution)/shard_map/ppermute | solution.py:43
  34.4 28.1 %collective-permute-start.2 = (f32[64,2048]{1,0:T(8,128)S(1)}, f32[64,2048]{1,0:T(8,128)S(1)}, u32[]{:S(2)}, u32[]{:S(2)}) collective-permute-start(f32[64,2048]{1,0:T(8,128)S(1)} %fusion.32), channel_id=1, source_target_pairs={{0,16},{16,32},{32,48},{48,64},{64,80},{80,96},{96,112},{112,128},... | collective-permute-start | bytes 1572872 | tf_op jit(solution)/shard_map/ppermute | solution.py:43
  38.4 31.1 %copy-start.1 = (f32[64,64]{1,0:T(8,128)S(1)}, f32[64,64]{1,0:T(8,128)}, u32[]{:S(2)}) copy-start(f32[64,64]{1,0:T(8,128)} %fusion.34) | copy-start | bytes 49156
  63.8 14.2 %all-to-all-start.1 = ((f32[16,32,128]{2,1,0:T(8,128)}), f32[16,32,128]{2,1,0:T(8,128)S(1)}, u32[]{:S(2)}, u32[]{:S(2)}) async-start(f32[16,32,128]{2,1,0:T(8,128)} %shard_map.31), calls=%async_computation.1 | async-start | bytes 524288 | tf_op jit(solution)/shard_map/all_to_all | solution.py:102
  69.5 7.1 %collective-permute-start.3 = (f32[64,64]{1,0:T(8,128)S(1)}, f32[64,64]{1,0:T(8,128)S(1)}, u32[]{:S(2)}, u32[]{:S(2)}) collective-permute-start(f32[64,64]{1,0:T(8,128)S(1)} %copy-done.1), channel_id=1, source_target_pairs={{0,16},{16,32},{32,48},{48,64},{64,80},{80,96},{96,112},{112,128},... | collective-permute-start | bytes 49160 | tf_op jit(solution)/shard_map/ppermute | solution.py:43
  81.9 16.1 %collective-permute-start.4 = (f32[64,2048]{1,0:T(8,128)S(1)}, f32[64,2048]{1,0:T(8,128)S(1)}, u32[]{:S(2)}, u32[]{:S(2)}) collective-permute-start(f32[64,2048]{1,0:T(8,128)S(1)} %fusion.10), channel_id=1, source_target_pairs={{0,16},{16,32},{32,48},{48,64},{64,80},{80,96},{96,112},{112,128},... | collective-permute-start | bytes 1572872 | tf_op jit(solution)/shard_map/ppermute | solution.py:43
  84.5 24.7 %collective-permute-start.5 = (f32[64,2048]{1,0:T(8,128)S(1)}, f32[64,2048]{1,0:T(8,128)S(1)}, u32[]{:S(2)}, u32[]{:S(2)}) collective-permute-start(f32[64,2048]{1,0:T(8,128)S(1)} %fusion.8), channel_id=1, source_target_pairs={{0,16},{16,32},{32,48},{48,64},{64,80},{80,96},{96,112},{112,128},... | collective-permute-start | bytes 1572872 | tf_op jit(solution)/shard_map/ppermute | solution.py:43
  110.3 5.0 %collective-permute-start.6 = (f32[96,128]{1,0:T(8,128)S(1)}, f32[96,128]{1,0:T(8,128)S(1)}, u32[]{:S(2)}, u32[]{:S(2)}) collective-permute-start(f32[96,128]{1,0:T(8,128)S(1)} %shard_map.34), channel_id=1, source_target_pairs={{0,1},{1,0},{2,3},{3,2},{4,5},{5,4},{6,7},{7,6},{8,9},{9,8},{10,11... | collective-permute-start | bytes 147464 | tf_op jit(solution)/shard_map/ppermute | solution.py:107
  133.5 15.5 %collective-permute-start.7 = (f32[64,2048]{1,0:T(8,128)S(1)}, f32[64,2048]{1,0:T(8,128)S(1)}, u32[]{:S(2)}, u32[]{:S(2)}) collective-permute-start(f32[64,2048]{1,0:T(8,128)S(1)} %fusion.6), channel_id=1, source_target_pairs={{0,16},{16,32},{32,48},{48,64},{64,80},{80,96},{96,112},{112,128},... | collective-permute-start | bytes 1572872 | tf_op jit(solution)/shard_map/ppermute | solution.py:43
  136.1 24.1 %collective-permute-start.8 = (f32[64,2048]{1,0:T(8,128)S(1)}, f32[64,2048]{1,0:T(8,128)S(1)}, u32[]{:S(2)}, u32[]{:S(2)}) collective-permute-start(f32[64,2048]{1,0:T(8,128)S(1)} %fusion.4), channel_id=1, source_target_pairs={{0,16},{16,32},{32,48},{48,64},{64,80},{80,96},{96,112},{112,128},... | collective-permute-start | bytes 1572872 | tf_op jit(solution)/shard_map/ppermute | solution.py:43
  161.5 14.9 %all-to-all-start.3 = ((f32[16,32,128]{2,1,0:T(8,128)}), f32[16,32,128]{2,1,0:T(8,128)S(1)}, u32[]{:S(2)}, u32[]{:S(2)}) async-start(f32[16,32,128]{2,1,0:T(8,128)} %shard_map.37), calls=%async_computation.3 | async-start | bytes 524288 | tf_op jit(solution)/shard_map/all_to_all | solution.py:102
  168.0 7.1 %collective-permute-start.9 = (f32[64,64]{1,0:T(8,128)S(1)}, f32[64,64]{1,0:T(8,128)S(1)}, u32[]{:S(2)}, u32[]{:S(2)}) collective-permute-start(f32[64,64]{1,0:T(8,128)S(1)} %fusion.21), channel_id=1, source_target_pairs={{0,16},{16,32},{32,48},{48,64},{64,80},{80,96},{96,112},{112,128},... | collective-permute-start | bytes 49160 | tf_op jit(solution)/shard_map/ppermute | solution.py:43
  180.4 16.1 %collective-permute-start.10 = (f32[64,2048]{1,0:T(8,128)S(1)}, f32[64,2048]{1,0:T(8,128)S(1)}, u32[]{:S(2)}, u32[]{:S(2)}) collective-permute-start(f32[64,2048]{1,0:T(8,128)S(1)} %fusion.2), channel_id=1, source_target_pairs={{0,16},{16,32},{32,48},{48,64},{64,80},{80,96},{96,112},{112,128},... | collective-permute-start | bytes 1572872 | tf_op jit(solution)/shard_map/ppermute | solution.py:43
  183.0 24.7 %collective-permute-start.11 = (f32[64,2048]{1,0:T(8,128)S(1)}, f32[64,2048]{1,0:T(8,128)S(1)}, u32[]{:S(2)}, u32[]{:S(2)}) collective-permute-start(f32[64,2048]{1,0:T(8,128)S(1)} %fusion), channel_id=1, source_target_pairs={{0,16},{16,32},{32,48},{48,64},{64,80},{80,96},{96,112},{112,128},... | collective-permute-start | bytes 1572872 | tf_op jit(solution)/shard_map/ppermute | solution.py:43

commit v7 on v6

--- a/solution.py
+++ b/solution.py
@@ -181,13 +181,19 @@
     part_ref[...] = products(stay_ref, arrived_ref, whole)
 
 
-def last_gram_kernel(whole, before_ref, stay_ref, arrived_ref, part_ref):
-    part = before_ref[...] + products(stay_ref, arrived_ref, whole)
-    if whole:
-        part_ref[...] = part
-    else:
-        for device in range(part_ref.shape[0]):
-            part_ref[device] = part
+def last_gram_kernel(before_ref, stay_ref, arrived_ref, part_ref):
+    part_ref[...] = before_ref[...] + products(stay_ref, arrived_ref, True)
+
+
+def last_cross_kernel(before_ref, stay_ref, arrived_ref, copies_ref, held_ref, sems):
+    held_ref[...] = before_ref[...] + products(stay_ref, arrived_ref, False)
+    copies = [
+        pltpu.make_async_copy(held_ref, copies_ref.at[device], sems.at[device]) for device in range(sems.shape[0])
+    ]
+    for copy in copies:
+        copy.start()
+    for copy in copies:
+        copy.wait()
 
 
 def gram_part(stays, arriveds, copies=None, beside=None):
@@ -196,17 +202,22 @@
     part = jax.ShapeDtypeStruct((3 * width // 2 if whole else width // 2, 2 * width), jnp.float32)
     result = part if whole else jax.ShapeDtypeStruct((copies,) + part.shape, jnp.float32)
     options = dict(
-        out_specs=IN_VMEM,
         compiler_params=pltpu.CompilerParams(vmem_limit_bytes=8 << 20),
         cost_estimate=pl.CostEstimate(flops=400_000_000, bytes_accessed=3_000_000, transcendentals=0),
     )
     first = pl.pallas_call(
-        functools.partial(first_gram_kernel, whole), out_shape=part, in_specs=[IN_VMEM] * 2, **options
+        functools.partial(first_gram_kernel, whole), out_shape=part, in_specs=[IN_VMEM] * 2, out_specs=IN_VMEM, **options
     )(stays[0], arriveds[0])
     if beside is not None:
         first, beside = lax.optimization_barrier((first, beside))
+    if not whole:
+        options["scratch_shapes"] = [pltpu.VMEM(part.shape, jnp.float32), pltpu.SemaphoreType.DMA((copies,))]
     result = pl.pallas_call(
-        functools.partial(last_gram_kernel, whole), out_shape=result, in_specs=[IN_VMEM] * 3, **options
+        last_gram_kernel if whole else last_cross_kernel,
+        out_shape=result,
+        in_specs=[IN_VMEM] * 3,
+        out_specs=IN_VMEM if whole else pl.BlockSpec(memory_space=pltpu.HBM),
+        **options,
     )(first, stays[1], arriveds[1])
     return result, beside
 

time: 210 us -> 210 us (level)
  no operation moved by 1% of the time
where the time goes in v7:
time: 210 us; the launch traced here: 209 us
  waiting for transfers between devices  107 us (51%)
  starting transfers between devices  48.2 us (23%)
  Pallas kernels  23.1 us (11%)
  blocking collectives  14 us (7%)
  matrix products  13 us (6%)
  local copies, waits for them, and re-layouts  3.22 us (2%)
    ppermute x10, waiting for transfers between devices, passed_along(): lax.ppermute(shard, axis, [(i, (i + by) % peers) for i in range(peers)])  93.8 us
    ppermute x10, starting transfers between devices, passed_along(): lax.ppermute(shard, axis, [(i, (i + by) % peers) for i in range(peers)])  20 us
    all_to_all x1, blocking collectives, shares_of_chips(): return lax.all_to_all(copies, 'row', 0, 0, axis_index_groups=groups)  14 us
    ppermute x2, starting transfers between devices, shares_of_chips(): part = part + lax.ppermute(part, 'row', [(i, i ^ 1) for i in range(peers)])  13 us
    pallas_call x4, Pallas kernels, turned(): pl.pallas_call(functools.partial(turn_kernel, total_rows, bool(blocks)),...  12.8 us
    all_to_all x2, starting transfers between devices, shares(): return lax.all_to_all(copies, 'row', 0, 0)  11.7 us
    dot_general x20, matrix products, mul(): return jnp.dot(a, b, precision=HIGHEST)  11.7 us
    all_to_all x1, waiting for transfers between devices, shares_of_chips(): return lax.all_to_all(copies, 'row', 0, 0, axis_index_groups=groups)  8.9 us
  transfers between devices with their start and end apart: 15, of which 15 were waited for; matrix products, arithmetic and copies ran while one was open for 5% of the time, Pallas kernels for 2%

profile of v7, /device:TPU:1, one launch (start us, length us, event | category | flops | bytes accessed | tf_op | source)
XLA Modules:
  0.0 209.3 jit_solution(8119295211447173673)
XLA Ops:
  1.6 1.9 shard_map.28
  3.5 8.8 %collective-permute-start = (f32[96,128]{1,0:T(8,128)S(1)}, f32[96,128]{1,0:T(8,128)S(1)}, u32[]{:S(2)}, u32[]{:S(2)}) collective-permute-start(f32[96,128]{1,0:T(8,128)S(1)} %get-tuple-element.20), channel_id=1, source_target_pairs={{0,1},{1,0},{2,3},{3,2},{4,5},{5,4},{6,7},{7,6},{8,9},{9,8},{10,11... | collective-permute-start | bytes 147464 | tf_op jit(solution)/shard_map/ppermute | solution.py:107
  13.9 3.5 %all-to-all-start = ((f32[8,96,128]{2,1,0:T(8,128)}), f32[8,96,128]{2,1,0:T(8,128)S(1)}, u32[]{:S(2)}, u32[]{:S(2)}) async-start(f32[8,96,128]{2,1,0:T(8,128)} %broadcast_in_dim.4), calls=%async_computation | async-start | bytes 786432 | tf_op jit(solution)/shard_map/all_to_all | solution.py:110
  18.1 8.9 %all-to-all-done.sums_ref = f32[8,96,128]{2,1,0:T(8,128)S(1)} async-done(((f32[8,96,128]{2,1,0:T(8,128)}), f32[8,96,128]{2,1,0:T(8,128)S(1)}, u32[]{:S(2)}, u32[]{:S(2)}) %all-to-all-start) | async-done | bytes 393248 | tf_op jit(solution)/shard_map/all_to_all | solution.py:110
  27.0 3.1 %shard_map.29 = (f32[128,128]{1,0:T(8,128)S(1)}, f32[128,128]{1,0:T(8,128)S(1)}) custom-call(s32[1]{0:T(128)} %bitcast.3.side_ref, f32[8,96,128]{2,1,0:T(8,128)S(1)} %all-to-all-done.sums_ref), custom_call_target="tpu_custom_call" | custom-call | flops 200000000 | bytes 500000 | tf_op jit(solution)/shard_map/pallas_call | solution.py:91
  31.6 1.9 collective-permute-start.1
  34.4 2.5 %collective-permute-start.2 = (f32[64,2048]{1,0:T(8,128)S(1)}, f32[64,2048]{1,0:T(8,128)S(1)}, u32[]{:S(2)}, u32[]{:S(2)}) collective-permute-start(f32[64,2048]{1,0:T(8,128)S(1)} %fusion.32), channel_id=1, source_target_pairs={{0,16},{16,32},{32,48},{48,64},{64,80},{80,96},{96,112},{112,128},... | collective-permute-start | bytes 1572872 | tf_op jit(solution)/shard_map/ppermute | solution.py:43
  38.4 12.9 %collective-permute-done.1.arrived_ref = f32[64,2048]{1,0:T(8,128)S(1)} collective-permute-done((f32[64,2048]{1,0:T(8,128)S(1)}, f32[64,2048]{1,0:T(8,128)S(1)}, u32[]{:S(2)}, u32[]{:S(2)}) %collective-permute-start.1) | collective-permute-done | bytes 524320 | tf_op jit(solution)/shard_map/ppermute | solution.py:43
  51.9 10.7 %collective-permute-done.2.arrived_ref = f32[64,2048]{1,0:T(8,128)S(1)} collective-permute-done((f32[64,2048]{1,0:T(8,128)S(1)}, f32[64,2048]{1,0:T(8,128)S(1)}, u32[]{:S(2)}, u32[]{:S(2)}) %collective-permute-start.2) | collective-permute-done | bytes 524320 | tf_op jit(solution)/shard_map/ppermute | solution.py:43
  63.9 5.5 %all-to-all-start.1 = ((f32[16,32,128]{2,1,0:T(8,128)}), f32[16,32,128]{2,1,0:T(8,128)S(1)}, u32[]{:S(2)}, u32[]{:S(2)}) async-start(f32[16,32,128]{2,1,0:T(8,128)} %shard_map.31), calls=%async_computation.1 | async-start | bytes 524288 | tf_op jit(solution)/shard_map/all_to_all | solution.py:102
  69.6 1.9 collective-permute-start.3
  71.8 4.9 %collective-permute-done.3.refs_1_ = f32[64,64]{1,0:T(8,128)S(1)} collective-permute-done((f32[64,64]{1,0:T(8,128)S(1)}, f32[64,64]{1,0:T(8,128)S(1)}, u32[]{:S(2)}, u32[]{:S(2)}) %collective-permute-start.3) | collective-permute-done | bytes 16416 | tf_op jit(solution)/shard_map/ppermute | solution.py:43
  78.1 3.2 %shard_map.32 = (f32[128,128]{1,0:T(8,128)}, f32[128,128]{1,0:T(8,128)S(1)}) custom-call(s32[1]{0:T(128)} %bitcast.2.side_ref, f32[16,32,128]{2,1,0:T(8,128)S(1)} %all-to-all-done.1.sums_ref, f32[64,64]{1,0:T(8,128)S(1)} %fusion.40.refs_0_, f32[64,64]{1,0:T(8,128)S(1)} %collective-permute-done.3.refs_1_), custom_call_target="tpu_custom_call" | custom-call | flops 200000000 | bytes 500000 | tf_op jit(solution)/shard_map/pallas_call | solution.py:91
  82.0 1.9 collective-permute-start.4
  84.7 2.1 %collective-permute-start.5 = (f32[64,2048]{1,0:T(8,128)S(1)}, f32[64,2048]{1,0:T(8,128)S(1)}, u32[]{:S(2)}, u32[]{:S(2)}) collective-permute-start(f32[64,2048]{1,0:T(8,128)S(1)} %fusion.8), channel_id=1, source_target_pairs={{0,16},{16,32},{32,48},{48,64},{64,80},{80,96},{96,112},{112,128},... | collective-permute-start | bytes 1572872 | tf_op jit(solution)/shard_map/ppermute | solution.py:43
  88.1 10.0 %collective-permute-done.4.arrived_ref = f32[64,2048]{1,0:T(8,128)S(1)} collective-permute-done((f32[64,2048]{1,0:T(8,128)S(1)}, f32[64,2048]{1,0:T(8,128)S(1)}, u32[]{:S(2)}, u32[]{:S(2)}) %collective-permute-start.4) | collective-permute-done | bytes 524320 | tf_op jit(solution)/shard_map/ppermute | solution.py:43
  99.2 10.2 %collective-permute-done.5.arrived_ref = f32[64,2048]{1,0:T(8,128)S(1)} collective-permute-done((f32[64,2048]{1,0:T(8,128)S(1)}, f32[64,2048]{1,0:T(8,128)S(1)}, u32[]{:S(2)}, u32[]{:S(2)}) %collective-permute-start.5) | collective-permute-done | bytes 524320 | tf_op jit(solution)/shard_map/ppermute | solution.py:43
  110.4 4.2 %collective-permute-start.6 = (f32[96,128]{1,0:T(8,128)S(1)}, f32[96,128]{1,0:T(8,128)S(1)}, u32[]{:S(2)}, u32[]{:S(2)}) collective-permute-start(f32[96,128]{1,0:T(8,128)S(1)} %shard_map.34), channel_id=1, source_target_pairs={{0,1},{1,0},{2,3},{3,2},{4,5},{5,4},{6,7},{7,6},{8,9},{9,8},{10,11... | collective-permute-start | bytes 147464 | tf_op jit(solution)/shard_map/ppermute | solution.py:107
  115.5 14.0 %all_to_all.20.sums_ref = f32[8,96,128]{2,1,0:T(8,128)S(1)} all-to-all(f32[8,96,128]{2,1,0:T(8,128)S(1)} %broadcast_in_dim.5), channel_id=1, replica_groups={{0,2,4,6,8,10,12,14},{1,3,5,7,9,11,13,15},{16,18,20,22,24,26,28,30},{17..., dimensions={0} | all-to-all | bytes 786432 | tf_op jit(solution)/shard_map/all_to_all | solution.py:110
  129.5 3.2 %shard_map.35 = (f32[128,128]{1,0:T(8,128)S(1)}, f32[128,128]{1,0:T(8,128)S(1)}) custom-call(s32[1]{0:T(128)} %bitcast.1.side_ref, f32[8,96,128]{2,1,0:T(8,128)S(1)} %all_to_all.20.sums_ref), custom_call_target="tpu_custom_call" | custom-call | flops 200000000 | bytes 500000 | tf_op jit(solution)/shard_map/pallas_call | solution.py:91
  133.6 1.9 collective-permute-start.7
  136.2 1.9 collective-permute-start.8
  139.7 9.4 %collective-permute-done.7.arrived_ref = f32[64,2048]{1,0:T(8,128)S(1)} collective-permute-done((f32[64,2048]{1,0:T(8,128)S(1)}, f32[64,2048]{1,0:T(8,128)S(1)}, u32[]{:S(2)}, u32[]{:S(2)}) %collective-permute-start.7) | collective-permute-done | bytes 524320 | tf_op jit(solution)/shard_map/ppermute | solution.py:43
  149.7 10.6 %collective-permute-done.8.arrived_ref = f32[64,2048]{1,0:T(8,128)S(1)} collective-permute-done((f32[64,2048]{1,0:T(8,128)S(1)}, f32[64,2048]{1,0:T(8,128)S(1)}, u32[]{:S(2)}, u32[]{:S(2)}) %collective-permute-start.8) | collective-permute-done | bytes 524320 | tf_op jit(solution)/shard_map/ppermute | solution.py:43
  161.8 6.2 %all-to-all-start.3 = ((f32[16,32,128]{2,1,0:T(8,128)}), f32[16,32,128]{2,1,0:T(8,128)S(1)}, u32[]{:S(2)}, u32[]{:S(2)}) async-start(f32[16,32,128]{2,1,0:T(8,128)} %shard_map.37), calls=%async_computation.3 | async-start | bytes 524288 | tf_op jit(solution)/shard_map/all_to_all | solution.py:102
  168.2 1.9 collective-permute-start.9
  170.3 4.9 %collective-permute-done.9.refs_1_ = f32[64,64]{1,0:T(8,128)S(1)} collective-permute-done((f32[64,64]{1,0:T(8,128)S(1)}, f32[64,64]{1,0:T(8,128)S(1)}, u32[]{:S(2)}, u32[]{:S(2)}) %collective-permute-start.9) | collective-permute-done | bytes 16416 | tf_op jit(solution)/shard_map/ppermute | solution.py:43
  176.7 3.3 %shard_map.38 = (f32[128,128]{1,0:T(8,128)}, f32[128,128]{1,0:T(8,128)S(1)}) custom-call(s32[1]{0:T(128)} %bitcast.side_ref, f32[16,32,128]{2,1,0:T(8,128)S(1)} %all-to-all-done.3.sums_ref, f32[64,64]{1,0:T(8,128)S(1)} %fusion.26.refs_0_, f32[64,64]{1,0:T(8,128)S(1)} %collective-permute-done.9.refs_1_), custom_call_target="tpu_custom_call" | custom-call | flops 200000000 | bytes 500000 | tf_op jit(solution)/shard_map/pallas_call | solution.py:91
  180.7 1.9 collective-permute-start.10
  183.3 1.9 collective-permute-start.11
  186.6 10.1 %collective-permute-done.10.refs_1_ = f32[64,2048]{1,0:T(8,128)S(1)} collective-permute-done((f32[64,2048]{1,0:T(8,128)S(1)}, f32[64,2048]{1,0:T(8,128)S(1)}, u32[]{:S(2)}, u32[]{:S(2)}) %collective-permute-start.10) | collective-permute-done | bytes 524320 | tf_op jit(solution)/shard_map/ppermute | solution.py:43
  197.9 10.1 %collective-permute-done.11.refs_2_ = f32[64,2048]{1,0:T(8,128)S(1)} collective-permute-done((f32[64,2048]{1,0:T(8,128)S(1)}, f32[64,2048]{1,0:T(8,128)S(1)}, u32[]{:S(2)}, u32[]{:S(2)}) %collective-permute-start.11) | collective-permute-done | bytes 524320 | tf_op jit(solution)/shard_map/ppermute | solution.py:43
  (51 shorter events, 29.1 us)
Async XLA Ops:
  0.0 1.6 copy-start
  3.5 9.6 %collective-permute-start = (f32[96,128]{1,0:T(8,128)S(1)}, f32[96,128]{1,0:T(8,128)S(1)}, u32[]{:S(2)}, u32[]{:S(2)}) collective-permute-start(f32[96,128]{1,0:T(8,128)S(1)} %get-tuple-element.20), channel_id=1, source_target_pairs={{0,1},{1,0},{2,3},{3,2},{4,5},{5,4},{6,7},{7,6},{8,9},{9,8},{10,11... | collective-permute-start | bytes 147464 | tf_op jit(solution)/shard_map/ppermute | solution.py:107
  12.3 5.1 %copy-start.2 = (s32[4,1]{0,1:T(1,128)S(1)}, s32[4,1]{0,1:T(1,128)}, u32[]{:S(2)}) copy-start(s32[4,1]{0,1:T(1,128)} %param.3) | copy-start | bytes 52
  13.9 13.1 %all-to-all-start = ((f32[8,96,128]{2,1,0:T(8,128)}), f32[8,96,128]{2,1,0:T(8,128)S(1)}, u32[]{:S(2)}, u32[]{:S(2)}) async-start(f32[8,96,128]{2,1,0:T(8,128)} %broadcast_in_dim.4), calls=%async_computation | async-start | bytes 786432 | tf_op jit(solution)/shard_map/all_to_all | solution.py:110
  31.6 19.7 %collective-permute-start.1 = (f32[64,2048]{1,0:T(8,128)S(1)}, f32[64,2048]{1,0:T(8,128)S(1)}, u32[]{:S(2)}, u32[]{:S(2)}) collective-permute-start(f32[64,2048]{1,0:T(8,128)S(1)} %fusion.38), channel_id=1, source_target_pairs={{0,16},{16,32},{32,48},{48,64},{64,80},{80,96},{96,112},{112,128},... | collective-permute-start | bytes 1572872 | tf_op jit(solution)/shard_map/ppermute | solution.py:43
  34.4 28.1 %collective-permute-start.2 = (f32[64,2048]{1,0:T(8,128)S(1)}, f32[64,2048]{1,0:T(8,128)S(1)}, u32[]{:S(2)}, u32[]{:S(2)}) collective-permute-start(f32[64,2048]{1,0:T(8,128)S(1)} %fusion.32), channel_id=1, source_target_pairs={{0,16},{16,32},{32,48},{48,64},{64,80},{80,96},{96,112},{112,128},... | collective-permute-start | bytes 1572872 | tf_op jit(solution)/shard_map/ppermute | solution.py:43
  38.4 31.2 %copy-start.1 = (f32[64,64]{1,0:T(8,128)S(1)}, f32[64,64]{1,0:T(8,128)}, u32[]{:S(2)}) copy-start(f32[64,64]{1,0:T(8,128)} %fusion.34) | copy-start | bytes 49156
  63.9 14.2 %all-to-all-start.1 = ((f32[16,32,128]{2,1,0:T(8,128)}), f32[16,32,128]{2,1,0:T(8,128)S(1)}, u32[]{:S(2)}, u32[]{:S(2)}) async-start(f32[16,32,128]{2,1,0:T(8,128)} %shard_map.31), calls=%async_computation.1 | async-start | bytes 524288 | tf_op jit(solution)/shard_map/all_to_all | solution.py:102
  69.6 7.1 %collective-permute-start.3 = (f32[64,64]{1,0:T(8,128)S(1)}, f32[64,64]{1,0:T(8,128)S(1)}, u32[]{:S(2)}, u32[]{:S(2)}) collective-permute-start(f32[64,64]{1,0:T(8,128)S(1)} %copy-done.1), channel_id=1, source_target_pairs={{0,16},{16,32},{32,48},{48,64},{64,80},{80,96},{96,112},{112,128},... | collective-permute-start | bytes 49160 | tf_op jit(solution)/shard_map/ppermute | solution.py:43
  82.0 16.1 %collective-permute-start.4 = (f32[64,2048]{1,0:T(8,128)S(1)}, f32[64,2048]{1,0:T(8,128)S(1)}, u32[]{:S(2)}, u32[]{:S(2)}) collective-permute-start(f32[64,2048]{1,0:T(8,128)S(1)} %fusion.10), channel_id=1, source_target_pairs={{0,16},{16,32},{32,48},{48,64},{64,80},{80,96},{96,112},{112,128},... | collective-permute-start | bytes 1572872 | tf_op jit(solution)/shard_map/ppermute | solution.py:43
  84.7 24.7 %collective-permute-start.5 = (f32[64,2048]{1,0:T(8,128)S(1)}, f32[64,2048]{1,0:T(8,128)S(1)}, u32[]{:S(2)}, u32[]{:S(2)}) collective-permute-start(f32[64,2048]{1,0:T(8,128)S(1)} %fusion.8), channel_id=1, source_target_pairs={{0,16},{16,32},{32,48},{48,64},{64,80},{80,96},{96,112},{112,128},... | collective-permute-start | bytes 1572872 | tf_op jit(solution)/shard_map/ppermute | solution.py:43
  110.4 5.0 %collective-permute-start.6 = (f32[96,128]{1,0:T(8,128)S(1)}, f32[96,128]{1,0:T(8,128)S(1)}, u32[]{:S(2)}, u32[]{:S(2)}) collective-permute-start(f32[96,128]{1,0:T(8,128)S(1)} %shard_map.34), channel_id=1, source_target_pairs={{0,1},{1,0},{2,3},{3,2},{4,5},{5,4},{6,7},{7,6},{8,9},{9,8},{10,11... | collective-permute-start | bytes 147464 | tf_op jit(solution)/shard_map/ppermute | solution.py:107
  133.6 15.5 %collective-permute-start.7 = (f32[64,2048]{1,0:T(8,128)S(1)}, f32[64,2048]{1,0:T(8,128)S(1)}, u32[]{:S(2)}, u32[]{:S(2)}) collective-permute-start(f32[64,2048]{1,0:T(8,128)S(1)} %fusion.6), channel_id=1, source_target_pairs={{0,16},{16,32},{32,48},{48,64},{64,80},{80,96},{96,112},{112,128},... | collective-permute-start | bytes 1572872 | tf_op jit(solution)/shard_map/ppermute | solution.py:43
  136.2 24.1 %collective-permute-start.8 = (f32[64,2048]{1,0:T(8,128)S(1)}, f32[64,2048]{1,0:T(8,128)S(1)}, u32[]{:S(2)}, u32[]{:S(2)}) collective-permute-start(f32[64,2048]{1,0:T(8,128)S(1)} %fusion.4), channel_id=1, source_target_pairs={{0,16},{16,32},{32,48},{48,64},{64,80},{80,96},{96,112},{112,128},... | collective-permute-start | bytes 1572872 | tf_op jit(solution)/shard_map/ppermute | solution.py:43
  161.8 14.9 %all-to-all-start.3 = ((f32[16,32,128]{2,1,0:T(8,128)}), f32[16,32,128]{2,1,0:T(8,128)S(1)}, u32[]{:S(2)}, u32[]{:S(2)}) async-start(f32[16,32,128]{2,1,0:T(8,128)} %shard_map.37), calls=%async_computation.3 | async-start | bytes 524288 | tf_op jit(solution)/shard_map/all_to_all | solution.py:102
  168.2 7.1 %collective-permute-start.9 = (f32[64,64]{1,0:T(8,128)S(1)}, f32[64,64]{1,0:T(8,128)S(1)}, u32[]{:S(2)}, u32[]{:S(2)}) collective-permute-start(f32[64,64]{1,0:T(8,128)S(1)} %fusion.21), channel_id=1, source_target_pairs={{0,16},{16,32},{32,48},{48,64},{64,80},{80,96},{96,112},{112,128},... | collective-permute-start | bytes 49160 | tf_op jit(solution)/shard_map/ppermute | solution.py:43
  180.7 16.1 %collective-permute-start.10 = (f32[64,2048]{1,0:T(8,128)S(1)}, f32[64,2048]{1,0:T(8,128)S(1)}, u32[]{:S(2)}, u32[]{:S(2)}) collective-permute-start(f32[64,2048]{1,0:T(8,128)S(1)} %fusion.2), channel_id=1, source_target_pairs={{0,16},{16,32},{32,48},{48,64},{64,80},{80,96},{96,112},{112,128},... | collective-permute-start | bytes 1572872 | tf_op jit(solution)/shard_map/ppermute | solution.py:43
  183.3 24.7 %collective-permute-start.11 = (f32[64,2048]{1,0:T(8,128)S(1)}, f32[64,2048]{1,0:T(8,128)S(1)}, u32[]{:S(2)}, u32[]{:S(2)}) collective-permute-start(f32[64,2048]{1,0:T(8,128)S(1)} %fusion), channel_id=1, source_target_pairs={{0,16},{16,32},{32,48},{48,64},{64,80},{80,96},{96,112},{112,128},... | collective-permute-start | bytes 1572872 | tf_op jit(solution)/shard_map/ppermute | solution.py:43

commit v8 on v6

--- a/solution.py
+++ b/solution.py
@@ -126,7 +126,7 @@
 
 def entry_kernel(x_ref, *refs):
     part_ref, xt_refs = refs[-1], refs[:-1]
-    pieces = 8
+    pieces = 4
     height = x_ref.shape[0] // pieces
     each = pieces // GROUPS
     width = x_ref.shape[1] // 2
@@ -161,7 +161,7 @@
 
 def products(stay_ref, arrived_ref, whole):
     rows = stay_ref.shape[1]
-    pieces = 2
+    pieces = 1
     length = rows // pieces
     total = None
     for piece in range(pieces):

time: 210 us -> 210 us (level)
  no operation moved by 1% of the time
where the time goes in v8:
time: 210 us; the launch traced here: 209 us
  waiting for transfers between devices  107 us (51%)
  starting transfers between devices  48.2 us (23%)
  Pallas kernels  22.9 us (11%)
  blocking collectives  14 us (7%)
  matrix products  13 us (6%)
  local copies, waits for them, and re-layouts  3.22 us (2%)
    ppermute x10, waiting for transfers between devices, passed_along(): lax.ppermute(shard, axis, [(i, (i + by) % peers) for i in range(peers)])  93.8 us
    ppermute x10, starting transfers between devices, passed_along(): lax.ppermute(shard, axis, [(i, (i + by) % peers) for i in range(peers)])  20 us
    all_to_all x1, blocking collectives, shares_of_chips(): return lax.all_to_all(copies, 'row', 0, 0, axis_index_groups=groups)  14 us
    ppermute x2, starting transfers between devices, shares_of_chips(): part = part + lax.ppermute(part, 'row', [(i, i ^ 1) for i in range(peers)])  13 us
    pallas_call x4, Pallas kernels, turned(): pl.pallas_call(functools.partial(turn_kernel, total_rows, bool(blocks)),...  12.8 us
    all_to_all x2, starting transfers between devices, shares(): return lax.all_to_all(copies, 'row', 0, 0)  11.7 us
    dot_general x20, matrix products, mul(): return jnp.dot(a, b, precision=HIGHEST)  11.7 us
    all_to_all x1, waiting for transfers between devices, shares_of_chips(): return lax.all_to_all(copies, 'row', 0, 0, axis_index_groups=groups)  8.9 us
  transfers between devices with their start and end apart: 15, of which 15 were waited for; matrix products, arithmetic and copies ran while one was open for 5% of the time, Pallas kernels for 2%

profile of v8, /device:TPU:1, one launch (start us, length us, event | category | flops | bytes accessed | tf_op | source)
XLA Modules:
  0.0 209.0 jit_solution(1741619386907489163)
XLA Ops:
  1.6 1.9 shard_map.28
  3.5 8.8 %collective-permute-start = (f32[96,128]{1,0:T(8,128)S(1)}, f32[96,128]{1,0:T(8,128)S(1)}, u32[]{:S(2)}, u32[]{:S(2)}) collective-permute-start(f32[96,128]{1,0:T(8,128)S(1)} %get-tuple-element.20), channel_id=1, source_target_pairs={{0,1},{1,0},{2,3},{3,2},{4,5},{5,4},{6,7},{7,6},{8,9},{9,8},{10,11... | collective-permute-start | bytes 147464 | tf_op jit(solution)/shard_map/ppermute | solution.py:107
  13.9 3.5 %all-to-all-start = ((f32[8,96,128]{2,1,0:T(8,128)}), f32[8,96,128]{2,1,0:T(8,128)S(1)}, u32[]{:S(2)}, u32[]{:S(2)}) async-start(f32[8,96,128]{2,1,0:T(8,128)} %broadcast_in_dim.4), calls=%async_computation | async-start | bytes 786432 | tf_op jit(solution)/shard_map/all_to_all | solution.py:110
  18.1 8.9 %all-to-all-done.sums_ref = f32[8,96,128]{2,1,0:T(8,128)S(1)} async-done(((f32[8,96,128]{2,1,0:T(8,128)}), f32[8,96,128]{2,1,0:T(8,128)S(1)}, u32[]{:S(2)}, u32[]{:S(2)}) %all-to-all-start) | async-done | bytes 393248 | tf_op jit(solution)/shard_map/all_to_all | solution.py:110
  27.0 3.1 %shard_map.29 = (f32[128,128]{1,0:T(8,128)S(1)}, f32[128,128]{1,0:T(8,128)S(1)}) custom-call(s32[1]{0:T(128)} %bitcast.3.side_ref, f32[8,96,128]{2,1,0:T(8,128)S(1)} %all-to-all-done.sums_ref), custom_call_target="tpu_custom_call" | custom-call | flops 200000000 | bytes 500000 | tf_op jit(solution)/shard_map/pallas_call | solution.py:91
  31.6 1.9 collective-permute-start.1
  34.4 2.5 %collective-permute-start.2 = (f32[64,2048]{1,0:T(8,128)S(1)}, f32[64,2048]{1,0:T(8,128)S(1)}, u32[]{:S(2)}, u32[]{:S(2)}) collective-permute-start(f32[64,2048]{1,0:T(8,128)S(1)} %fusion.32), channel_id=1, source_target_pairs={{0,16},{16,32},{32,48},{48,64},{64,80},{80,96},{96,112},{112,128},... | collective-permute-start | bytes 1572872 | tf_op jit(solution)/shard_map/ppermute | solution.py:43
  38.4 12.8 %collective-permute-done.1.arrived_ref = f32[64,2048]{1,0:T(8,128)S(1)} collective-permute-done((f32[64,2048]{1,0:T(8,128)S(1)}, f32[64,2048]{1,0:T(8,128)S(1)}, u32[]{:S(2)}, u32[]{:S(2)}) %collective-permute-start.1) | collective-permute-done | bytes 524320 | tf_op jit(solution)/shard_map/ppermute | solution.py:43
  51.8 10.7 %collective-permute-done.2.arrived_ref = f32[64,2048]{1,0:T(8,128)S(1)} collective-permute-done((f32[64,2048]{1,0:T(8,128)S(1)}, f32[64,2048]{1,0:T(8,128)S(1)}, u32[]{:S(2)}, u32[]{:S(2)}) %collective-permute-start.2) | collective-permute-done | bytes 524320 | tf_op jit(solution)/shard_map/ppermute | solution.py:43
  63.8 5.5 %all-to-all-start.1 = ((f32[16,32,128]{2,1,0:T(8,128)}), f32[16,32,128]{2,1,0:T(8,128)S(1)}, u32[]{:S(2)}, u32[]{:S(2)}) async-start(f32[16,32,128]{2,1,0:T(8,128)} %shard_map.31), calls=%async_computation.1 | async-start | bytes 524288 | tf_op jit(solution)/shard_map/all_to_all | solution.py:102
  69.5 1.9 collective-permute-start.3
  71.6 4.9 %collective-permute-done.3.refs_1_ = f32[64,64]{1,0:T(8,128)S(1)} collective-permute-done((f32[64,64]{1,0:T(8,128)S(1)}, f32[64,64]{1,0:T(8,128)S(1)}, u32[]{:S(2)}, u32[]{:S(2)}) %collective-permute-start.3) | collective-permute-done | bytes 16416 | tf_op jit(solution)/shard_map/ppermute | solution.py:43
  78.0 3.2 %shard_map.32 = (f32[128,128]{1,0:T(8,128)}, f32[128,128]{1,0:T(8,128)S(1)}) custom-call(s32[1]{0:T(128)} %bitcast.2.side_ref, f32[16,32,128]{2,1,0:T(8,128)S(1)} %all-to-all-done.1.sums_ref, f32[64,64]{1,0:T(8,128)S(1)} %fusion.40.refs_0_, f32[64,64]{1,0:T(8,128)S(1)} %collective-permute-done.3.refs_1_), custom_call_target="tpu_custom_call" | custom-call | flops 200000000 | bytes 500000 | tf_op jit(solution)/shard_map/pallas_call | solution.py:91
  81.9 1.9 collective-permute-start.4
  84.5 2.1 %collective-permute-start.5 = (f32[64,2048]{1,0:T(8,128)S(1)}, f32[64,2048]{1,0:T(8,128)S(1)}, u32[]{:S(2)}, u32[]{:S(2)}) collective-permute-start(f32[64,2048]{1,0:T(8,128)S(1)} %fusion.8), channel_id=1, source_target_pairs={{0,16},{16,32},{32,48},{48,64},{64,80},{80,96},{96,112},{112,128},... | collective-permute-start | bytes 1572872 | tf_op jit(solution)/shard_map/ppermute | solution.py:43
  88.0 10.0 %collective-permute-done.4.arrived_ref = f32[64,2048]{1,0:T(8,128)S(1)} collective-permute-done((f32[64,2048]{1,0:T(8,128)S(1)}, f32[64,2048]{1,0:T(8,128)S(1)}, u32[]{:S(2)}, u32[]{:S(2)}) %collective-permute-start.4) | collective-permute-done | bytes 524320 | tf_op jit(solution)/shard_map/ppermute | solution.py:43
  99.1 10.2 %collective-permute-done.5.arrived_ref = f32[64,2048]{1,0:T(8,128)S(1)} collective-permute-done((f32[64,2048]{1,0:T(8,128)S(1)}, f32[64,2048]{1,0:T(8,128)S(1)}, u32[]{:S(2)}, u32[]{:S(2)}) %collective-permute-start.5) | collective-permute-done | bytes 524320 | tf_op jit(solution)/shard_map/ppermute | solution.py:43
  110.3 4.2 %collective-permute-start.6 = (f32[96,128]{1,0:T(8,128)S(1)}, f32[96,128]{1,0:T(8,128)S(1)}, u32[]{:S(2)}, u32[]{:S(2)}) collective-permute-start(f32[96,128]{1,0:T(8,128)S(1)} %shard_map.34), channel_id=1, source_target_pairs={{0,1},{1,0},{2,3},{3,2},{4,5},{5,4},{6,7},{7,6},{8,9},{9,8},{10,11... | collective-permute-start | bytes 147464 | tf_op jit(solution)/shard_map/ppermute | solution.py:107
  115.4 14.0 %all_to_all.20.sums_ref = f32[8,96,128]{2,1,0:T(8,128)S(1)} all-to-all(f32[8,96,128]{2,1,0:T(8,128)S(1)} %broadcast_in_dim.5), channel_id=1, replica_groups={{0,2,4,6,8,10,12,14},{1,3,5,7,9,11,13,15},{16,18,20,22,24,26,28,30},{17..., dimensions={0} | all-to-all | bytes 786432 | tf_op jit(solution)/shard_map/all_to_all | solution.py:110
  129.4 3.2 %shard_map.35 = (f32[128,128]{1,0:T(8,128)S(1)}, f32[128,128]{1,0:T(8,128)S(1)}) custom-call(s32[1]{0:T(128)} %bitcast.1.side_ref, f32[8,96,128]{2,1,0:T(8,128)S(1)} %all_to_all.20.sums_ref), custom_call_target="tpu_custom_call" | custom-call | flops 200000000 | bytes 500000 | tf_op jit(solution)/shard_map/pallas_call | solution.py:91
  133.5 1.9 collective-permute-start.7
  136.1 1.9 collective-permute-start.8
  139.6 9.4 %collective-permute-done.7.arrived_ref = f32[64,2048]{1,0:T(8,128)S(1)} collective-permute-done((f32[64,2048]{1,0:T(8,128)S(1)}, f32[64,2048]{1,0:T(8,128)S(1)}, u32[]{:S(2)}, u32[]{:S(2)}) %collective-permute-start.7) | collective-permute-done | bytes 524320 | tf_op jit(solution)/shard_map/ppermute | solution.py:43
  149.6 10.6 %collective-permute-done.8.arrived_ref = f32[64,2048]{1,0:T(8,128)S(1)} collective-permute-done((f32[64,2048]{1,0:T(8,128)S(1)}, f32[64,2048]{1,0:T(8,128)S(1)}, u32[]{:S(2)}, u32[]{:S(2)}) %collective-permute-start.8) | collective-permute-done | bytes 524320 | tf_op jit(solution)/shard_map/ppermute | solution.py:43
  161.5 6.2 %all-to-all-start.3 = ((f32[16,32,128]{2,1,0:T(8,128)}), f32[16,32,128]{2,1,0:T(8,128)S(1)}, u32[]{:S(2)}, u32[]{:S(2)}) async-start(f32[16,32,128]{2,1,0:T(8,128)} %shard_map.37), calls=%async_computation.3 | async-start | bytes 524288 | tf_op jit(solution)/shard_map/all_to_all | solution.py:102
  167.9 1.9 collective-permute-start.9
  170.1 4.9 %collective-permute-done.9.refs_1_ = f32[64,64]{1,0:T(8,128)S(1)} collective-permute-done((f32[64,64]{1,0:T(8,128)S(1)}, f32[64,64]{1,0:T(8,128)S(1)}, u32[]{:S(2)}, u32[]{:S(2)}) %collective-permute-start.9) | collective-permute-done | bytes 16416 | tf_op jit(solution)/shard_map/ppermute | solution.py:43
  176.4 3.3 %shard_map.38 = (f32[128,128]{1,0:T(8,128)}, f32[128,128]{1,0:T(8,128)S(1)}) custom-call(s32[1]{0:T(128)} %bitcast.side_ref, f32[16,32,128]{2,1,0:T(8,128)S(1)} %all-to-all-done.3.sums_ref, f32[64,64]{1,0:T(8,128)S(1)} %fusion.26.refs_0_, f32[64,64]{1,0:T(8,128)S(1)} %collective-permute-done.9.refs_1_), custom_call_target="tpu_custom_call" | custom-call | flops 200000000 | bytes 500000 | tf_op jit(solution)/shard_map/pallas_call | solution.py:91
  180.4 1.9 collective-permute-start.10
  183.0 1.9 collective-permute-start.11
  186.3 10.1 %collective-permute-done.10.refs_1_ = f32[64,2048]{1,0:T(8,128)S(1)} collective-permute-done((f32[64,2048]{1,0:T(8,128)S(1)}, f32[64,2048]{1,0:T(8,128)S(1)}, u32[]{:S(2)}, u32[]{:S(2)}) %collective-permute-start.10) | collective-permute-done | bytes 524320 | tf_op jit(solution)/shard_map/ppermute | solution.py:43
  197.6 10.1 %collective-permute-done.11.refs_2_ = f32[64,2048]{1,0:T(8,128)S(1)} collective-permute-done((f32[64,2048]{1,0:T(8,128)S(1)}, f32[64,2048]{1,0:T(8,128)S(1)}, u32[]{:S(2)}, u32[]{:S(2)}) %collective-permute-start.11) | collective-permute-done | bytes 524320 | tf_op jit(solution)/shard_map/ppermute | solution.py:43
  (51 shorter events, 28.8 us)
Async XLA Ops:
  0.0 1.6 copy-start
  3.5 9.6 %collective-permute-start = (f32[96,128]{1,0:T(8,128)S(1)}, f32[96,128]{1,0:T(8,128)S(1)}, u32[]{:S(2)}, u32[]{:S(2)}) collective-permute-start(f32[96,128]{1,0:T(8,128)S(1)} %get-tuple-element.20), channel_id=1, source_target_pairs={{0,1},{1,0},{2,3},{3,2},{4,5},{5,4},{6,7},{7,6},{8,9},{9,8},{10,11... | collective-permute-start | bytes 147464 | tf_op jit(solution)/shard_map/ppermute | solution.py:107
  12.3 5.1 %copy-start.2 = (s32[4,1]{0,1:T(1,128)S(1)}, s32[4,1]{0,1:T(1,128)}, u32[]{:S(2)}) copy-start(s32[4,1]{0,1:T(1,128)} %param.3) | copy-start | bytes 52
  13.9 13.1 %all-to-all-start = ((f32[8,96,128]{2,1,0:T(8,128)}), f32[8,96,128]{2,1,0:T(8,128)S(1)}, u32[]{:S(2)}, u32[]{:S(2)}) async-start(f32[8,96,128]{2,1,0:T(8,128)} %broadcast_in_dim.4), calls=%async_computation | async-start | bytes 786432 | tf_op jit(solution)/shard_map/all_to_all | solution.py:110
  31.6 19.7 %collective-permute-start.1 = (f32[64,2048]{1,0:T(8,128)S(1)}, f32[64,2048]{1,0:T(8,128)S(1)}, u32[]{:S(2)}, u32[]{:S(2)}) collective-permute-start(f32[64,2048]{1,0:T(8,128)S(1)} %fusion.38), channel_id=1, source_target_pairs={{0,16},{16,32},{32,48},{48,64},{64,80},{80,96},{96,112},{112,128},... | collective-permute-start | bytes 1572872 | tf_op jit(solution)/shard_map/ppermute | solution.py:43
  34.4 28.1 %collective-permute-start.2 = (f32[64,2048]{1,0:T(8,128)S(1)}, f32[64,2048]{1,0:T(8,128)S(1)}, u32[]{:S(2)}, u32[]{:S(2)}) collective-permute-start(f32[64,2048]{1,0:T(8,128)S(1)} %fusion.32), channel_id=1, source_target_pairs={{0,16},{16,32},{32,48},{48,64},{64,80},{80,96},{96,112},{112,128},... | collective-permute-start | bytes 1572872 | tf_op jit(solution)/shard_map/ppermute | solution.py:43
  38.4 31.1 %copy-start.1 = (f32[64,64]{1,0:T(8,128)S(1)}, f32[64,64]{1,0:T(8,128)}, u32[]{:S(2)}) copy-start(f32[64,64]{1,0:T(8,128)} %fusion.34) | copy-start | bytes 49156
  63.8 14.2 %all-to-all-start.1 = ((f32[16,32,128]{2,1,0:T(8,128)}), f32[16,32,128]{2,1,0:T(8,128)S(1)}, u32[]{:S(2)}, u32[]{:S(2)}) async-start(f32[16,32,128]{2,1,0:T(8,128)} %shard_map.31), calls=%async_computation.1 | async-start | bytes 524288 | tf_op jit(solution)/shard_map/all_to_all | solution.py:102
  69.5 7.1 %collective-permute-start.3 = (f32[64,64]{1,0:T(8,128)S(1)}, f32[64,64]{1,0:T(8,128)S(1)}, u32[]{:S(2)}, u32[]{:S(2)}) collective-permute-start(f32[64,64]{1,0:T(8,128)S(1)} %copy-done.1), channel_id=1, source_target_pairs={{0,16},{16,32},{32,48},{48,64},{64,80},{80,96},{96,112},{112,128},... | collective-permute-start | bytes 49160 | tf_op jit(solution)/shard_map/ppermute | solution.py:43
  81.9 16.1 %collective-permute-start.4 = (f32[64,2048]{1,0:T(8,128)S(1)}, f32[64,2048]{1,0:T(8,128)S(1)}, u32[]{:S(2)}, u32[]{:S(2)}) collective-permute-start(f32[64,2048]{1,0:T(8,128)S(1)} %fusion.10), channel_id=1, source_target_pairs={{0,16},{16,32},{32,48},{48,64},{64,80},{80,96},{96,112},{112,128},... | collective-permute-start | bytes 1572872 | tf_op jit(solution)/shard_map/ppermute | solution.py:43
  84.5 24.7 %collective-permute-start.5 = (f32[64,2048]{1,0:T(8,128)S(1)}, f32[64,2048]{1,0:T(8,128)S(1)}, u32[]{:S(2)}, u32[]{:S(2)}) collective-permute-start(f32[64,2048]{1,0:T(8,128)S(1)} %fusion.8), channel_id=1, source_target_pairs={{0,16},{16,32},{32,48},{48,64},{64,80},{80,96},{96,112},{112,128},... | collective-permute-start | bytes 1572872 | tf_op jit(solution)/shard_map/ppermute | solution.py:43
  110.3 5.0 %collective-permute-start.6 = (f32[96,128]{1,0:T(8,128)S(1)}, f32[96,128]{1,0:T(8,128)S(1)}, u32[]{:S(2)}, u32[]{:S(2)}) collective-permute-start(f32[96,128]{1,0:T(8,128)S(1)} %shard_map.34), channel_id=1, source_target_pairs={{0,1},{1,0},{2,3},{3,2},{4,5},{5,4},{6,7},{7,6},{8,9},{9,8},{10,11... | collective-permute-start | bytes 147464 | tf_op jit(solution)/shard_map/ppermute | solution.py:107
  133.5 15.5 %collective-permute-start.7 = (f32[64,2048]{1,0:T(8,128)S(1)}, f32[64,2048]{1,0:T(8,128)S(1)}, u32[]{:S(2)}, u32[]{:S(2)}) collective-permute-start(f32[64,2048]{1,0:T(8,128)S(1)} %fusion.6), channel_id=1, source_target_pairs={{0,16},{16,32},{32,48},{48,64},{64,80},{80,96},{96,112},{112,128},... | collective-permute-start | bytes 1572872 | tf_op jit(solution)/shard_map/ppermute | solution.py:43
  136.1 24.1 %collective-permute-start.8 = (f32[64,2048]{1,0:T(8,128)S(1)}, f32[64,2048]{1,0:T(8,128)S(1)}, u32[]{:S(2)}, u32[]{:S(2)}) collective-permute-start(f32[64,2048]{1,0:T(8,128)S(1)} %fusion.4), channel_id=1, source_target_pairs={{0,16},{16,32},{32,48},{48,64},{64,80},{80,96},{96,112},{112,128},... | collective-permute-start | bytes 1572872 | tf_op jit(solution)/shard_map/ppermute | solution.py:43
  161.5 14.9 %all-to-all-start.3 = ((f32[16,32,128]{2,1,0:T(8,128)}), f32[16,32,128]{2,1,0:T(8,128)S(1)}, u32[]{:S(2)}, u32[]{:S(2)}) async-start(f32[16,32,128]{2,1,0:T(8,128)} %shard_map.37), calls=%async_computation.3 | async-start | bytes 524288 | tf_op jit(solution)/shard_map/all_to_all | solution.py:102
  167.9 7.1 %collective-permute-start.9 = (f32[64,64]{1,0:T(8,128)S(1)}, f32[64,64]{1,0:T(8,128)S(1)}, u32[]{:S(2)}, u32[]{:S(2)}) collective-permute-start(f32[64,64]{1,0:T(8,128)S(1)} %fusion.21), channel_id=1, source_target_pairs={{0,16},{16,32},{32,48},{48,64},{64,80},{80,96},{96,112},{112,128},... | collective-permute-start | bytes 49160 | tf_op jit(solution)/shard_map/ppermute | solution.py:43
  180.4 16.1 %collective-permute-start.10 = (f32[64,2048]{1,0:T(8,128)S(1)}, f32[64,2048]{1,0:T(8,128)S(1)}, u32[]{:S(2)}, u32[]{:S(2)}) collective-permute-start(f32[64,2048]{1,0:T(8,128)S(1)} %fusion.2), channel_id=1, source_target_pairs={{0,16},{16,32},{32,48},{48,64},{64,80},{80,96},{96,112},{112,128},... | collective-permute-start | bytes 1572872 | tf_op jit(solution)/shard_map/ppermute | solution.py:43
  183.0 24.7 %collective-permute-start.11 = (f32[64,2048]{1,0:T(8,128)S(1)}, f32[64,2048]{1,0:T(8,128)S(1)}, u32[]{:S(2)}, u32[]{:S(2)}) collective-permute-start(f32[64,2048]{1,0:T(8,128)S(1)} %fusion), channel_id=1, source_target_pairs={{0,16},{16,32},{32,48},{48,64},{64,80},{80,96},{96,112},{112,128},... | collective-permute-start | bytes 1572872 | tf_op jit(solution)/shard_map/ppermute | solution.py:43
